TPU v7x, 1024 devices: a whole 8x8x8 slice. The times are simulated.
1024 devices in a mesh: col: 64 (over y_hi, z, core), red: 16 (over y_lo, x).
Axes of the slice: x: 8, y: 8 (y_hi: 4, y_lo: 2; y = y_hi * 2 + y_lo), z: 8, core: 2. Of those that a mesh axis runs over, the one named last changes fastest.
Arguments:
- amplitudes: bfloat16 [128, 1048576], P(None, ('red', 'col')), may hold values from -6 to 6
- block_tiles: bfloat16 [16, 64, 64, 24576], P('red', 'col'), may hold values from -0.029907227 to 0.029907227
- block_rows: int32 [16, 64, 48], P('red', 'col'), may hold values from 0 to 1023, as said below
- tile_mask: int32 [16, 64, 48, 8], P('red', 'col'), may hold values 0 or 1
- block_counts: int32 [16, 64], P('red', 'col'), may hold values from 40 to 48, as said below
Outputs:
- ladder: float32 [128, 32768], P(None, 'col')
Inputs may be any that keep to these rules, and one draw needn't show every extreme that they name: In every device's list, at most 2 slots name tile rows of one range of 16 rows (block_rows // 16), and some range gets exactly 2 within the first 40 slots. `block_counts`: some device has 48 live slots and some 40.
All inputs are finite; a program needn't handle non-finite values. No bound on the sum of `tile_mask` on one device may be relied on, other than what follows from the above.
Results may differ from a plain program's by a relative error of at most 0.0003.
Values may be sent and summed in bfloat16 or wider, within the bound.
No kernel may reach another device: no remote copies, remote signals or barrier semaphores. Data moves between devices by JAX's collectives and lax.ppermute only.
A program may use at most 32 MiB of HBM per device.

v0:
```python
import jax
import jax.numpy as jnp
from jax import lax
from jax.sharding import PartitionSpec as P


def peer_order(owners):
    width = owners.shape[-1]
    same = owners[..., :, None] == owners[..., None, :]
    earlier = jnp.arange(width)[None, :] < jnp.arange(width)[:, None]
    return jnp.sum(same & earlier, axis=-1)


def body(amplitudes, block_tiles, block_rows, tile_mask, block_counts):
    row_ids = block_rows[0, 0]
    slots = row_ids.shape[0]
    col_tiles = tile_mask.shape[-1]
    cols_here = col_tiles * 64
    tile_data = block_tiles[0, 0].reshape(64, slots, cols_here)
    col_mask = jnp.repeat(tile_mask[0, 0], 64, axis=1).astype(jnp.bfloat16)
    masked = tile_data * col_mask[None, :, :]
    alive_mask = (jnp.arange(slots) < block_counts[0, 0]).astype(jnp.bfloat16)
    row_count = amplitudes.shape[0]
    blocks_here = amplitudes.shape[1] // 64
    n_col = lax.axis_size("col")
    capacity = max(2, (slots + n_col - 1) // n_col)
    wanted, wanted_counts = (
        lax.all_gather(row_ids, "col", axis=0, tiled=True),
        lax.all_gather(block_counts[0], "col", axis=0, tiled=True),
    )
    wanted = wanted.reshape(n_col, slots)
    owners = wanted // blocks_here
    within = wanted % blocks_here
    ranks = peer_order(owners)
    alive_all = jnp.arange(slots)[None, :] < wanted_counts[:, None]
    mine = alive_all & (owners == lax.axis_index("col"))
    chosen = (mine[:, None, :] & (ranks[:, None, :] == jnp.arange(capacity)[None, :, None])).astype(
        jnp.int32
    )
    block_index = jnp.sum(chosen * within[:, None, :], axis=-1)
    blocks_first = jnp.transpose(amplitudes.reshape(row_count, blocks_here, 64), (1, 0, 2))
    outgoing = blocks_first[block_index]
    incoming = lax.all_to_all(outgoing, "col", split_axis=0, concat_axis=0, tiled=True)
    own_peers = row_ids // blocks_here
    flat_index = own_peers * capacity + peer_order(own_peers)
    picked = incoming.reshape(n_col * capacity, row_count, 64)[flat_index]
    picked = picked * alive_mask[:, None, None]
    partial_value = jnp.einsum("srk,ksj->rj", picked, masked, preferred_element_type=jnp.float32)
    result = lax.psum(partial_value, "red")
    return result


def solution(mesh):
    placed = (
        P(None, ("red", "col")),
        P("red", "col", None, None),
        P("red", "col", None),
        P("red", "col", None, None),
        P("red", "col"),
    )
    return jax.shard_map(
        body, mesh=mesh, in_specs=placed, out_specs=P(None, "col"), check_vma=False
    )
```

profile of v0, /device:TPU:32, one launch (start us, length us, event | category | flops | bytes accessed | tf_op | source)
XLA Modules:
  0.0 523.2 jit_solution(13215125485242100124)
XLA Ops:
  7.2 1.3 dynamic-slice
  9.1 0.7 and_select_fusion
  9.9 0.7 bitcast_dynamic-update-slice_fusion.1
  10.6 251.2 %all-reduce.2 = (s32[3072]{0:T(1024)S(1)}, s32[64]{0:T(128)S(1)}) all-reduce(s32[3072]{0:T(1024)S(1)} %get-tuple-element.10, s32[64]{0:T(128)S(1)} %bitcast_dynamic-update-slice_fusion.1), channel_id=3, replica_groups=mesh['col'=64,'red'=16] {'col'}, use_global_device_ids=true, to_apply=%add.1 | all-reduce | flops 3136 | bytes 25088
  261.7 0.1 reshape.280
  261.8 0.1 fusion.6
  261.9 0.1 copy.15
  262.0 0.1 copy.14
  262.1 0.1 copy.17
  262.1 0.5 convert_reduce_fusion
  262.7 0.1 copy.18
  262.8 0.1 reshape.284
  262.9 1.1 copy.13
  264.1 2.2 gather_fusion
  266.3 47.3 %all-to-all-start = ((bf16[64,2,128,64]{2,3,1,0:T(8,128)(2,1)}), bf16[64,2,128,64]{2,3,1,0:T(8,128)(2,1)S(1)}, u32[]{:S(2)}, u32[]{:S(2)}) async-start(bf16[64,2,128,64]{2,3,1,0:T(8,128)(2,1)} %bitcast.7), calls=%async_computation | async-start | bytes 4194304 | tf_op jit(solution)/shard_map/all_to_all | solution.py:43
  313.6 0.0 all-reduce.5.cloned.1.call-start
  313.6 0.0 copy-start
  313.6 0.0 copy-start.1
  313.6 4.7 copy.21
  318.4 0.0 copy-done
  318.4 0.1 copy.19
  318.5 0.1 broadcast_in_dim.2
  318.6 0.1 convert_element_type.33
  318.8 0.2 convert_reduce_fusion.1
  318.9 0.0 copy-done.1
  319.0 45.2 %all-to-all-done = bf16[64,2,128,64]{2,3,1,0:T(8,128)(2,1)S(1)} async-done(((bf16[64,2,128,64]{2,3,1,0:T(8,128)(2,1)}), bf16[64,2,128,64]{2,3,1,0:T(8,128)(2,1)S(1)}, u32[]{:S(2)}, u32[]{:S(2)}) %all-to-all-start) | async-done | bytes 2097184 | tf_op jit(solution)/shard_map/all_to_all | solution.py:43
  364.2 0.7 gather_fusion.1
  364.9 6.2 %fusion.2 = f32[128,512]{1,0:T(8,128)} fusion(bf16[64,48,512]{2,1,0:T(8,128)(2,1)} %bitcast.51, bf16[48,512]{1,0:T(8,128)(2,1)S(1)} %convert_element_type.33, bf16[48,128,64]{1,2,0:T(8,128)(2,1)S(1)} %gather_fusion.1, bf16[48]{0:T(256)(128)(2,1)S(1)} %compare_convert_fusion), kind=kOutput, calls=%fused_computation.6 | convolution fusion | flops 404619264 | bytes 4243552 | tf_op jit(solution)/shard_map/srk,ksj->rj/dot_general | solution.py:48
  371.1 0.0 all-reduce.5.cloned.1.call-update
  371.1 143.5 %all-reduce.5.cloned.1.call-done = f32[128,512]{1,0:T(8,128)} async-done(((f32[128,512]{1,0:T(8,128)}), f32[128,512]{1,0:T(8,128)}) %all-reduce.5.cloned.1.call-update) | async-done | bytes 262160 | tf_op jit(solution)/shard_map/psum | solution.py:49
  514.6 1.7 copy.30
  (11 shorter events, 0.1 us)
Async XLA Ops:
  266.3 97.9 %all-to-all-start = ((bf16[64,2,128,64]{2,3,1,0:T(8,128)(2,1)}), bf16[64,2,128,64]{2,3,1,0:T(8,128)(2,1)S(1)}, u32[]{:S(2)}, u32[]{:S(2)}) async-start(bf16[64,2,128,64]{2,3,1,0:T(8,128)(2,1)} %bitcast.7), calls=%async_computation | async-start | bytes 4194304 | tf_op jit(solution)/shard_map/all_to_all | solution.py:43
  313.6 201.1 %all-reduce.5.cloned.1.call-start = ((), (), s32[]{:S(2)}) async-start(), calls=%async_computation.1 | async-start | bytes 524288 | tf_op jit(solution)/shard_map/psum | solution.py:49
  313.6 4.8 copy-start
  313.6 5.3 %copy-start.1 = (s32[1,1,48]{2,1,0:T(1,128)S(1)}, s32[1,1,48]{2,1,0:T(1,128)}, u32[]{:S(2)}) copy-start(s32[1,1,48]{2,1,0:T(1,128)} %param.7) | copy-start | bytes 580
Sparse Core Ops, SparseCore 0:
  371.3 143.3 all-reduce.4
where the time goes:
time: 524 us; the launch traced here: 523 us
  blocking collectives  251 us (48%)
  waiting for transfers between devices  189 us (36%)
  starting transfers between devices  47.3 us (9%)
  between operations  14.8 us (3%)
  local copies, waits for them, and re-layouts  13.3 us (3%)
  matrix products  6.25 us (1%)
    unnamed x1, blocking collectives  251 us
    psum x1, waiting for transfers between devices, body(): result = lax.psum(partial_value, 'red')  144 us
    all_to_all x1, starting transfers between devices, body(): lax.all_to_all(outgoing, 'col', split_axis=0, concat_axis=0, tiled=True)  47.3 us
    all_to_all x1, waiting for transfers between devices, body(): lax.all_to_all(outgoing, 'col', split_axis=0, concat_axis=0, tiled=True)  45.2 us
  transfers between devices with their start and end apart: 2, of which 2 were waited for; matrix products, arithmetic and copies ran while one was open for 1% of the time, Pallas kernels for 0%

commit v1 on v0

v1 whole, which is shorter than its diff:
```python
import jax
import jax.numpy as jnp
from jax import lax
from jax.sharding import PartitionSpec as P

BLOCK = 64
CAP = 2


def peer_rank(owners):
    width = owners.shape[0]
    same = owners[:, None] == owners[None, :]
    earlier = jnp.arange(width)[None, :] < jnp.arange(width)[:, None]
    return jnp.sum((same & earlier).astype(jnp.int32), axis=-1)


def body(amplitudes, block_tiles, block_rows, tile_mask, block_counts):
    row_ids = block_rows[0, 0]
    slots = row_ids.shape[0]
    col_tiles = tile_mask.shape[-1]
    cols_here = col_tiles * BLOCK
    rows = amplitudes.shape[0]
    blocks_here = amplitudes.shape[1] // BLOCK
    n_col = lax.axis_size("col")
    n_red = lax.axis_size("red")
    alive = jnp.arange(slots) < block_counts[0, 0]

    owners = row_ids // blocks_here
    place = owners * CAP + peer_rank(owners)
    here = (place[None, :] == jnp.arange(n_col * CAP)[:, None]) & alive[None, :]
    ask = jnp.sum(jnp.where(here, (row_ids % blocks_here + 1)[None, :], 0), axis=-1)
    asked = lax.all_to_all(ask.reshape(n_col, CAP), "col", split_axis=0, concat_axis=0, tiled=True)

    blocks = amplitudes.T.reshape(blocks_here, BLOCK, rows)
    outgoing = blocks[jnp.maximum(asked - 1, 0)]
    incoming = lax.all_to_all(outgoing, "col", split_axis=0, concat_axis=0, tiled=True)

    tile_data = block_tiles[0, 0].reshape(BLOCK, slots, cols_here)
    keep = jnp.repeat(tile_mask[0, 0], BLOCK, axis=1).astype(jnp.bfloat16)
    masked = tile_data * keep[None, :, :]
    picked = incoming.reshape(n_col * CAP, BLOCK, rows)[place]
    picked = picked * alive.astype(jnp.bfloat16)[:, None, None]
    partial_value = jnp.einsum("skr,ksj->rj", picked, masked, preferred_element_type=jnp.float32)

    slices = partial_value.reshape(n_red, rows // n_red, cols_here)
    gathered = lax.all_to_all(slices, "red", split_axis=0, concat_axis=0, tiled=True)
    mine = jnp.sum(gathered, axis=0)
    copies = jnp.broadcast_to(mine[None], gathered.shape)
    whole = lax.all_to_all(copies, "red", split_axis=0, concat_axis=0, tiled=True)
    return whole.reshape(rows, cols_here)


def solution(mesh):
    placed = (
        P(None, ("red", "col")),
        P("red", "col", None, None),
        P("red", "col", None),
        P("red", "col", None, None),
        P("red", "col"),
    )
    return jax.shard_map(
        body, mesh=mesh, in_specs=placed, out_specs=P(None, "col"), check_vma=False
    )
```

time: 524 us -> 141 us (0.27)
  the two profiles are of different devices: /device:TPU:32 before, /device:TPU:114 now
where the time goes in v1:
time: 141 us; the launch traced here: 140 us
  waiting for transfers between devices  52.8 us (37%)
  blocking collectives  34 us (24%)
  starting transfers between devices  30.4 us (22%)
  local copies, waits for them, and re-layouts  13.8 us (10%)
  other arithmetic  5.17 us (4%)
  matrix products  3.25 us (2%)
    all_to_all x1, waiting for transfers between devices, body(): lax.all_to_all(outgoing, 'col', split_axis=0, concat_axis=0, tiled=True)  46.6 us
    all_to_all x1, starting transfers between devices, body(): lax.all_to_all(ask.reshape(n_col, CAP), 'col', split_axis=0, concat_axis=...  22.4 us
    all_to_all x1, blocking collectives, body(): lax.all_to_all(slices, 'red', split_axis=0, concat_axis=0, tiled=True)  18.7 us
    all_to_all x1, blocking collectives, body(): lax.all_to_all(copies, 'red', split_axis=0, concat_axis=0, tiled=True)  15.2 us
    all_to_all x1, starting transfers between devices, body(): lax.all_to_all(outgoing, 'col', split_axis=0, concat_axis=0, tiled=True)  8.07 us
    all_to_all x1, waiting for transfers between devices, body(): lax.all_to_all(ask.reshape(n_col, CAP), 'col', split_axis=0, concat_axis=...  6.26 us
    unnamed x5, local copies, waits for them, and re-layouts  4.7 us
    dot_general x1, matrix products, body(): jnp.einsum('skr,ksj->rj', picked, masked, preferred_element_type=jnp.floa...  3.25 us
  transfers between devices with their start and end apart: 2, of which 2 were waited for; matrix products, arithmetic and copies ran while one was open for 5% of the time, Pallas kernels for 0%

profile of v1, /device:TPU:114, one launch (start us, length us, event | category | flops | bytes accessed | tf_op | source)
XLA Modules:
  0.0 140.2 jit_solution(4414500485808489664)
XLA Ops:
  0.7 0.7 and_select_fusion.2
  1.3 0.2 convert_reduce_fusion
  1.5 0.1 select_reduce_fusion
  1.6 0.8 all_to_all.15
  2.4 22.4 %all-to-all-start = ((s32[64,1,2]{2,1,0:T(1,128)}), s32[64,1,2]{2,1,0:T(1,128)S(1)}, u32[]{:S(2)}, u32[]{:S(2)}) async-start(s32[64,1,2]{2,1,0:T(1,128)} %bitcast.4), calls=%async_computation | async-start | bytes 65536 | tf_op jit(solution)/shard_map/all_to_all | solution.py:32
  24.8 0.7 convert_bitcast_fusion
  25.5 0.1 copy.21
  25.6 0.1 broadcast_in_dim.18
  25.7 0.1 convert_element_type.28
  25.8 1.1 copy.18
  26.9 6.3 %all-to-all-done = s32[64,1,2]{2,1,0:T(1,128)S(1)} async-done(((s32[64,1,2]{2,1,0:T(1,128)}), s32[64,1,2]{2,1,0:T(1,128)S(1)}, u32[]{:S(2)}, u32[]{:S(2)}) %all-to-all-start) | async-done | bytes 544 | tf_op jit(solution)/shard_map/all_to_all | solution.py:32
  33.2 0.1 maximum_reduce_fusion
  33.3 0.1 reshape.219
  33.4 2.2 %gather_fusion = bf16[128,64,128]{2,1,0:T(8,128)(2,1)} fusion(bf16[16,64,128]{2,1,0:T(8,128)(2,1)S(1)} %bitcast.57, s32[1024]{0:T(1024)S(1)} %pad_clamp_fusion.1), kind=kCustom, calls=%fused_computation | custom fusion | bytes 4194816 | tf_op jit(solution)/shard_map/gather | solution.py:35
  35.6 8.1 %all-to-all-start.1 = ((bf16[64,2,64,128]{3,2,1,0:T(8,128)(2,1)}), bf16[64,2,64,128]{3,2,1,0:T(8,128)(2,1)S(1)}, u32[]{:S(2)}, u32[]{:S(2)}) async-start(bf16[64,2,64,128]{3,2,1,0:T(8,128)(2,1)} %bitcast.5), calls=%async_computation.1 | async-start | bytes 4194304 | tf_op jit(solution)/shard_map/all_to_all | solution.py:36
  43.7 2.3 %broadcast_multiply_fusion = bf16[1,1,64,24576]{3,2,1,0:T(8,128)(2,1)S(1)} fusion(bf16[1,1,64,24576]{3,2,1,0:T(8,128)(2,1)} %param.6, bf16[24576]{0:T(1024)(128)(2,1)S(1)} %convert_element_type.28), kind=kLoop, calls=%fused_computation.2 | loop fusion | flops 1572864 | bytes 6340608 | tf_op jit(solution)/shard_map/mul | solution.py:40
  46.0 0.0 copy-start
  46.0 2.9 %copy.24 = bf16[8,8,48,512]{3,2,1,0:T(8,128)(2,1)} copy(bf16[8,8,48,512]{3,1,2,0:T(8,128)(2,1)S(1)} %bitcast.58) | data formatting | bytes 6291456
  48.9 0.0 copy-done
  49.0 46.6 %all-to-all-done.1 = bf16[64,2,64,128]{3,2,1,0:T(8,128)(2,1)S(1)} async-done(((bf16[64,2,64,128]{3,2,1,0:T(8,128)(2,1)}), bf16[64,2,64,128]{3,2,1,0:T(8,128)(2,1)S(1)}, u32[]{:S(2)}, u32[]{:S(2)}) %all-to-all-start.1) | async-done | bytes 2097184 | tf_op jit(solution)/shard_map/all_to_all | solution.py:36
  95.5 0.7 gather_fusion.1
  96.2 1.0 multiply_bitcast_fusion
  97.3 1.9 %copy.20 = bf16[128,64,48]{1,2,0:T(8,128)(2,1)S(1)} copy(bf16[128,64,48]{0,1,2:T(8,128)(2,1)} %multiply_bitcast_fusion) | data formatting | bytes 1572864 | tf_op jit(solution)/shard_map/mul | solution.py:42
  99.1 3.1 %copy.22 = bf16[16,8,64,48]{3,1,2,0:T(8,128)(2,1)} copy(bf16[16,8,64,48]{2,3,1,0:T(8,128)(2,1)S(1)} %bitcast.59) | data formatting | bytes 1572864 | tf_op jit(solution)/shard_map/skr,ksj->rj/dot_general | solution.py:43
  102.2 3.3 %convolution_bitcast_fusion = f32[16,8,512]{2,1,0:T(8,128)S(1)} fusion(bf16[16,8,64,48]{3,1,2,0:T(8,128)(2,1)} %copy.22, bf16[64,48,512,1]{2,1,0,3:T(8,128)(2,1)} %bitcast.61), kind=kOutput, calls=%fused_computation.3 | convolution fusion | flops 402653184 | bytes 4194304 | tf_op jit(solution)/shard_map/skr,ksj->rj/dot_general | solution.py:43
  105.5 18.7 %all_to_all.24 = f32[16,8,512]{2,1,0:T(8,128)S(1)} all-to-all(f32[16,8,512]{2,1,0:T(8,128)S(1)} %convolution_bitcast_fusion), channel_id=1, replica_groups=mesh['col'=64,'red'=16] {'red'}, dimensions={0} | all-to-all | bytes 524288 | tf_op jit(solution)/shard_map/all_to_all | solution.py:46
  124.3 15.2 %all_to_all.25 = f32[16,8,512]{2,1,0:T(8,128)S(1)} all-to-all(f32[16,8,512]{2,1,0:T(8,128)S(1)} %broadcast_in_dim.19), channel_id=1, replica_groups=mesh['col'=64,'red'=16] {'red'}, dimensions={0} | all-to-all | bytes 524288 | tf_op jit(solution)/shard_map/all_to_all | solution.py:49
  139.5 0.7 copy.27
  (8 shorter events, 0.1 us)
Async XLA Ops:
  2.4 30.8 %all-to-all-start = ((s32[64,1,2]{2,1,0:T(1,128)}), s32[64,1,2]{2,1,0:T(1,128)S(1)}, u32[]{:S(2)}, u32[]{:S(2)}) async-start(s32[64,1,2]{2,1,0:T(1,128)} %bitcast.4), calls=%async_computation | async-start | bytes 65536 | tf_op jit(solution)/shard_map/all_to_all | solution.py:32
  35.6 59.9 %all-to-all-start.1 = ((bf16[64,2,64,128]{3,2,1,0:T(8,128)(2,1)}), bf16[64,2,64,128]{3,2,1,0:T(8,128)(2,1)S(1)}, u32[]{:S(2)}, u32[]{:S(2)}) async-start(bf16[64,2,64,128]{3,2,1,0:T(8,128)(2,1)} %bitcast.5), calls=%async_computation.1 | async-start | bytes 4194304 | tf_op jit(solution)/shard_map/all_to_all | solution.py:36
  46.0 2.9 %copy-start = (s32[1,1,48]{2,1,0:T(1,128)S(1)}, s32[1,1,48]{2,1,0:T(1,128)}, u32[]{:S(2)}) copy-start(s32[1,1,48]{2,1,0:T(1,128)} %param.7) | copy-start | bytes 580

commit v2 on v1

--- a/solution.py
+++ b/solution.py
@@ -1,10 +1,13 @@
 import jax
 import jax.numpy as jnp
 from jax import lax
+from jax.experimental import pallas as pl
+from jax.experimental.pallas import tpu as pltpu
 from jax.sharding import PartitionSpec as P
 
 BLOCK = 64
 CAP = 2
+GROUP = 4
 
 
 def peer_rank(owners):
@@ -12,6 +15,66 @@
     same = owners[:, None] == owners[None, :]
     earlier = jnp.arange(width)[None, :] < jnp.arange(width)[:, None]
     return jnp.sum((same & earlier).astype(jnp.int32), axis=-1)
+
+
+def contract_kernel(place, blocks, tiles, keep, out, a_buf, w_buf, a_sem, w_sem):
+    slots, cols = keep.shape
+    groups = slots // GROUP
+
+    def a_copy(s):
+        return pltpu.make_async_copy(
+            blocks.at[place[s]], a_buf.at[pl.ds(s * BLOCK, BLOCK)], a_sem.at[s]
+        )
+
+    def w_copy(s):
+        return pltpu.make_async_copy(
+            tiles.at[:, pl.ds(s * cols, cols)], w_buf.at[pl.ds(s * BLOCK, BLOCK)], w_sem.at[s]
+        )
+
+    for s in range(slots):
+        w_copy(s).start()
+        a_copy(s).start()
+    total = jnp.zeros(out.shape, jnp.float32)
+    for g in range(groups):
+        parts = []
+        for s in range(g * GROUP, (g + 1) * GROUP):
+            a_copy(s).wait()
+            w_copy(s).wait()
+            parts.append(w_buf[pl.ds(s * BLOCK, BLOCK), :] * keep[pl.ds(s, 1), :])
+        lhs = a_buf[pl.ds(g * GROUP * BLOCK, GROUP * BLOCK), :]
+        total += lax.dot_general(
+            lhs,
+            jnp.concatenate(parts, axis=0),
+            (((0,), (0,)), ((), ())),
+            preferred_element_type=jnp.float32,
+        )
+    out[...] = total
+
+
+def contract(place, blocks, tiles, keep):
+    slots, cols = keep.shape
+    rows = blocks.shape[-1]
+    return pl.pallas_call(
+        contract_kernel,
+        out_shape=jax.ShapeDtypeStruct((rows, cols), jnp.float32),
+        in_specs=[
+            pl.BlockSpec(memory_space=pltpu.SMEM),
+            pl.BlockSpec(memory_space=pl.ANY),
+            pl.BlockSpec(memory_space=pl.ANY),
+            pl.BlockSpec(memory_space=pltpu.VMEM),
+        ],
+        out_specs=pl.BlockSpec(memory_space=pltpu.VMEM),
+        scratch_shapes=[
+            pltpu.VMEM((slots * BLOCK, rows), jnp.bfloat16),
+            pltpu.VMEM((slots * BLOCK, cols), jnp.bfloat16),
+            pltpu.SemaphoreType.DMA((slots,)),
+            pltpu.SemaphoreType.DMA((slots,)),
+        ],
+        compiler_params=pltpu.CompilerParams(vmem_limit_bytes=16 * 1024 * 1024),
+        cost_estimate=pl.CostEstimate(
+            flops=2 * slots * BLOCK * rows * cols, bytes_accessed=4 * 1024 * 1024, transcendentals=0
+        ),
+    )(place, blocks, tiles, keep)
 
 
 def body(amplitudes, block_tiles, block_rows, tile_mask, block_counts):
@@ -35,12 +98,13 @@
     outgoing = blocks[jnp.maximum(asked - 1, 0)]
     incoming = lax.all_to_all(outgoing, "col", split_axis=0, concat_axis=0, tiled=True)
 
-    tile_data = block_tiles[0, 0].reshape(BLOCK, slots, cols_here)
-    keep = jnp.repeat(tile_mask[0, 0], BLOCK, axis=1).astype(jnp.bfloat16)
-    masked = tile_data * keep[None, :, :]
-    picked = incoming.reshape(n_col * CAP, BLOCK, rows)[place]
-    picked = picked * alive.astype(jnp.bfloat16)[:, None, None]
-    partial_value = jnp.einsum("skr,ksj->rj", picked, masked, preferred_element_type=jnp.float32)
+    keep = jnp.repeat(tile_mask[0, 0] * alive[:, None], BLOCK, axis=1).astype(jnp.bfloat16)
+    partial_value = contract(
+        jnp.clip(place, 0, n_col * CAP - 1),
+        incoming.reshape(n_col * CAP, BLOCK, rows),
+        block_tiles[0, 0],
+        keep,
+    )
 
     slices = partial_value.reshape(n_red, rows // n_red, cols_here)
     gathered = lax.all_to_all(slices, "red", split_axis=0, concat_axis=0, tiled=True)

time: 141 us -> 138 us (0.979)
  local copies, waits for them, and re-layouts: 13.8 us -> 7.14 us
  waiting for transfers between devices: 52.8 us -> 58.8 us
  Pallas kernels: 0 us -> 4.84 us
  other arithmetic: 5.17 us -> 1.1 us
  matrix products: 3.25 us -> 0 us
    all_to_all x1, waiting for transfers between devices: 46.6 us -> 51.5 us  [body(): lax.all_to_all(outgoing, 'col', split_axis=0, concat_axis=0, tiled=True)]
    pallas_call x0 -> x1, Pallas kernels: none -> 4.84 us  [contract(): pl.pallas_call(contract_kernel, out_shape=jax.ShapeDtypeStruct((rows, col...]
    mul x2 -> x0, other arithmetic: 3.34 us -> none  [the longest x1 2.34 us: body(): masked = tile_data * keep[None, :, :]]
    dot_general x1 -> x0, matrix products: 3.25 us -> none  [body(): jnp.einsum('skr,ksj->rj', picked, masked, preferred_element_type=jnp.floa...]
    dot_general x1 -> x0, local copies, waits for them, and re-layouts: 3.07 us -> none  [body(): jnp.einsum('skr,ksj->rj', picked, masked, preferred_element_type=jnp.floa...]
    mul x1 -> x0, local copies, waits for them, and re-layouts: 1.89 us -> none  [body(): picked = picked * alive.astype(jnp.bfloat16)[:, None, None]]
    unnamed x5 -> x6, local copies, waits for them, and re-layouts: 4.7 us -> 3.71 us
  transfers between devices with their start and end apart: 2 -> 2, of which waited for: 2 -> 2; matrix products, arithmetic and copies ran while one was open for 5% -> 1% of each run, Pallas kernels for 0% -> 0%
where the time goes in v2:
time: 138 us; the launch traced here: 137 us
  waiting for transfers between devices  58.8 us (43%)
  blocking collectives  34 us (25%)
  starting transfers between devices  30.6 us (22%)
  local copies, waits for them, and re-layouts  7.14 us (5%)
  Pallas kernels  4.84 us (4%)
    all_to_all x1, waiting for transfers between devices, body(): lax.all_to_all(outgoing, 'col', split_axis=0, concat_axis=0, tiled=True)  51.5 us
    all_to_all x1, starting transfers between devices, body(): lax.all_to_all(ask.reshape(n_col, CAP), 'col', split_axis=0, concat_axis=...  22.4 us
    all_to_all x1, blocking collectives, body(): lax.all_to_all(slices, 'red', split_axis=0, concat_axis=0, tiled=True)  18.7 us
    all_to_all x1, blocking collectives, body(): lax.all_to_all(copies, 'red', split_axis=0, concat_axis=0, tiled=True)  15.2 us
    all_to_all x1, starting transfers between devices, body(): lax.all_to_all(outgoing, 'col', split_axis=0, concat_axis=0, tiled=True)  8.2 us
    all_to_all x1, waiting for transfers between devices, body(): lax.all_to_all(ask.reshape(n_col, CAP), 'col', split_axis=0, concat_axis=...  7.28 us
    pallas_call x1, Pallas kernels, contract(): pl.pallas_call(contract_kernel, out_shape=jax.ShapeDtypeStruct((rows, col...  4.84 us
    unnamed x6, local copies, waits for them, and re-layouts  3.71 us
  transfers between devices with their start and end apart: 2, of which 2 were waited for; matrix products, arithmetic and copies ran while one was open for 1% of the time, Pallas kernels for 0%

profile of v2, /device:TPU:114, one launch (start us, length us, event | category | flops | bytes accessed | tf_op | source)
XLA Modules:
  0.0 137.1 jit_solution(13750422705968523696)
XLA Ops:
  0.0 0.7 fusion.3
  0.7 0.2 convert_reduce_fusion
  1.5 0.1 select_reduce_fusion
  1.6 0.8 all_to_all.15
  2.4 22.4 %all-to-all-start = ((s32[64,1,2]{2,1,0:T(1,128)}), s32[64,1,2]{2,1,0:T(1,128)S(1)}, u32[]{:S(2)}, u32[]{:S(2)}) async-start(s32[64,1,2]{2,1,0:T(1,128)} %bitcast.4), calls=%async_computation | async-start | bytes 65536 | tf_op jit(solution)/shard_map/all_to_all | solution.py:95
  24.8 1.1 copy.13
  25.9 7.3 %all-to-all-done = s32[64,1,2]{2,1,0:T(1,128)S(1)} async-done(((s32[64,1,2]{2,1,0:T(1,128)}), s32[64,1,2]{2,1,0:T(1,128)S(1)}, u32[]{:S(2)}, u32[]{:S(2)}) %all-to-all-start) | async-done | bytes 544 | tf_op jit(solution)/shard_map/all_to_all | solution.py:95
  33.2 0.1 maximum_reduce_fusion
  33.3 0.1 reshape.143
  33.4 2.2 %gather_fusion = bf16[128,64,128]{2,1,0:T(8,128)(2,1)} fusion(bf16[16,64,128]{2,1,0:T(8,128)(2,1)S(1)} %bitcast.33, s32[1024]{0:T(1024)S(1)} %pad_clamp_fusion), kind=kCustom, calls=%fused_computation | custom fusion | bytes 4194816 | tf_op jit(solution)/shard_map/gather | solution.py:98
  35.6 0.0 copy-start.1
  35.6 8.2 %all-to-all-start.1 = ((bf16[64,2,64,128]{3,2,1,0:T(8,128)(2,1)}), bf16[64,2,64,128]{3,2,1,0:T(8,128)(2,1)S(1)}, u32[]{:S(2)}, u32[]{:S(2)}) async-start(bf16[64,2,64,128]{3,2,1,0:T(8,128)(2,1)} %bitcast.34), calls=%async_computation.1 | async-start | bytes 4194304 | tf_op jit(solution)/shard_map/all_to_all | solution.py:99
  43.8 0.0 copy-done.1
  43.8 0.1 copy.15
  43.9 0.1 broadcast_in_dim.18
  44.0 0.1 convert_element_type.19.keep
  44.2 51.5 %all-to-all-done.1 = bf16[64,2,64,128]{3,2,1,0:T(8,128)(2,1)S(1)} async-done(((bf16[64,2,64,128]{3,2,1,0:T(8,128)(2,1)}), bf16[64,2,64,128]{3,2,1,0:T(8,128)(2,1)S(1)}, u32[]{:S(2)}, u32[]{:S(2)}) %all-to-all-start.1) | async-done | bytes 2097184 | tf_op jit(solution)/shard_map/all_to_all | solution.py:99
  95.7 0.0 copy-start
  95.7 1.9 %copy-done = bf16[1,1,64,24576]{3,2,1,0:T(8,128)(2,1)S(1)} copy-done((bf16[1,1,64,24576]{3,2,1,0:T(8,128)(2,1)S(1)}, bf16[1,1,64,24576]{3,2,1,0:T(8,128)(2,1)}, u32[]{:S(2)}) %copy-start) | copy-done | bytes 3145752
  97.5 4.8 %shard_map.55 = f32[128,512]{1,0:T(8,128)S(1)} custom-call(s32[48]{0:T(128)S(1)} %get-tuple-element.5.place, bf16[128,64,128]{2,1,0:T(8,128)(2,1)S(1)} %bitcast.30, bf16[64,24576]{1,0:T(8,128)(2,1)S(1)} %bitcast.31, bf16[48,512]{1,0:T(8,128)(2,1)S(1)} %convert_element_type.19.keep), custom_call_target="tpu_custom_call" | custom-call | flops 402653184 | bytes 4194304 | tf_op jit(solution)/shard_map/pallas_call | solution.py:57
  102.4 18.7 %all_to_all.24 = f32[16,8,512]{2,1,0:T(8,128)S(1)} all-to-all(f32[16,8,512]{2,1,0:T(8,128)S(1)} %bitcast.32), channel_id=1, replica_groups=mesh['col'=64,'red'=16] {'red'}, dimensions={0} | all-to-all | bytes 524288 | tf_op jit(solution)/shard_map/all_to_all | solution.py:110
  121.2 15.2 %all_to_all.25 = f32[16,8,512]{2,1,0:T(8,128)S(1)} all-to-all(f32[16,8,512]{2,1,0:T(8,128)S(1)} %broadcast_in_dim.19), channel_id=1, replica_groups=mesh['col'=64,'red'=16] {'red'}, dimensions={0} | all-to-all | bytes 524288 | tf_op jit(solution)/shard_map/all_to_all | solution.py:113
  136.4 0.7 copy.18
  (6 shorter events, 0.1 us)
Async XLA Ops:
  2.4 30.8 %all-to-all-start = ((s32[64,1,2]{2,1,0:T(1,128)}), s32[64,1,2]{2,1,0:T(1,128)S(1)}, u32[]{:S(2)}, u32[]{:S(2)}) async-start(s32[64,1,2]{2,1,0:T(1,128)} %bitcast.4), calls=%async_computation | async-start | bytes 65536 | tf_op jit(solution)/shard_map/all_to_all | solution.py:95
  35.6 8.2 %copy-start.1 = (s32[1,1,48,8]{2,3,1,0:T(8,128)S(1)}, s32[1,1,48,8]{2,3,1,0:T(8,128)}, u32[]{:S(2)}) copy-start(s32[1,1,48,8]{2,3,1,0:T(8,128)} %param.8) | copy-start | bytes 4612
  35.6 60.1 %all-to-all-start.1 = ((bf16[64,2,64,128]{3,2,1,0:T(8,128)(2,1)}), bf16[64,2,64,128]{3,2,1,0:T(8,128)(2,1)S(1)}, u32[]{:S(2)}, u32[]{:S(2)}) async-start(bf16[64,2,64,128]{3,2,1,0:T(8,128)(2,1)} %bitcast.34), calls=%async_computation.1 | async-start | bytes 4194304 | tf_op jit(solution)/shard_map/all_to_all | solution.py:99
  95.7 1.9 %copy-start = (bf16[1,1,64,24576]{3,2,1,0:T(8,128)(2,1)S(1)}, bf16[1,1,64,24576]{3,2,1,0:T(8,128)(2,1)}, u32[]{:S(2)}) copy-start(bf16[1,1,64,24576]{3,2,1,0:T(8,128)(2,1)} %param.6) | copy-start | bytes 9437188

commit v3 on v1

--- a/solution.py
+++ b/solution.py
@@ -1,10 +1,13 @@
 import jax
 import jax.numpy as jnp
 from jax import lax
+from jax.experimental import pallas as pl
+from jax.experimental.pallas import tpu as pltpu
 from jax.sharding import PartitionSpec as P
 
 BLOCK = 64
 CAP = 2
+GROUP = 4
 
 
 def peer_rank(owners):
@@ -12,6 +15,78 @@
     same = owners[:, None] == owners[None, :]
     earlier = jnp.arange(width)[None, :] < jnp.arange(width)[:, None]
     return jnp.sum((same & earlier).astype(jnp.int32), axis=-1)
+
+
+def stack_kernel(tiles, keep, out, buf, sem):
+    slots, cols = keep.shape
+    chunks, _, width = buf.shape
+    each = slots // chunks
+
+    def copy(i):
+        return pltpu.make_async_copy(tiles.at[:, pl.ds(i * width, width)], buf.at[i], sem.at[i])
+
+    for i in range(chunks):
+        copy(i).start()
+    for i in range(chunks):
+        copy(i).wait()
+        for j in range(each):
+            s = i * each + j
+            out[pl.ds(s * BLOCK, BLOCK), :] = buf[i, :, pl.ds(j * cols, cols)] * keep[pl.ds(s, 1), :]
+
+
+def stack(tiles, keep):
+    slots, cols = keep.shape
+    chunks = slots // GROUP
+    return pl.pallas_call(
+        stack_kernel,
+        out_shape=jax.ShapeDtypeStruct((slots * BLOCK, cols), tiles.dtype),
+        in_specs=[
+            pl.BlockSpec(memory_space=pl.ANY),
+            pl.BlockSpec(memory_space=pltpu.VMEM),
+        ],
+        out_specs=pl.BlockSpec(memory_space=pltpu.VMEM),
+        scratch_shapes=[
+            pltpu.VMEM((chunks, BLOCK, GROUP * cols), tiles.dtype),
+            pltpu.SemaphoreType.DMA((chunks,)),
+        ],
+        compiler_params=pltpu.CompilerParams(vmem_limit_bytes=16 * 1024 * 1024),
+        cost_estimate=pl.CostEstimate(
+            flops=slots * BLOCK * cols, bytes_accessed=4 * slots * BLOCK * cols, transcendentals=0
+        ),
+    )(tiles, keep)
+
+
+def contract_kernel(place, blocks, weights, out):
+    total = jnp.zeros(out.shape, jnp.float32)
+    depth = GROUP * BLOCK
+    for g in range(weights.shape[0] // depth):
+        lhs = jnp.concatenate([blocks[place[g * GROUP + s]] for s in range(GROUP)], axis=0)
+        total += lax.dot_general(
+            lhs,
+            weights[pl.ds(g * depth, depth), :],
+            (((0,), (0,)), ((), ())),
+            preferred_element_type=jnp.float32,
+        )
+    out[...] = total
+
+
+def contract(place, blocks, weights):
+    depth, cols = weights.shape
+    rows = blocks.shape[-1]
+    return pl.pallas_call(
+        contract_kernel,
+        out_shape=jax.ShapeDtypeStruct((rows, cols), jnp.float32),
+        in_specs=[
+            pl.BlockSpec(memory_space=pltpu.SMEM),
+            pl.BlockSpec(memory_space=pltpu.VMEM),
+            pl.BlockSpec(memory_space=pltpu.VMEM),
+        ],
+        out_specs=pl.BlockSpec(memory_space=pltpu.VMEM),
+        compiler_params=pltpu.CompilerParams(vmem_limit_bytes=16 * 1024 * 1024),
+        cost_estimate=pl.CostEstimate(
+            flops=2 * depth * rows * cols, bytes_accessed=5 * 1024 * 1024, transcendentals=0
+        ),
+    )(place, blocks, weights)
 
 
 def body(amplitudes, block_tiles, block_rows, tile_mask, block_counts):
@@ -35,12 +110,11 @@
     outgoing = blocks[jnp.maximum(asked - 1, 0)]
     incoming = lax.all_to_all(outgoing, "col", split_axis=0, concat_axis=0, tiled=True)
 
-    tile_data = block_tiles[0, 0].reshape(BLOCK, slots, cols_here)
-    keep = jnp.repeat(tile_mask[0, 0], BLOCK, axis=1).astype(jnp.bfloat16)
-    masked = tile_data * keep[None, :, :]
-    picked = incoming.reshape(n_col * CAP, BLOCK, rows)[place]
-    picked = picked * alive.astype(jnp.bfloat16)[:, None, None]
-    partial_value = jnp.einsum("skr,ksj->rj", picked, masked, preferred_element_type=jnp.float32)
+    keep = jnp.repeat(tile_mask[0, 0] * alive[:, None], BLOCK, axis=1).astype(jnp.bfloat16)
+    weights = stack(block_tiles[0, 0], keep)
+    partial_value = contract(
+        jnp.clip(place, 0, n_col * CAP - 1), incoming.reshape(n_col * CAP, BLOCK, rows), weights
+    )
 
     slices = partial_value.reshape(n_red, rows // n_red, cols_here)
     gathered = lax.all_to_all(slices, "red", split_axis=0, concat_axis=0, tiled=True)

time: 141 us -> 134 us (0.950)
  local copies, waits for them, and re-layouts: 13.8 us -> 7.08 us
  other arithmetic: 5.17 us -> 1.11 us
  waiting for transfers between devices: 52.8 us -> 56.3 us
  matrix products: 3.25 us -> 0 us
  Pallas kernels: 0 us -> 2.83 us
    mul x2 -> x0, other arithmetic: 3.34 us -> none  [the longest x1 2.34 us: body(): masked = tile_data * keep[None, :, :]]
    dot_general x1 -> x0, matrix products: 3.25 us -> none  [body(): jnp.einsum('skr,ksj->rj', picked, masked, preferred_element_type=jnp.floa...]
    dot_general x1 -> x0, local copies, waits for them, and re-layouts: 3.07 us -> none  [body(): jnp.einsum('skr,ksj->rj', picked, masked, preferred_element_type=jnp.floa...]
    pallas_call x0 -> x2, Pallas kernels: none -> 2.83 us  [the longest x1 2.21 us: contract(): pl.pallas_call(contract_kernel, out_shape=jax.ShapeDtypeStruct((rows, col...]
    all_to_all x1, waiting for transfers between devices: 46.6 us -> 49 us  [body(): lax.all_to_all(outgoing, 'col', split_axis=0, concat_axis=0, tiled=True)]
    mul x1 -> x0, local copies, waits for them, and re-layouts: 1.89 us -> none  [body(): picked = picked * alive.astype(jnp.bfloat16)[:, None, None]]
    unnamed x5 -> x6, local copies, waits for them, and re-layouts: 4.7 us -> 3.71 us
  transfers between devices with their start and end apart: 2 -> 2, of which waited for: 2 -> 2; matrix products, arithmetic and copies ran while one was open for 5% -> 1% of each run, Pallas kernels for 0% -> 0%
where the time goes in v3:
time: 134 us; the launch traced here: 133 us
  waiting for transfers between devices  56.3 us (42%)
  blocking collectives  33.9 us (25%)
  starting transfers between devices  31.3 us (23%)
  local copies, waits for them, and re-layouts  7.08 us (5%)
  Pallas kernels  2.83 us (2%)
    all_to_all x1, waiting for transfers between devices, body(): lax.all_to_all(outgoing, 'col', split_axis=0, concat_axis=0, tiled=True)  49 us
    all_to_all x1, starting transfers between devices, body(): lax.all_to_all(ask.reshape(n_col, CAP), 'col', split_axis=0, concat_axis=...  22.4 us
    all_to_all x1, blocking collectives, body(): lax.all_to_all(slices, 'red', split_axis=0, concat_axis=0, tiled=True)  18.6 us
    all_to_all x1, blocking collectives, body(): lax.all_to_all(copies, 'red', split_axis=0, concat_axis=0, tiled=True)  15.3 us
    all_to_all x1, starting transfers between devices, body(): lax.all_to_all(outgoing, 'col', split_axis=0, concat_axis=0, tiled=True)  8.99 us
    all_to_all x1, waiting for transfers between devices, body(): lax.all_to_all(ask.reshape(n_col, CAP), 'col', split_axis=0, concat_axis=...  7.28 us
    unnamed x6, local copies, waits for them, and re-layouts  3.71 us
  transfers between devices with their start and end apart: 2, of which 2 were waited for; matrix products, arithmetic and copies ran while one was open for 1% of the time, Pallas kernels for 0%

profile of v3, /device:TPU:114, one launch (start us, length us, event | category | flops | bytes accessed | tf_op | source)
XLA Modules:
  0.0 133.3 jit_solution(11194197291842248348)
XLA Ops:
  0.7 0.7 fusion.3
  1.3 0.2 convert_reduce_fusion
  1.5 0.1 select_reduce_fusion
  1.6 0.8 all_to_all.15
  2.4 22.4 %all-to-all-start = ((s32[64,1,2]{2,1,0:T(1,128)}), s32[64,1,2]{2,1,0:T(1,128)S(1)}, u32[]{:S(2)}, u32[]{:S(2)}) async-start(s32[64,1,2]{2,1,0:T(1,128)} %bitcast.4), calls=%async_computation | async-start | bytes 65536 | tf_op jit(solution)/shard_map/all_to_all | solution.py:107
  24.8 1.1 copy.13
  25.9 7.3 %all-to-all-done = s32[64,1,2]{2,1,0:T(1,128)S(1)} async-done(((s32[64,1,2]{2,1,0:T(1,128)}), s32[64,1,2]{2,1,0:T(1,128)S(1)}, u32[]{:S(2)}, u32[]{:S(2)}) %all-to-all-start) | async-done | bytes 544 | tf_op jit(solution)/shard_map/all_to_all | solution.py:107
  33.2 0.1 maximum_reduce_fusion
  33.3 0.1 reshape.143
  33.4 2.1 %gather_fusion = bf16[128,64,128]{2,1,0:T(8,128)(2,1)} fusion(bf16[16,64,128]{2,1,0:T(8,128)(2,1)S(1)} %bitcast.32, s32[1024]{0:T(1024)S(1)} %pad_clamp_fusion), kind=kCustom, calls=%fused_computation | custom fusion | bytes 4194816 | tf_op jit(solution)/shard_map/gather | solution.py:110
  35.5 0.0 copy-start.1
  35.5 9.0 %all-to-all-start.1 = ((bf16[64,2,64,128]{3,2,1,0:T(8,128)(2,1)}), bf16[64,2,64,128]{3,2,1,0:T(8,128)(2,1)}, u32[]{:S(2)}, u32[]{:S(2)}) async-start(bf16[64,2,64,128]{3,2,1,0:T(8,128)(2,1)} %bitcast.5), calls=%async_computation.1 | async-start | bytes 4194304 | tf_op jit(solution)/shard_map/all_to_all | solution.py:111
  44.5 0.0 copy-done.1
  44.6 0.1 copy.15
  44.7 0.1 broadcast_in_dim.18
  44.8 0.1 convert_element_type.19.keep
  44.9 0.0 copy-start
  44.9 1.9 %copy-done = bf16[1,1,64,24576]{3,2,1,0:T(8,128)(2,1)S(1)} copy-done((bf16[1,1,64,24576]{3,2,1,0:T(8,128)(2,1)S(1)}, bf16[1,1,64,24576]{3,2,1,0:T(8,128)(2,1)}, u32[]{:S(2)}) %copy-start) | copy-done | bytes 3145752
  46.8 0.6 shard_map.55.weights
  47.4 49.0 %all-to-all-done.1 = bf16[64,2,64,128]{3,2,1,0:T(8,128)(2,1)} async-done(((bf16[64,2,64,128]{3,2,1,0:T(8,128)(2,1)}), bf16[64,2,64,128]{3,2,1,0:T(8,128)(2,1)}, u32[]{:S(2)}, u32[]{:S(2)}) %all-to-all-start.1) | async-done | bytes 2097184 | tf_op jit(solution)/shard_map/all_to_all | solution.py:111
  96.4 2.2 %shard_map.56 = f32[128,512]{1,0:T(8,128)S(1)} custom-call(s32[48]{0:T(128)S(1)} %get-tuple-element.5.place, bf16[128,64,128]{2,1,0:T(8,128)(2,1)} %bitcast.6.blocks, bf16[3072,512]{1,0:T(8,128)(2,1)S(1)} %shard_map.55.weights), custom_call_target="tpu_custom_call" | custom-call | flops 402653184 | bytes 5242880 | tf_op jit(solution)/shard_map/pallas_call | solution.py:76
  98.7 18.6 %all_to_all.24 = f32[16,8,512]{2,1,0:T(8,128)S(1)} all-to-all(f32[16,8,512]{2,1,0:T(8,128)S(1)} %bitcast.31), channel_id=1, replica_groups=mesh['col'=64,'red'=16] {'red'}, dimensions={0} | all-to-all | bytes 524288 | tf_op jit(solution)/shard_map/all_to_all | solution.py:120
  117.3 15.3 %all_to_all.25 = f32[16,8,512]{2,1,0:T(8,128)S(1)} all-to-all(f32[16,8,512]{2,1,0:T(8,128)S(1)} %broadcast_in_dim.19), channel_id=1, replica_groups=mesh['col'=64,'red'=16] {'red'}, dimensions={0} | all-to-all | bytes 524288 | tf_op jit(solution)/shard_map/all_to_all | solution.py:123
  132.6 0.7 copy.18
  (6 shorter events, 0.1 us)
Async XLA Ops:
  2.4 30.8 %all-to-all-start = ((s32[64,1,2]{2,1,0:T(1,128)}), s32[64,1,2]{2,1,0:T(1,128)S(1)}, u32[]{:S(2)}, u32[]{:S(2)}) async-start(s32[64,1,2]{2,1,0:T(1,128)} %bitcast.4), calls=%async_computation | async-start | bytes 65536 | tf_op jit(solution)/shard_map/all_to_all | solution.py:107
  35.5 9.0 %copy-start.1 = (s32[1,1,48,8]{2,3,1,0:T(8,128)S(1)}, s32[1,1,48,8]{2,3,1,0:T(8,128)}, u32[]{:S(2)}) copy-start(s32[1,1,48,8]{2,3,1,0:T(8,128)} %param.8) | copy-start | bytes 4612
  35.5 60.9 %all-to-all-start.1 = ((bf16[64,2,64,128]{3,2,1,0:T(8,128)(2,1)}), bf16[64,2,64,128]{3,2,1,0:T(8,128)(2,1)}, u32[]{:S(2)}, u32[]{:S(2)}) async-start(bf16[64,2,64,128]{3,2,1,0:T(8,128)(2,1)} %bitcast.5), calls=%async_computation.1 | async-start | bytes 4194304 | tf_op jit(solution)/shard_map/all_to_all | solution.py:111
  44.9 1.9 %copy-start = (bf16[1,1,64,24576]{3,2,1,0:T(8,128)(2,1)S(1)}, bf16[1,1,64,24576]{3,2,1,0:T(8,128)(2,1)}, u32[]{:S(2)}) copy-start(bf16[1,1,64,24576]{3,2,1,0:T(8,128)(2,1)} %param.6) | copy-start | bytes 9437188

commit v4 on v3

--- a/solution.py
+++ b/solution.py
@@ -3,11 +3,17 @@
 from jax import lax
 from jax.experimental import pallas as pl
 from jax.experimental.pallas import tpu as pltpu
+from jax.sharding import Mesh
 from jax.sharding import PartitionSpec as P
 
 BLOCK = 64
 CAP = 2
 GROUP = 4
+AXES = ("y_hi1", "y_hi0", "z", "core", "y_lo", "x")
+SIZES = (2, 2, 8, 2, 2, 8)
+COL = AXES[:4]
+RED = AXES[4:]
+SERVERS = ("y_hi0", "z")
 
 
 def peer_rank(owners):
@@ -89,6 +95,29 @@
     )(place, blocks, weights)
 
 
+def pick_kernel(asked, *refs):
+    *sources, out = refs
+    each = len(sources) * CAP
+    for slot in range(out.shape[0]):
+        out[slot] = sources[slot % each // CAP][jnp.maximum(asked[slot] - 1, 0)]
+
+
+def pick(asked, sources):
+    slots = asked.shape[0]
+    shape = (slots,) + sources[0].shape[1:]
+    return pl.pallas_call(
+        pick_kernel,
+        out_shape=jax.ShapeDtypeStruct(shape, sources[0].dtype),
+        in_specs=[pl.BlockSpec(memory_space=pltpu.SMEM)]
+        + [pl.BlockSpec(memory_space=pltpu.VMEM)] * len(sources),
+        out_specs=pl.BlockSpec(memory_space=pltpu.VMEM),
+        compiler_params=pltpu.CompilerParams(vmem_limit_bytes=16 * 1024 * 1024),
+        cost_estimate=pl.CostEstimate(
+            flops=0, bytes_accessed=4 * slots * BLOCK * shape[-1], transcendentals=0
+        ),
+    )(asked, *sources)
+
+
 def body(amplitudes, block_tiles, block_rows, tile_mask, block_counts):
     row_ids = block_rows[0, 0]
     slots = row_ids.shape[0]
@@ -96,42 +125,65 @@
     cols_here = col_tiles * BLOCK
     rows = amplitudes.shape[0]
     blocks_here = amplitudes.shape[1] // BLOCK
-    n_col = lax.axis_size("col")
-    n_red = lax.axis_size("red")
+    n_servers = lax.axis_size(SERVERS)
+    n_red = lax.axis_size(RED)
     alive = jnp.arange(slots) < block_counts[0, 0]
 
+    own = amplitudes.T.reshape(blocks_here, BLOCK, rows)
+    n_y = lax.axis_size(AXES[:2])
+    n_core = lax.axis_size("core")
+    opposite = [(y, n_y - 1 - y) for y in range(n_y)]
+    across = [(c, n_core - 1 - c) for c in range(n_core)]
+    both = [(y * n_core + c, (n_y - 1 - y) * n_core + n_core - 1 - c) for y in range(n_y) for c in range(n_core)]
+    sources = [
+        own,
+        lax.ppermute(own, AXES[:2], opposite),
+        lax.ppermute(own, "core", across),
+        lax.ppermute(own, AXES[:2] + ("core",), both),
+    ]
+
     owners = row_ids // blocks_here
-    place = owners * CAP + peer_rank(owners)
-    here = (place[None, :] == jnp.arange(n_col * CAP)[:, None]) & alive[None, :]
+    owner_core = owners % n_core
+    owner_z = owners // n_core % lax.axis_size("z")
+    owner_y = owners // (n_core * lax.axis_size("z"))
+    flip = (owner_y // 2 != lax.axis_index("y_hi1")).astype(jnp.int32)
+    server = (owner_y % 2 ^ flip) * lax.axis_size("z") + owner_z
+    source = flip + 2 * (owner_core != lax.axis_index("core")).astype(jnp.int32)
+    place = (server * len(sources) + source) * CAP + peer_rank(owners)
+    n_places = n_servers * len(sources) * CAP
+
+    here = (place[None, :] == jnp.arange(n_places)[:, None]) & alive[None, :]
     ask = jnp.sum(jnp.where(here, (row_ids % blocks_here + 1)[None, :], 0), axis=-1)
-    asked = lax.all_to_all(ask.reshape(n_col, CAP), "col", split_axis=0, concat_axis=0, tiled=True)
+    ask = ask.reshape(n_servers, len(sources) * CAP)
+    asked = lax.all_to_all(ask, SERVERS, split_axis=0, concat_axis=0, tiled=True)
 
-    blocks = amplitudes.T.reshape(blocks_here, BLOCK, rows)
-    outgoing = blocks[jnp.maximum(asked - 1, 0)]
-    incoming = lax.all_to_all(outgoing, "col", split_axis=0, concat_axis=0, tiled=True)
+    outgoing = pick(asked.reshape(n_places), sources)
+    outgoing = outgoing.reshape(n_servers, len(sources) * CAP, BLOCK, rows)
+    incoming = lax.all_to_all(outgoing, SERVERS, split_axis=0, concat_axis=0, tiled=True)
 
     keep = jnp.repeat(tile_mask[0, 0] * alive[:, None], BLOCK, axis=1).astype(jnp.bfloat16)
     weights = stack(block_tiles[0, 0], keep)
     partial_value = contract(
-        jnp.clip(place, 0, n_col * CAP - 1), incoming.reshape(n_col * CAP, BLOCK, rows), weights
+        jnp.clip(place, 0, n_places - 1), incoming.reshape(n_places, BLOCK, rows), weights
     )
 
     slices = partial_value.reshape(n_red, rows // n_red, cols_here)
-    gathered = lax.all_to_all(slices, "red", split_axis=0, concat_axis=0, tiled=True)
+    gathered = lax.all_to_all(slices, RED, split_axis=0, concat_axis=0, tiled=True)
     mine = jnp.sum(gathered, axis=0)
     copies = jnp.broadcast_to(mine[None], gathered.shape)
-    whole = lax.all_to_all(copies, "red", split_axis=0, concat_axis=0, tiled=True)
+    whole = lax.all_to_all(copies, RED, split_axis=0, concat_axis=0, tiled=True)
     return whole.reshape(rows, cols_here)
 
 
 def solution(mesh):
+    fine = Mesh(mesh.devices.reshape(SIZES), AXES)
     placed = (
-        P(None, ("red", "col")),
-        P("red", "col", None, None),
-        P("red", "col", None),
-        P("red", "col", None, None),
-        P("red", "col"),
+        P(None, RED + COL),
+        P(RED, COL, None, None),
+        P(RED, COL, None),
+        P(RED, COL, None, None),
+        P(RED, COL),
     )
     return jax.shard_map(
-        body, mesh=mesh, in_specs=placed, out_specs=P(None, "col"), check_vma=False
+        body, mesh=fine, in_specs=placed, out_specs=P(None, COL), check_vma=False
     )

time: 134 us -> 146 us (1.090)
  blocking collectives: 33.9 us -> 66.9 us
  starting transfers between devices: 31.3 us -> 19.1 us
  waiting for transfers between devices: 56.3 us -> 47.4 us
  local copies, waits for them, and re-layouts: 7.08 us -> 4.75 us
  Pallas kernels: 2.83 us -> 4.87 us
    all_to_all x2 -> x3, blocking collectives: 33.9 us -> 66.9 us  [the longest x1 27.2 us: body(): lax.all_to_all(slices, RED, split_axis=0, concat_axis=0, tiled=True)]
    all_to_all x2 -> x1, starting transfers between devices: 31.3 us -> 9.08 us  [body(): lax.all_to_all(outgoing, SERVERS, split_axis=0, concat_axis=0, tiled=True)]
    ppermute x0 -> x3, starting transfers between devices: none -> 9.98 us  [the longest x1 5.95 us: body(): lax.ppermute(own, AXES[:2], opposite)]
    all_to_all x2 -> x1, waiting for transfers between devices: 56.3 us -> 47.4 us  [body(): lax.all_to_all(outgoing, SERVERS, split_axis=0, concat_axis=0, tiled=True)]
    gather x1 -> x0, local copies, waits for them, and re-layouts: 2.11 us -> none  [body(): outgoing = blocks[jnp.maximum(asked - 1, 0)]]
    pallas_call x0 -> x1, Pallas kernels: none -> 2.04 us  [pick(): pl.pallas_call(pick_kernel, out_shape=jax.ShapeDtypeStruct(shape, sources...]
    unnamed x6 -> x5, local copies, waits for them, and re-layouts: 3.71 us -> 2.59 us
  transfers between devices with their start and end apart: 2 -> 4, of which waited for: 2 -> 1; matrix products, arithmetic and copies ran while one was open for 1% -> 2% of each run, Pallas kernels for 0% -> 0%
where the time goes in v4:
time: 146 us; the launch traced here: 145 us
  blocking collectives  66.9 us (46%)
  waiting for transfers between devices  47.4 us (32%)
  starting transfers between devices  19.1 us (13%)
  Pallas kernels  4.87 us (3%)
  local copies, waits for them, and re-layouts  4.75 us (3%)
  other arithmetic  1.68 us (1%)
    all_to_all x1, waiting for transfers between devices, body(): lax.all_to_all(outgoing, SERVERS, split_axis=0, concat_axis=0, tiled=True)  47.4 us
    all_to_all x1, blocking collectives, body(): lax.all_to_all(slices, RED, split_axis=0, concat_axis=0, tiled=True)  27.2 us
    all_to_all x1, blocking collectives, body(): lax.all_to_all(ask, SERVERS, split_axis=0, concat_axis=0, tiled=True)  26 us
    all_to_all x1, blocking collectives, body(): whole = lax.all_to_all(copies, RED, split_axis=0, concat_axis=0, tiled=True)  13.7 us
    all_to_all x1, starting transfers between devices, body(): lax.all_to_all(outgoing, SERVERS, split_axis=0, concat_axis=0, tiled=True)  9.08 us
    ppermute x1, starting transfers between devices, body(): lax.ppermute(own, AXES[:2], opposite)  5.95 us
  transfers between devices with their start and end apart: 4, of which 1 were waited for; matrix products, arithmetic and copies ran while one was open for 2% of the time, Pallas kernels for 0%

profile of v4, /device:TPU:114, one launch (start us, length us, event | category | flops | bytes accessed | tf_op | source)
XLA Modules:
  0.0 145.5 jit_solution(11612955495199957478)
XLA Ops:
  0.0 1.1 copy.14
  1.1 1.9 %collective-permute-start.2 = (bf16[16,64,128]{2,1,0:T(8,128)(2,1)S(1)}, bf16[16,64,128]{2,1,0:T(8,128)(2,1)S(1)}, u32[]{:S(2)}, u32[]{:S(2)}) collective-permute-start(bf16[16,64,128]{2,1,0:T(8,128)(2,1)S(1)} %bitcast.31), channel_id=1, source_target_pairs={{0,784},{16,768},{256,528},{272,512},{512,272},{528,256},{768,16},... | collective-permute-start | bytes 786440 | tf_op jit(solution)/shard_map/ppermute | solution.py:142
  3.1 2.1 %collective-permute-start.1 = (bf16[16,64,128]{2,1,0:T(8,128)(2,1)S(1)}, bf16[16,64,128]{2,1,0:T(8,128)(2,1)S(1)}, u32[]{:S(2)}, u32[]{:S(2)}) collective-permute-start(bf16[16,64,128]{2,1,0:T(8,128)(2,1)S(1)} %bitcast.32), channel_id=1, source_target_pairs={{0,16},{16,0},{1,17},{17,1},{2,18},{18,2},{3,19},{19,3},{4,20},{20... | collective-permute-start | bytes 786440 | tf_op jit(solution)/shard_map/ppermute | solution.py:141
  5.2 5.9 %collective-permute-start = (bf16[16,64,128]{2,1,0:T(8,128)(2,1)S(1)}, bf16[16,64,128]{2,1,0:T(8,128)(2,1)S(1)}, u32[]{:S(2)}, u32[]{:S(2)}) collective-permute-start(bf16[16,64,128]{2,1,0:T(8,128)(2,1)S(1)} %bitcast.33), channel_id=1, source_target_pairs={{0,768},{256,512},{512,256},{768,0},{1,769},{257,513},{513,257},{7... | collective-permute-start | bytes 786440 | tf_op jit(solution)/shard_map/ppermute | solution.py:140
  11.1 0.7 fusion.7
  11.8 0.2 convert_reduce_fusion
  12.7 0.1 select_reduce_fusion
  12.8 0.1 all_to_all.15
  12.9 26.0 %all_to_all.24 = s32[16,1,8]{2,1,0:T(1,128)S(1)} all-to-all(s32[16,1,8]{2,1,0:T(1,128)S(1)} %bitcast.37), channel_id=1, replica_groups=mesh['y_hi1'=2,'y_hi0'=2,'z'=8,'core'=2,'y_lo'=2,'x'=8] {'y_hi0','z'}, dimensions={0} | all-to-all | bytes 1024 | tf_op jit(solution)/shard_map/all_to_all | solution.py:158
  38.9 0.5 broadcast.305
  39.4 0.7 reduce.3
  40.1 0.1 reshape.210.asked
  40.2 0.0 copy-start.1
  40.2 0.0 collective-permute-done.2.refs_3_
  40.2 0.0 collective-permute-done.1.refs_2_
  40.2 0.0 collective-permute-done.refs_1_
  40.2 2.0 %shard_map.55 = bf16[128,64,128]{2,1,0:T(8,128)(2,1)} custom-call(s32[128]{0:T(128)S(1)} %reshape.210.asked, bf16[16,64,128]{2,1,0:T(8,128)(2,1)S(1)} %bitcast.34, bf16[16,64,128]{2,1,0:T(8,128)(2,1)S(1)} %collective-permute-done.refs_1_, bf16[16,64,128]{2,1,0:T(8,128)(2,1)S(1)} %collective-permute-done.1.refs_2_, ...), custom_call_target="tpu_custom_call" | custom-call | bytes 4194304 | tf_op jit(solution)/shard_map/pallas_call | solution.py:108
  42.2 9.1 %all-to-all-start.1 = ((bf16[16,8,64,128]{3,2,1,0:T(8,128)(2,1)}), bf16[16,8,64,128]{3,2,1,0:T(8,128)(2,1)}, u32[]{:S(2)}, u32[]{:S(2)}) async-start(bf16[16,8,64,128]{3,2,1,0:T(8,128)(2,1)} %bitcast.5), calls=%async_computation.1 | async-start | bytes 4194304 | tf_op jit(solution)/shard_map/all_to_all | solution.py:162
  51.3 0.0 copy-done.1
  51.3 0.1 copy.15
  51.4 0.1 broadcast_in_dim.18
  51.6 0.1 convert_element_type.28.keep
  51.7 0.0 copy-start
  51.7 1.9 %copy-done = bf16[1,1,64,24576]{3,2,1,0:T(8,128)(2,1)S(1)} copy-done((bf16[1,1,64,24576]{3,2,1,0:T(8,128)(2,1)S(1)}, bf16[1,1,64,24576]{3,2,1,0:T(8,128)(2,1)}, u32[]{:S(2)}) %copy-start) | copy-done | bytes 3145752
  53.6 0.6 shard_map.56.weights
  54.2 47.4 %all-to-all-done.1 = bf16[16,8,64,128]{3,2,1,0:T(8,128)(2,1)} async-done(((bf16[16,8,64,128]{3,2,1,0:T(8,128)(2,1)}), bf16[16,8,64,128]{3,2,1,0:T(8,128)(2,1)}, u32[]{:S(2)}, u32[]{:S(2)}) %all-to-all-start.1) | async-done | bytes 2097184 | tf_op jit(solution)/shard_map/all_to_all | solution.py:162
  101.6 2.2 %shard_map.57 = f32[128,512]{1,0:T(8,128)S(1)} custom-call(s32[48]{0:T(128)S(1)} %get-tuple-element.5.place, bf16[128,64,128]{2,1,0:T(8,128)(2,1)} %bitcast.6.blocks, bf16[3072,512]{1,0:T(8,128)(2,1)S(1)} %shard_map.56.weights), custom_call_target="tpu_custom_call" | custom-call | flops 402653184 | bytes 5242880 | tf_op jit(solution)/shard_map/pallas_call | solution.py:82
  103.9 27.2 %all_to_all.25 = f32[16,8,512]{2,1,0:T(8,128)S(1)} all-to-all(f32[16,8,512]{2,1,0:T(8,128)S(1)} %bitcast.30), channel_id=1, replica_groups=mesh['y_hi1'=2,'y_hi0'=2,'z'=8,'core'=2,'y_lo'=2,'x'=8] {'y_lo','x'}, dimensions={0} | all-to-all | bytes 524288 | tf_op jit(solution)/shard_map/all_to_all | solution.py:171
  131.1 13.7 %all_to_all.26 = f32[16,8,512]{2,1,0:T(8,128)S(1)} all-to-all(f32[16,8,512]{2,1,0:T(8,128)S(1)} %broadcast_in_dim.19), channel_id=1, replica_groups=mesh['y_hi1'=2,'y_hi0'=2,'z'=8,'core'=2,'y_lo'=2,'x'=8] {'y_lo','x'}, dimensions={0} | all-to-all | bytes 524288 | tf_op jit(solution)/shard_map/all_to_all | solution.py:174
  144.8 0.7 copy.18
  (5 shorter events, 0.1 us)
Async XLA Ops:
  1.1 39.1 %collective-permute-start.2 = (bf16[16,64,128]{2,1,0:T(8,128)(2,1)S(1)}, bf16[16,64,128]{2,1,0:T(8,128)(2,1)S(1)}, u32[]{:S(2)}, u32[]{:S(2)}) collective-permute-start(bf16[16,64,128]{2,1,0:T(8,128)(2,1)S(1)} %bitcast.31), channel_id=1, source_target_pairs={{0,784},{16,768},{256,528},{272,512},{512,272},{528,256},{768,16},... | collective-permute-start | bytes 786440 | tf_op jit(solution)/shard_map/ppermute | solution.py:142
  3.1 37.1 %collective-permute-start.1 = (bf16[16,64,128]{2,1,0:T(8,128)(2,1)S(1)}, bf16[16,64,128]{2,1,0:T(8,128)(2,1)S(1)}, u32[]{:S(2)}, u32[]{:S(2)}) collective-permute-start(bf16[16,64,128]{2,1,0:T(8,128)(2,1)S(1)} %bitcast.32), channel_id=1, source_target_pairs={{0,16},{16,0},{1,17},{17,1},{2,18},{18,2},{3,19},{19,3},{4,20},{20... | collective-permute-start | bytes 786440 | tf_op jit(solution)/shard_map/ppermute | solution.py:141
  5.2 35.0 %collective-permute-start = (bf16[16,64,128]{2,1,0:T(8,128)(2,1)S(1)}, bf16[16,64,128]{2,1,0:T(8,128)(2,1)S(1)}, u32[]{:S(2)}, u32[]{:S(2)}) collective-permute-start(bf16[16,64,128]{2,1,0:T(8,128)(2,1)S(1)} %bitcast.33), channel_id=1, source_target_pairs={{0,768},{256,512},{512,256},{768,0},{1,769},{257,513},{513,257},{7... | collective-permute-start | bytes 786440 | tf_op jit(solution)/shard_map/ppermute | solution.py:140
  40.2 11.2 %copy-start.1 = (s32[1,1,48,8]{2,3,1,0:T(8,128)S(1)}, s32[1,1,48,8]{2,3,1,0:T(8,128)}, u32[]{:S(2)}) copy-start(s32[1,1,48,8]{2,3,1,0:T(8,128)} %param.8) | copy-start | bytes 4612
  42.2 59.4 %all-to-all-start.1 = ((bf16[16,8,64,128]{3,2,1,0:T(8,128)(2,1)}), bf16[16,8,64,128]{3,2,1,0:T(8,128)(2,1)}, u32[]{:S(2)}, u32[]{:S(2)}) async-start(bf16[16,8,64,128]{3,2,1,0:T(8,128)(2,1)} %bitcast.5), calls=%async_computation.1 | async-start | bytes 4194304 | tf_op jit(solution)/shard_map/all_to_all | solution.py:162
  51.7 1.9 %copy-start = (bf16[1,1,64,24576]{3,2,1,0:T(8,128)(2,1)S(1)}, bf16[1,1,64,24576]{3,2,1,0:T(8,128)(2,1)}, u32[]{:S(2)}) copy-start(bf16[1,1,64,24576]{3,2,1,0:T(8,128)(2,1)} %param.6) | copy-start | bytes 9437188

commit v5 on v3

v5 whole, which is shorter than its diff:
```python
import jax
import jax.numpy as jnp
from jax import lax
from jax.experimental import pallas as pl
from jax.experimental.pallas import tpu as pltpu
from jax.sharding import PartitionSpec as P

BLOCK = 64
HALF = 32
CAP = 2
GROUP = 4
NY = 4
NZ = 8
NCORE = 2
STEPS = 4
LIMIT = pltpu.CompilerParams(vmem_limit_bytes=16 * 1024 * 1024)


def col_index(y, z, core):
    return (y % NY * NZ + z % NZ) * NCORE + core


def server_groups():
    along_z = [[col_index(y, z, 0) for z in range(NZ)] for y in range(NY)]
    along_y = [
        [col_index(y, 2 * pair + odd, 1) for y in range(NY) for odd in range(2)]
        for pair in range(NZ // 2)
    ]
    return along_z + along_y


def step_pairs(step):
    pairs = []
    for y in range(NY):
        for z in range(NZ):
            pairs.append((col_index(y + step, z, 0), col_index(y, z, 0)))
            pairs.append((col_index(y, z + 2 * step, 1), col_index(y, z, 1)))
    return pairs


def swap_pairs():
    return [(i, i ^ 1) for i in range(NY * NZ * NCORE)]


def peer_rank(owners):
    width = owners.shape[-1]
    same = owners[..., :, None] == owners[..., None, :]
    earlier = jnp.arange(width)[None, :] < jnp.arange(width)[:, None]
    return jnp.sum((same & earlier).astype(jnp.int32), axis=-1)


def stack_kernel(mine, tiles, keep, out, buf, sem):
    slots, cols = keep.shape
    chunks, _, width = buf.shape
    each = slots // chunks

    def copy(i):
        return pltpu.make_async_copy(tiles.at[:, pl.ds(i * width, width)], buf.at[i], sem.at[i])

    for i in range(chunks):
        copy(i).start()
    for i in range(chunks):
        copy(i).wait()
        for part in range(2):
            half = mine[0] if part == 0 else 1 - mine[0]
            rows = pl.ds(pl.multiple_of(half * HALF, HALF), HALF)
            for j in range(each):
                s = i * each + j
                out[part, pl.ds(s * HALF, HALF), :] = (
                    buf[i, rows, pl.ds(j * cols, cols)] * keep[pl.ds(s, 1), :]
                )


def stack(mine, tiles, keep):
    slots, cols = keep.shape
    chunks = slots // GROUP
    return pl.pallas_call(
        stack_kernel,
        out_shape=jax.ShapeDtypeStruct((2, slots * HALF, cols), tiles.dtype),
        in_specs=[
            pl.BlockSpec(memory_space=pltpu.SMEM),
            pl.BlockSpec(memory_space=pl.ANY),
            pl.BlockSpec(memory_space=pltpu.VMEM),
        ],
        out_specs=pl.BlockSpec(memory_space=pltpu.VMEM),
        scratch_shapes=[
            pltpu.VMEM((chunks, BLOCK, GROUP * cols), tiles.dtype),
            pltpu.SemaphoreType.DMA((chunks,)),
        ],
        compiler_params=LIMIT,
        cost_estimate=pl.CostEstimate(
            flops=slots * BLOCK * cols, bytes_accessed=4 * slots * BLOCK * cols, transcendentals=0
        ),
    )(mine, tiles, keep)


def pick_kernel(asked, *refs):
    *sources, out = refs
    per_peer = STEPS * NCORE * CAP
    blocks_here = sources[0].shape[0] // NCORE
    for slot in range(out.shape[0]):
        step = slot % per_peer // (NCORE * CAP)
        core = slot // CAP % NCORE
        out[slot] = sources[step][core * blocks_here + jnp.maximum(asked[slot] - 1, 0)]


def pick(asked, sources):
    slots = asked.shape[0]
    shape = (slots,) + sources[0].shape[1:]
    return pl.pallas_call(
        pick_kernel,
        out_shape=jax.ShapeDtypeStruct(shape, sources[0].dtype),
        in_specs=[pl.BlockSpec(memory_space=pltpu.SMEM)]
        + [pl.BlockSpec(memory_space=pltpu.VMEM)] * len(sources),
        out_specs=pl.BlockSpec(memory_space=pltpu.VMEM),
        compiler_params=LIMIT,
        cost_estimate=pl.CostEstimate(
            flops=0, bytes_accessed=4 * slots * HALF * shape[-1], transcendentals=0
        ),
    )(asked, *sources)


def select_kernel(place, blocks, out):
    for s in range(out.shape[0]):
        out[s] = blocks[place[s]]


def select(place, blocks):
    slots = place.shape[0]
    shape = (slots,) + blocks.shape[1:]
    return pl.pallas_call(
        select_kernel,
        out_shape=jax.ShapeDtypeStruct(shape, blocks.dtype),
        in_specs=[
            pl.BlockSpec(memory_space=pltpu.SMEM),
            pl.BlockSpec(memory_space=pltpu.VMEM),
        ],
        out_specs=pl.BlockSpec(memory_space=pltpu.VMEM),
        compiler_params=LIMIT,
        cost_estimate=pl.CostEstimate(
            flops=0, bytes_accessed=2 * blocks.size, transcendentals=0
        ),
    )(place, blocks)


def contract_kernel(place, blocks, weights, *refs):
    *start, out = refs
    total = start[0][...] if start else jnp.zeros(out.shape, jnp.float32)
    half = 1 if start else 0
    each = 2 * GROUP
    depth = each * HALF
    for g in range(weights.shape[1] // depth):
        lhs = jnp.concatenate([blocks[place[g * each + s]] for s in range(each)], axis=0)
        total += lax.dot_general(
            lhs,
            weights[half, pl.ds(g * depth, depth), :],
            (((0,), (0,)), ((), ())),
            preferred_element_type=jnp.float32,
        )
    out[...] = total


def contract(place, blocks, weights, *start):
    _, depth, cols = weights.shape
    rows = blocks.shape[-1]
    return pl.pallas_call(
        contract_kernel,
        out_shape=jax.ShapeDtypeStruct((rows, cols), jnp.float32),
        in_specs=[pl.BlockSpec(memory_space=pltpu.SMEM)]
        + [pl.BlockSpec(memory_space=pltpu.VMEM)] * (2 + len(start)),
        out_specs=pl.BlockSpec(memory_space=pltpu.VMEM),
        compiler_params=LIMIT,
        cost_estimate=pl.CostEstimate(
            flops=2 * depth * rows * cols, bytes_accessed=5 * 1024 * 1024, transcendentals=0
        ),
    )(place, blocks, weights, *start)


def body(amplitudes, block_tiles, block_rows, tile_mask, block_counts):
    row_ids = block_rows[0, 0]
    slots = row_ids.shape[0]
    cols_here = tile_mask.shape[-1] * BLOCK
    rows = amplitudes.shape[0]
    blocks_here = amplitudes.shape[1] // BLOCK
    n_red = lax.axis_size("red")
    groups = server_groups()
    members = len(groups[0])
    alive = jnp.arange(slots) < block_counts[0, 0]
    here = lax.axis_index("col")
    core = here & 1
    z = here >> 1 & NZ - 1
    y = here >> 4

    halves = amplitudes.T.reshape(blocks_here, NCORE, HALF, rows)
    given = lax.ppermute(lax.dynamic_index_in_dim(halves, 1 - core, 1, False), "col", swap_pairs())
    chip = jnp.concatenate([lax.dynamic_index_in_dim(halves, core, 1, False), given])
    sources = [chip] + [lax.ppermute(chip, "col", step_pairs(s)) for s in range(1, STEPS)]

    listed = jnp.where(alive, row_ids, -1)
    other = lax.ppermute(listed, "col", swap_pairs())
    lists = jnp.where(core == 0, jnp.stack([listed, other]), jnp.stack([other, listed]))
    owners = lists >> 4
    owner_z = owners >> 1 & NZ - 1
    owner_y = owners >> 4
    server = jnp.where(core == 0, owner_z, owner_y * 2 + (owner_z & 1))
    step = jnp.where(core == 0, owner_y - y, (owner_z >> 1) - (z >> 1)) & STEPS - 1
    away = owners & 1 ^ core
    place = ((server * NCORE + jnp.arange(NCORE)[:, None]) * STEPS + step) * NCORE + away
    place = place * CAP + peer_rank(owners)
    n_places = members * NCORE * STEPS * NCORE * CAP

    flat = jnp.where(lists >= 0, place, -1).reshape(-1)
    within = ((lists & blocks_here - 1) + 1).reshape(-1)
    match = flat[None, :] == jnp.arange(n_places)[:, None]
    ask = jnp.sum(jnp.where(match, within[None, :], 0), axis=-1)
    asked = lax.all_to_all(
        ask.reshape(members, -1), "col", split_axis=0, concat_axis=0, tiled=True, axis_index_groups=groups
    )

    keep = jnp.repeat(tile_mask[0, 0] * alive[:, None], BLOCK, axis=1).astype(jnp.bfloat16)
    weights = stack(core.reshape(1), block_tiles[0, 0], keep)
    asked, weights = lax.optimization_barrier((asked, weights))
    outgoing = pick(asked.reshape(n_places), sources)
    incoming = lax.all_to_all(
        outgoing.reshape(members, -1, HALF, rows),
        "col",
        split_axis=0,
        concat_axis=0,
        tiled=True,
        axis_index_groups=groups,
    ).reshape(n_places, HALF, rows)

    place = jnp.clip(place, 0, n_places - 1)
    place_own = jnp.where(core == 0, place[0], place[1])
    place_other = jnp.where(core == 0, place[1], place[0])
    received = lax.ppermute(select(place_other, incoming), "col", swap_pairs())
    first = contract(place_own, incoming, weights)
    partial_value = contract(jnp.arange(slots, dtype=jnp.int32), received, weights, first)

    slices = partial_value.reshape(n_red, rows // n_red, cols_here)
    gathered = lax.all_to_all(slices, "red", split_axis=0, concat_axis=0, tiled=True)
    mine = jnp.sum(gathered, axis=0)
    copies = jnp.broadcast_to(mine[None], gathered.shape)
    whole = lax.all_to_all(copies, "red", split_axis=0, concat_axis=0, tiled=True)
    return whole.reshape(rows, cols_here)


def solution(mesh):
    placed = (
        P(None, ("red", "col")),
        P("red", "col", None, None),
        P("red", "col", None),
        P("red", "col", None, None),
        P("red", "col"),
    )
    return jax.shard_map(
        body, mesh=mesh, in_specs=placed, out_specs=P(None, "col"), check_vma=False
    )
```

time: 134 us -> 134 us (level)
  the two profiles are of different devices: /device:TPU:114 before, /device:TPU:82 now
where the time goes in v5:
time: 134 us
  waiting for transfers between devices  45.4 us (34%)
  starting transfers between devices  37.7 us (28%)
  blocking collectives  33 us (25%)
  local copies, waits for them, and re-layouts  6.82 us (5%)
  Pallas kernels  6.74 us (5%)
  other arithmetic  3.08 us (2%)
    all_to_all x1, waiting for transfers between devices, body(): lax.all_to_all(outgoing.reshape(members, -1, HALF, rows), 'col', split_ax...  41.4 us
    all_to_all x1, blocking collectives, body(): lax.all_to_all(slices, 'red', split_axis=0, concat_axis=0, tiled=True)  18.7 us
    all_to_all x1, starting transfers between devices, body(): lax.all_to_all(ask.reshape(members, -1), 'col', split_axis=0, concat_axis...  16.7 us
    all_to_all x1, blocking collectives, body(): lax.all_to_all(copies, 'red', split_axis=0, concat_axis=0, tiled=True)  14.2 us
    ppermute x3, starting transfers between devices, body(): lax.ppermute(chip, 'col', step_pairs(s))  10.4 us
    unnamed x6, local copies, waits for them, and re-layouts  5.01 us
    all_to_all x1, starting transfers between devices, body(): lax.all_to_all(outgoing.reshape(members, -1, HALF, rows), 'col', split_ax...  4.34 us
    all_to_all x1, waiting for transfers between devices, body(): lax.all_to_all(ask.reshape(members, -1), 'col', split_axis=0, concat_axis...  4.03 us
  transfers between devices with their start and end apart: 8, of which 2 were waited for; matrix products, arithmetic and copies ran while one was open for 3% of the time, Pallas kernels for 2%

profile of v5, /device:TPU:82, one launch (start us, length us, event | category | flops | bytes accessed | tf_op | source)
XLA Modules:
  0.0 133.6 jit_solution(5449577548233602919)
XLA Ops:
  0.7 0.7 compare_select_fusion.2
  1.3 1.9 %collective-permute-start = (s32[48]{0:T(128)S(1)}, s32[48]{0:T(128)S(1)}, u32[]{:S(2)}, u32[]{:S(2)}) collective-permute-start(s32[48]{0:T(128)S(1)} %compare_select_fusion.2), channel_id=1, source_target_pairs={{0,16},{16,0},{32,48},{48,32},{64,80},{80,64},{96,112},{112,96},{1... | collective-permute-start | bytes 584 | tf_op jit(solution)/shard_map/ppermute | solution.py:200
  3.2 1.1 copy.12
  4.4 2.4 %collective-permute-start.1 = (bf16[16,32,128]{2,1,0:T(8,128)(2,1)S(1)}, bf16[16,32,128]{2,1,0:T(8,128)(2,1)S(1)}, u32[]{:S(2)}, u32[]{:S(2)}) collective-permute-start(bf16[16,32,128]{2,1,0:T(8,128)(2,1)S(1)} %get-tuple-element.12), channel_id=1, source_target_pairs={{0,16},{16,0},{32,48},{48,32},{64,80},{80,64},{96,112},{112,96},{1... | collective-permute-start | bytes 393224 | tf_op jit(solution)/shard_map/ppermute | solution.py:195
  6.8 0.7 compare_select_fusion.1
  7.5 0.7 fusion.10
  8.4 0.1 ge.12
  8.5 0.2 convert_reduce_fusion
  9.1 2.9 %collective-permute-start.4 = (bf16[32,32,128]{2,1,0:T(8,128)(2,1)S(1)}, bf16[32,32,128]{2,1,0:T(8,128)(2,1)}, u32[]{:S(2)}, u32[]{:S(2)}) collective-permute-start(bf16[32,32,128]{2,1,0:T(8,128)(2,1)S(1)} %pad_maximum_fusion.refs_0_), channel_id=1, source_target_pairs={{768,0},{208,16},{800,32},{240,48},{832,64},{16,80},{864,96},{48,1... | collective-permute-start | bytes 786440 | tf_op jit(solution)/shard_map/ppermute | solution.py:197
  12.1 4.3 %collective-permute-start.3 = (bf16[32,32,128]{2,1,0:T(8,128)(2,1)S(1)}, bf16[32,32,128]{2,1,0:T(8,128)(2,1)}, u32[]{:S(2)}, u32[]{:S(2)}) collective-permute-start(bf16[32,32,128]{2,1,0:T(8,128)(2,1)S(1)} %pad_maximum_fusion.refs_0_), channel_id=1, source_target_pairs={{512,0},{144,16},{544,32},{176,48},{576,64},{208,80},{608,96},{240... | collective-permute-start | bytes 786440 | tf_op jit(solution)/shard_map/ppermute | solution.py:197
  16.3 3.2 %collective-permute-start.2 = (bf16[32,32,128]{2,1,0:T(8,128)(2,1)S(1)}, bf16[32,32,128]{2,1,0:T(8,128)(2,1)}, u32[]{:S(2)}, u32[]{:S(2)}) collective-permute-start(bf16[32,32,128]{2,1,0:T(8,128)(2,1)S(1)} %pad_maximum_fusion.refs_0_), channel_id=1, source_target_pairs={{256,0},{80,16},{288,32},{112,48},{320,64},{144,80},{352,96},{176,... | collective-permute-start | bytes 786440 | tf_op jit(solution)/shard_map/ppermute | solution.py:197
  19.6 0.1 select_reduce_fusion
  19.7 0.7 all_to_all.17
  20.4 16.7 %all-to-all-start = ((s32[8,1,32]{2,1,0:T(1,128)}), s32[8,1,32]{2,1,0:T(1,128)S(1)}, u32[]{:S(2)}, u32[]{:S(2)}) async-start(s32[8,1,32]{2,1,0:T(1,128)} %all_to_all.17), calls=%async_computation | async-start | bytes 8192 | tf_op jit(solution)/shard_map/all_to_all | solution.py:216
  37.0 0.7 fusion
  37.7 0.1 copy.11
  37.8 0.1 broadcast_in_dim.47
  38.0 0.1 convert_element_type.19.keep
  38.1 1.9 %copy-done.1 = bf16[1,1,64,24576]{3,2,1,0:T(8,128)(2,1)S(1)} copy-done((bf16[1,1,64,24576]{3,2,1,0:T(8,128)(2,1)S(1)}, bf16[1,1,64,24576]{3,2,1,0:T(8,128)(2,1)}, u32[]{:S(2)}) %copy-start.1) | copy-done | bytes 3145752
  40.0 0.6 shard_map.55.weights
  40.6 4.0 %all-to-all-done = s32[8,1,32]{2,1,0:T(1,128)S(1)} async-done(((s32[8,1,32]{2,1,0:T(1,128)}), s32[8,1,32]{2,1,0:T(1,128)S(1)}, u32[]{:S(2)}, u32[]{:S(2)}) %all-to-all-start) | async-done | bytes 1056 | tf_op jit(solution)/shard_map/all_to_all | solution.py:216
  44.7 1.5 %shard_map.56 = bf16[256,32,128]{2,1,0:T(8,128)(2,1)S(1)} custom-call(s32[256]{0:T(256)S(1)} %reshape.211.asked, bf16[32,32,128]{2,1,0:T(8,128)(2,1)S(1)} %pad_maximum_fusion.refs_0_, bf16[32,32,128]{2,1,0:T(8,128)(2,1)} %collective-permute-done.2.refs_1_, bf16[32,32,128]{2,1,0:T(8,128)(2,1)} %collective-permute-done.3.refs_2_, ...), custom_call_target="tpu_custom_call" | custom-call | bytes 4194304 | tf_op jit(solution)/shard_map/pallas_call | solution.py:110
  46.3 1.3 copy-done
  47.6 4.3 %all-to-all-start.1 = ((bf16[8,32,32,128]{3,2,1,0:T(8,128)(2,1)}), bf16[8,32,32,128]{3,2,1,0:T(8,128)(2,1)}, u32[]{:S(2)}, u32[]{:S(2)}) async-start(bf16[8,32,32,128]{3,2,1,0:T(8,128)(2,1)} %bitcast.34), calls=%async_computation.1 | async-start | bytes 4194304 | tf_op jit(solution)/shard_map/all_to_all | solution.py:224
  52.0 41.4 %all-to-all-done.1 = bf16[8,32,32,128]{3,2,1,0:T(8,128)(2,1)} async-done(((bf16[8,32,32,128]{3,2,1,0:T(8,128)(2,1)}), bf16[8,32,32,128]{3,2,1,0:T(8,128)(2,1)}, u32[]{:S(2)}, u32[]{:S(2)}) %all-to-all-start.1) | async-done | bytes 2097184 | tf_op jit(solution)/shard_map/all_to_all | solution.py:224
  93.4 1.6 %shard_map.57 = bf16[48,32,128]{2,1,0:T(8,128)(2,1)S(1)} custom-call(s32[48]{0:T(128)S(1)} %get-tuple-element.14.place, bf16[256,32,128]{2,1,0:T(8,128)(2,1)} %bitcast.16.blocks), custom_call_target="tpu_custom_call" | custom-call | bytes 2097152 | tf_op jit(solution)/shard_map/pallas_call | solution.py:131
  95.0 1.9 %collective-permute-start.5 = (bf16[48,32,128]{2,1,0:T(8,128)(2,1)S(1)}, bf16[48,32,128]{2,1,0:T(8,128)(2,1)S(1)}, u32[]{:S(2)}, u32[]{:S(2)}) collective-permute-start(bf16[48,32,128]{2,1,0:T(8,128)(2,1)S(1)} %shard_map.57), channel_id=1, source_target_pairs={{0,16},{16,0},{32,48},{48,32},{64,80},{80,64},{96,112},{112,96},{1... | collective-permute-start | bytes 1179656 | tf_op jit(solution)/shard_map/ppermute | solution.py:236
  96.9 2.0 %shard_map.58.refs_0_ = f32[128,512]{1,0:T(8,128)S(1)} custom-call(s32[48]{0:T(128)S(1)} %get-tuple-element.13.place, bf16[256,32,128]{2,1,0:T(8,128)(2,1)} %bitcast.16.blocks, bf16[2,1536,512]{2,1,0:T(8,128)(2,1)S(1)} %shard_map.55.weights), custom_call_target="tpu_custom_call" | custom-call | flops 201326592 | bytes 5242880 | tf_op jit(solution)/shard_map/pallas_call | solution.py:166
  99.0 0.9 shard_map.59
  99.9 18.7 %all_to_all.27 = f32[16,8,512]{2,1,0:T(8,128)S(1)} all-to-all(f32[16,8,512]{2,1,0:T(8,128)S(1)} %bitcast.36), channel_id=1, replica_groups=mesh['col'=64,'red'=16] {'red'}, dimensions={0} | all-to-all | bytes 524288 | tf_op jit(solution)/shard_map/all_to_all | solution.py:241
  118.7 14.2 %all_to_all.28 = f32[16,8,512]{2,1,0:T(8,128)S(1)} all-to-all(f32[16,8,512]{2,1,0:T(8,128)S(1)} %broadcast_in_dim.48), channel_id=1, replica_groups=mesh['col'=64,'red'=16] {'red'}, dimensions={0} | all-to-all | bytes 524288 | tf_op jit(solution)/shard_map/all_to_all | solution.py:244
  132.9 0.7 copy.15
  (30 shorter events, 0.8 us)
Async XLA Ops:
  1.3 6.9 %collective-permute-start = (s32[48]{0:T(128)S(1)}, s32[48]{0:T(128)S(1)}, u32[]{:S(2)}, u32[]{:S(2)}) collective-permute-start(s32[48]{0:T(128)S(1)} %compare_select_fusion.2), channel_id=1, source_target_pairs={{0,16},{16,0},{32,48},{48,32},{64,80},{80,64},{96,112},{112,96},{1... | collective-permute-start | bytes 584 | tf_op jit(solution)/shard_map/ppermute | solution.py:200
  4.4 4.7 %collective-permute-start.1 = (bf16[16,32,128]{2,1,0:T(8,128)(2,1)S(1)}, bf16[16,32,128]{2,1,0:T(8,128)(2,1)S(1)}, u32[]{:S(2)}, u32[]{:S(2)}) collective-permute-start(bf16[16,32,128]{2,1,0:T(8,128)(2,1)S(1)} %get-tuple-element.12), channel_id=1, source_target_pairs={{0,16},{16,0},{32,48},{48,32},{64,80},{80,64},{96,112},{112,96},{1... | collective-permute-start | bytes 393224 | tf_op jit(solution)/shard_map/ppermute | solution.py:195
  9.1 35.6 %collective-permute-start.4 = (bf16[32,32,128]{2,1,0:T(8,128)(2,1)S(1)}, bf16[32,32,128]{2,1,0:T(8,128)(2,1)}, u32[]{:S(2)}, u32[]{:S(2)}) collective-permute-start(bf16[32,32,128]{2,1,0:T(8,128)(2,1)S(1)} %pad_maximum_fusion.refs_0_), channel_id=1, source_target_pairs={{768,0},{208,16},{800,32},{240,48},{832,64},{16,80},{864,96},{48,1... | collective-permute-start | bytes 786440 | tf_op jit(solution)/shard_map/ppermute | solution.py:197
  12.1 32.7 %collective-permute-start.3 = (bf16[32,32,128]{2,1,0:T(8,128)(2,1)S(1)}, bf16[32,32,128]{2,1,0:T(8,128)(2,1)}, u32[]{:S(2)}, u32[]{:S(2)}) collective-permute-start(bf16[32,32,128]{2,1,0:T(8,128)(2,1)S(1)} %pad_maximum_fusion.refs_0_), channel_id=1, source_target_pairs={{512,0},{144,16},{544,32},{176,48},{576,64},{208,80},{608,96},{240... | collective-permute-start | bytes 786440 | tf_op jit(solution)/shard_map/ppermute | solution.py:197
  16.3 28.4 %collective-permute-start.2 = (bf16[32,32,128]{2,1,0:T(8,128)(2,1)S(1)}, bf16[32,32,128]{2,1,0:T(8,128)(2,1)}, u32[]{:S(2)}, u32[]{:S(2)}) collective-permute-start(bf16[32,32,128]{2,1,0:T(8,128)(2,1)S(1)} %pad_maximum_fusion.refs_0_), channel_id=1, source_target_pairs={{256,0},{80,16},{288,32},{112,48},{320,64},{144,80},{352,96},{176,... | collective-permute-start | bytes 786440 | tf_op jit(solution)/shard_map/ppermute | solution.py:197
  20.4 24.3 %all-to-all-start = ((s32[8,1,32]{2,1,0:T(1,128)}), s32[8,1,32]{2,1,0:T(1,128)S(1)}, u32[]{:S(2)}, u32[]{:S(2)}) async-start(s32[8,1,32]{2,1,0:T(1,128)} %all_to_all.17), calls=%async_computation | async-start | bytes 8192 | tf_op jit(solution)/shard_map/all_to_all | solution.py:216
  38.1 1.9 %copy-start.1 = (bf16[1,1,64,24576]{3,2,1,0:T(8,128)(2,1)S(1)}, bf16[1,1,64,24576]{3,2,1,0:T(8,128)(2,1)}, u32[]{:S(2)}) copy-start(bf16[1,1,64,24576]{3,2,1,0:T(8,128)(2,1)} %param.6) | copy-start | bytes 9437188
  46.3 1.3 copy-start
  47.6 45.8 %all-to-all-start.1 = ((bf16[8,32,32,128]{3,2,1,0:T(8,128)(2,1)}), bf16[8,32,32,128]{3,2,1,0:T(8,128)(2,1)}, u32[]{:S(2)}, u32[]{:S(2)}) async-start(bf16[8,32,32,128]{3,2,1,0:T(8,128)(2,1)} %bitcast.34), calls=%async_computation.1 | async-start | bytes 4194304 | tf_op jit(solution)/shard_map/all_to_all | solution.py:224
  95.0 3.9 %collective-permute-start.5 = (bf16[48,32,128]{2,1,0:T(8,128)(2,1)S(1)}, bf16[48,32,128]{2,1,0:T(8,128)(2,1)S(1)}, u32[]{:S(2)}, u32[]{:S(2)}) collective-permute-start(bf16[48,32,128]{2,1,0:T(8,128)(2,1)S(1)} %shard_map.57), channel_id=1, source_target_pairs={{0,16},{16,0},{32,48},{48,32},{64,80},{80,64},{96,112},{112,96},{1... | collective-permute-start | bytes 1179656 | tf_op jit(solution)/shard_map/ppermute | solution.py:236

commit v6 on v5

--- a/solution.py
+++ b/solution.py
@@ -13,6 +13,7 @@
 NZ = 8
 NCORE = 2
 STEPS = 4
+MEMBERS = 8
 LIMIT = pltpu.CompilerParams(vmem_limit_bytes=16 * 1024 * 1024)
 
 
@@ -42,11 +43,98 @@
     return [(i, i ^ 1) for i in range(NY * NZ * NCORE)]
 
 
-def peer_rank(owners):
-    width = owners.shape[-1]
-    same = owners[..., :, None] == owners[..., None, :]
-    earlier = jnp.arange(width)[None, :] < jnp.arange(width)[:, None]
-    return jnp.sum((same & earlier).astype(jnp.int32), axis=-1)
+def front_kernel(here, count, amplitudes, rows, mine, send, note):
+    core = here[0] & 1
+    blocks_here = mine.shape[0]
+    for pair in range(blocks_here // 2):
+        width = 2 * BLOCK
+        block = amplitudes[:, pl.ds(pair * width, width)].T
+        for i in range(2):
+            low = block[i * BLOCK : i * BLOCK + HALF]
+            high = block[i * BLOCK + HALF : (i + 1) * BLOCK]
+            mine[2 * pair + i] = jnp.where(core == 0, low, high)
+            send[2 * pair + i] = jnp.where(core == 0, high, low)
+    ids = rows[...]
+    alive = lax.broadcasted_iota(jnp.int32, ids.shape, 1) < count[0]
+    note[...] = jnp.zeros(note.shape, jnp.float32)
+    note[0:1, : ids.shape[1]] = (ids >> 4).astype(jnp.float32)
+    note[1:2, : ids.shape[1]] = jnp.where(alive, (ids & blocks_here - 1) + 1, 0).astype(jnp.float32)
+    send[blocks_here] = note[...].astype(send.dtype)
+
+
+def front(amplitudes, rows, count, here):
+    lanes, columns = amplitudes.shape
+    blocks_here = columns // BLOCK
+    vmem = pl.BlockSpec(memory_space=pltpu.VMEM)
+    smem = pl.BlockSpec(memory_space=pltpu.SMEM)
+    return pl.pallas_call(
+        front_kernel,
+        out_shape=(
+            jax.ShapeDtypeStruct((blocks_here, HALF, lanes), amplitudes.dtype),
+            jax.ShapeDtypeStruct((blocks_here + 1, HALF, lanes), amplitudes.dtype),
+        ),
+        in_specs=[smem, smem, vmem, vmem],
+        out_specs=(vmem, vmem),
+        scratch_shapes=[pltpu.VMEM((HALF, lanes), jnp.float32)],
+        compiler_params=LIMIT,
+        cost_estimate=pl.CostEstimate(flops=0, bytes_accessed=4 * amplitudes.size, transcendentals=0),
+    )(here, count, amplitudes, rows)
+
+
+def requests_kernel(here, own, other, ask, place):
+    core = here[0] & 1
+    z = here[0] >> 1 & NZ - 1
+    y = here[0] >> 4
+    members, _, lanes = ask.shape
+    per_member = NCORE * STEPS * NCORE * CAP
+    square = (lanes, lanes)
+    down = lax.broadcasted_iota(jnp.int32, square, 0)
+    along = lax.broadcasted_iota(jnp.int32, square, 1)
+    total = jnp.zeros((members, lanes), jnp.float32)
+    for turn, note in enumerate((own, other)):
+        device = core if turn == 0 else 1 - core
+        values = note[...].astype(jnp.float32)
+        owner = values[0:1].astype(jnp.int32)
+        index = values[1:2]
+        wide = jnp.broadcast_to(values[0:1], square)
+        live = jnp.broadcast_to(index, square)
+        earlier = (wide.T == wide) & (down < along) & (live.T > 0.5)
+        rank = jnp.sum(jnp.where(earlier, 1.0, 0.0), axis=0, keepdims=True).astype(jnp.int32)
+        owner_z = owner >> 1 & NZ - 1
+        owner_y = owner >> 4
+        server = jnp.where(core == 0, owner_z, owner_y * 2 + (owner_z & 1))
+        step = jnp.where(core == 0, owner_y - y, (owner_z >> 1) - (z >> 1)) & STEPS - 1
+        within = ((device * STEPS + step) * NCORE + (owner & 1 ^ core)) * CAP + rank
+        spot = server * per_member + within
+        place[turn : turn + 1, :] = jnp.minimum(spot, members * per_member - 1)
+        rows = lax.broadcasted_iota(jnp.int32, (members, lanes), 0)
+        asked = jnp.where(rows == server, jnp.broadcast_to(index, (members, lanes)), 0.0)
+        slot = jnp.where(down == within, 1.0, 0.0)
+        total += lax.dot_general(
+            asked.astype(jnp.bfloat16),
+            slot.astype(jnp.bfloat16),
+            (((1,), (1,)), ((), ())),
+            preferred_element_type=jnp.float32,
+        )
+    found = total.astype(jnp.int32)
+    for member in range(members):
+        ask[member] = jnp.broadcast_to(found[member : member + 1], ask.shape[1:])
+
+
+def requests(own, other, here):
+    lanes = own.shape[-1]
+    vmem = pl.BlockSpec(memory_space=pltpu.VMEM)
+    return pl.pallas_call(
+        requests_kernel,
+        out_shape=(
+            jax.ShapeDtypeStruct((MEMBERS, 8, lanes), jnp.int32),
+            jax.ShapeDtypeStruct((8, lanes), jnp.int32),
+        ),
+        in_specs=[pl.BlockSpec(memory_space=pltpu.SMEM), vmem, vmem],
+        out_specs=(vmem, vmem),
+        compiler_params=LIMIT,
+        cost_estimate=pl.CostEstimate(flops=0, bytes_accessed=65536, transcendentals=0),
+    )(here, own, other)
 
 
 def stack_kernel(mine, tiles, keep, out, buf, sem):
@@ -96,16 +184,20 @@
 
 def pick_kernel(asked, *refs):
     *sources, out = refs
-    per_peer = STEPS * NCORE * CAP
+    members = asked.shape[0]
+    per_member = out.shape[0] // members
     blocks_here = sources[0].shape[0] // NCORE
-    for slot in range(out.shape[0]):
-        step = slot % per_peer // (NCORE * CAP)
-        core = slot // CAP % NCORE
-        out[slot] = sources[step][core * blocks_here + jnp.maximum(asked[slot] - 1, 0)]
+    for member in range(members):
+        for slot in range(per_member):
+            step = slot % (STEPS * NCORE * CAP) // (NCORE * CAP)
+            core = slot // CAP % NCORE
+            block = jnp.maximum(asked[member, 0, slot] - 1, 0)
+            out[member * per_member + slot] = sources[step][core * blocks_here + block]
 
 
 def pick(asked, sources):
-    slots = asked.shape[0]
+    members = asked.shape[0]
+    slots = members * NCORE * STEPS * NCORE * CAP
     shape = (slots,) + sources[0].shape[1:]
     return pl.pallas_call(
         pick_kernel,
@@ -122,11 +214,10 @@
 
 def select_kernel(place, blocks, out):
     for s in range(out.shape[0]):
-        out[s] = blocks[place[s]]
-
-
-def select(place, blocks):
-    slots = place.shape[0]
+        out[s] = blocks[place[1, s]]
+
+
+def select(place, blocks, slots):
     shape = (slots,) + blocks.shape[1:]
     return pl.pallas_call(
         select_kernel,
@@ -147,10 +238,11 @@
     *start, out = refs
     total = start[0][...] if start else jnp.zeros(out.shape, jnp.float32)
     half = 1 if start else 0
+    at = (lambda i: i) if start else (lambda i: place[0, i])
     each = 2 * GROUP
     depth = each * HALF
     for g in range(weights.shape[1] // depth):
-        lhs = jnp.concatenate([blocks[place[g * each + s]] for s in range(each)], axis=0)
+        lhs = jnp.concatenate([blocks[at(g * each + s)] for s in range(each)], axis=0)
         total += lax.dot_general(
             lhs,
             weights[half, pl.ds(g * depth, depth), :],
@@ -177,65 +269,42 @@
 
 
 def body(amplitudes, block_tiles, block_rows, tile_mask, block_counts):
-    row_ids = block_rows[0, 0]
-    slots = row_ids.shape[0]
+    slots = block_rows.shape[-1]
     cols_here = tile_mask.shape[-1] * BLOCK
     rows = amplitudes.shape[0]
-    blocks_here = amplitudes.shape[1] // BLOCK
     n_red = lax.axis_size("red")
     groups = server_groups()
-    members = len(groups[0])
+    here = lax.axis_index("col").astype(jnp.int32)
+    core = here & 1
+    here = here.reshape(1)
+
+    mine, send = front(amplitudes, block_rows[0], block_counts[0], here)
+    given = lax.ppermute(send, "col", swap_pairs())
+    chip = jnp.concatenate([mine, given[:-1]])
+    sources = [chip] + [lax.ppermute(chip, "col", step_pairs(s)) for s in range(1, STEPS)]
+
+    ask, place = requests(send[-1], given[-1], here)
+    asked = lax.all_to_all(
+        ask, "col", split_axis=0, concat_axis=0, tiled=True, axis_index_groups=groups
+    )
+
     alive = jnp.arange(slots) < block_counts[0, 0]
-    here = lax.axis_index("col")
-    core = here & 1
-    z = here >> 1 & NZ - 1
-    y = here >> 4
-
-    halves = amplitudes.T.reshape(blocks_here, NCORE, HALF, rows)
-    given = lax.ppermute(lax.dynamic_index_in_dim(halves, 1 - core, 1, False), "col", swap_pairs())
-    chip = jnp.concatenate([lax.dynamic_index_in_dim(halves, core, 1, False), given])
-    sources = [chip] + [lax.ppermute(chip, "col", step_pairs(s)) for s in range(1, STEPS)]
-
-    listed = jnp.where(alive, row_ids, -1)
-    other = lax.ppermute(listed, "col", swap_pairs())
-    lists = jnp.where(core == 0, jnp.stack([listed, other]), jnp.stack([other, listed]))
-    owners = lists >> 4
-    owner_z = owners >> 1 & NZ - 1
-    owner_y = owners >> 4
-    server = jnp.where(core == 0, owner_z, owner_y * 2 + (owner_z & 1))
-    step = jnp.where(core == 0, owner_y - y, (owner_z >> 1) - (z >> 1)) & STEPS - 1
-    away = owners & 1 ^ core
-    place = ((server * NCORE + jnp.arange(NCORE)[:, None]) * STEPS + step) * NCORE + away
-    place = place * CAP + peer_rank(owners)
-    n_places = members * NCORE * STEPS * NCORE * CAP
-
-    flat = jnp.where(lists >= 0, place, -1).reshape(-1)
-    within = ((lists & blocks_here - 1) + 1).reshape(-1)
-    match = flat[None, :] == jnp.arange(n_places)[:, None]
-    ask = jnp.sum(jnp.where(match, within[None, :], 0), axis=-1)
-    asked = lax.all_to_all(
-        ask.reshape(members, -1), "col", split_axis=0, concat_axis=0, tiled=True, axis_index_groups=groups
-    )
-
     keep = jnp.repeat(tile_mask[0, 0] * alive[:, None], BLOCK, axis=1).astype(jnp.bfloat16)
     weights = stack(core.reshape(1), block_tiles[0, 0], keep)
     asked, weights = lax.optimization_barrier((asked, weights))
-    outgoing = pick(asked.reshape(n_places), sources)
+    outgoing = pick(asked, sources)
     incoming = lax.all_to_all(
-        outgoing.reshape(members, -1, HALF, rows),
+        outgoing.reshape(MEMBERS, -1, HALF, rows),
         "col",
         split_axis=0,
         concat_axis=0,
         tiled=True,
         axis_index_groups=groups,
-    ).reshape(n_places, HALF, rows)
-
-    place = jnp.clip(place, 0, n_places - 1)
-    place_own = jnp.where(core == 0, place[0], place[1])
-    place_other = jnp.where(core == 0, place[1], place[0])
-    received = lax.ppermute(select(place_other, incoming), "col", swap_pairs())
-    first = contract(place_own, incoming, weights)
-    partial_value = contract(jnp.arange(slots, dtype=jnp.int32), received, weights, first)
+    ).reshape(-1, HALF, rows)
+
+    received = lax.ppermute(select(place, incoming, slots), "col", swap_pairs())
+    first = contract(place, incoming, weights)
+    partial_value = contract(place, received, weights, first)
 
     slices = partial_value.reshape(n_red, rows // n_red, cols_here)
     gathered = lax.all_to_all(slices, "red", split_axis=0, concat_axis=0, tiled=True)

time: 134 us -> 127 us (0.948)
  the two profiles are of different devices: /device:TPU:82 before, /device:TPU:2 now
where the time goes in v6:
time: 127 us; the launch traced here: 126 us
  blocking collectives  71.2 us (56%)
  starting transfers between devices  36.7 us (29%)
  waiting for transfers between devices  6.45 us (5%)
  Pallas kernels  5.85 us (5%)
  local copies, waits for them, and re-layouts  4.56 us (4%)
    all_to_all x1, blocking collectives, body(): lax.all_to_all(outgoing.reshape(MEMBERS, -1, HALF, rows), 'col', split_ax...  39.4 us
    all_to_all x1, blocking collectives, body(): lax.all_to_all(slices, 'red', split_axis=0, concat_axis=0, tiled=True)  17.5 us
    all_to_all x1, starting transfers between devices, body(): lax.all_to_all(ask, 'col', split_axis=0, concat_axis=0, tiled=True, axis_...  16.7 us
    ppermute x3, starting transfers between devices, body(): lax.ppermute(chip, 'col', step_pairs(s))  16.1 us
    all_to_all x1, blocking collectives, body(): lax.all_to_all(copies, 'red', split_axis=0, concat_axis=0, tiled=True)  14.3 us
    all_to_all x1, waiting for transfers between devices, body(): lax.all_to_all(ask, 'col', split_axis=0, concat_axis=0, tiled=True, axis_...  4.45 us
    unnamed x7, local copies, waits for them, and re-layouts  4.19 us
  transfers between devices with their start and end apart: 6, of which 3 were waited for; matrix products, arithmetic and copies ran while one was open for 1% of the time, Pallas kernels for 2%

profile of v6, /device:TPU:2, one launch (start us, length us, event | category | flops | bytes accessed | tf_op | source)
XLA Modules:
  0.0 126.3 jit_solution(17215543399471975513)
XLA Ops:
  0.7 0.0 copy-start.1
  0.7 0.9 copy-done.1
  1.6 0.7 copy-done.2
  2.3 0.1 shard_map.55
  2.4 1.9 %collective-permute-start = (bf16[17,32,128]{2,1,0:T(8,128)(2,1)S(1)}, bf16[17,32,128]{2,1,0:T(8,128)(2,1)S(1)}, u32[]{:S(2)}, u32[]{:S(2)}) collective-permute-start(bf16[17,32,128]{2,1,0:T(8,128)(2,1)S(1)} %get-tuple-element.11), channel_id=1, source_target_pairs={{0,16},{16,0},{32,48},{48,32},{64,80},{80,64},{96,112},{112,96},{1... | collective-permute-start | bytes 417800 | tf_op jit(solution)/shard_map/ppermute | solution.py:282
  4.3 1.3 %collective-permute-done = bf16[17,32,128]{2,1,0:T(8,128)(2,1)S(1)} collective-permute-done((bf16[17,32,128]{2,1,0:T(8,128)(2,1)S(1)}, bf16[17,32,128]{2,1,0:T(8,128)(2,1)S(1)}, u32[]{:S(2)}, u32[]{:S(2)}) %collective-permute-start) | collective-permute-done | bytes 139296 | tf_op jit(solution)/shard_map/ppermute | solution.py:282
  5.7 4.7 %collective-permute-start.3 = (bf16[32,32,128]{2,1,0:T(8,128)(2,1)S(1)}, bf16[32,32,128]{2,1,0:T(8,128)(2,1)}, u32[]{:S(2)}, u32[]{:S(2)}) collective-permute-start(bf16[32,32,128]{2,1,0:T(8,128)(2,1)S(1)} %pad_maximum_fusion.refs_0_), channel_id=1, source_target_pairs={{768,0},{208,16},{800,32},{240,48},{832,64},{16,80},{864,96},{48,1... | collective-permute-start | bytes 786440 | tf_op jit(solution)/shard_map/ppermute | solution.py:284
  10.4 6.4 %collective-permute-start.2 = (bf16[32,32,128]{2,1,0:T(8,128)(2,1)S(1)}, bf16[32,32,128]{2,1,0:T(8,128)(2,1)}, u32[]{:S(2)}, u32[]{:S(2)}) collective-permute-start(bf16[32,32,128]{2,1,0:T(8,128)(2,1)S(1)} %pad_maximum_fusion.refs_0_), channel_id=1, source_target_pairs={{512,0},{144,16},{544,32},{176,48},{576,64},{208,80},{608,96},{240... | collective-permute-start | bytes 786440 | tf_op jit(solution)/shard_map/ppermute | solution.py:284
  16.8 5.0 %collective-permute-start.1 = (bf16[32,32,128]{2,1,0:T(8,128)(2,1)S(1)}, bf16[32,32,128]{2,1,0:T(8,128)(2,1)}, u32[]{:S(2)}, u32[]{:S(2)}) collective-permute-start(bf16[32,32,128]{2,1,0:T(8,128)(2,1)S(1)} %pad_maximum_fusion.refs_0_), channel_id=1, source_target_pairs={{256,0},{80,16},{288,32},{112,48},{320,64},{144,80},{352,96},{176,... | collective-permute-start | bytes 786440 | tf_op jit(solution)/shard_map/ppermute | solution.py:284
  21.9 0.9 shard_map.56
  22.8 16.7 %all-to-all-start = ((s32[8,8,128]{2,1,0:T(8,128)}), s32[8,8,128]{2,1,0:T(8,128)S(1)}, u32[]{:S(2)}, u32[]{:S(2)}) async-start(s32[8,8,128]{2,1,0:T(8,128)} %get-tuple-element.13), calls=%async_computation | async-start | bytes 65536 | tf_op jit(solution)/shard_map/all_to_all | solution.py:287
  39.5 0.7 fusion
  40.2 0.1 copy.6
  40.3 0.1 broadcast_in_dim.4
  40.4 0.1 convert_element_type.15.keep
  40.5 0.0 copy-start
  40.5 1.9 %copy-done = bf16[1,1,64,24576]{3,2,1,0:T(8,128)(2,1)S(1)} copy-done((bf16[1,1,64,24576]{3,2,1,0:T(8,128)(2,1)S(1)}, bf16[1,1,64,24576]{3,2,1,0:T(8,128)(2,1)}, u32[]{:S(2)}) %copy-start) | copy-done | bytes 3145752
  42.4 0.6 shard_map.57.weights
  43.0 4.5 %all-to-all-done.asked = s32[8,8,128]{2,1,0:T(8,128)S(1)} async-done(((s32[8,8,128]{2,1,0:T(8,128)}), s32[8,8,128]{2,1,0:T(8,128)S(1)}, u32[]{:S(2)}, u32[]{:S(2)}) %all-to-all-start) | async-done | bytes 32800 | tf_op jit(solution)/shard_map/all_to_all | solution.py:287
  47.5 0.0 collective-permute-done.3.refs_3_
  47.5 0.0 collective-permute-done.2.refs_2_
  47.5 0.0 collective-permute-done.1.refs_1_
  47.5 1.5 %shard_map.58 = bf16[256,32,128]{2,1,0:T(8,128)(2,1)S(1)} custom-call(s32[8,8,128]{2,1,0:T(8,128)S(1)} %all-to-all-done.asked, bf16[32,32,128]{2,1,0:T(8,128)(2,1)S(1)} %pad_maximum_fusion.refs_0_, bf16[32,32,128]{2,1,0:T(8,128)(2,1)} %collective-permute-done.1.refs_1_, bf16[32,32,128]{2,1,0:T(8,128)(2,1)} %collective-permute-done.2.refs_2_, ...), custom_call_target="tpu_custom_call" | custom-call | bytes 4194304 | tf_op jit(solution)/shard_map/pallas_call | solution.py:202
  49.0 39.4 %all_to_all.20 = bf16[8,32,32,128]{3,2,1,0:T(8,128)(2,1)S(1)} all-to-all(bf16[8,32,32,128]{3,2,1,0:T(8,128)(2,1)S(1)} %bitcast.22), channel_id=1, replica_groups={{0,32,64,96,128,160,192,224},{256,288,320,352,384,416,448,480},{512,544..., dimensions={0} | all-to-all | bytes 4194304 | tf_op jit(solution)/shard_map/all_to_all | solution.py:296
  88.5 0.6 shard_map.59
  89.1 1.9 %collective-permute-start.4 = (bf16[48,32,128]{2,1,0:T(8,128)(2,1)S(1)}, bf16[48,32,128]{2,1,0:T(8,128)(2,1)S(1)}, u32[]{:S(2)}, u32[]{:S(2)}) collective-permute-start(bf16[48,32,128]{2,1,0:T(8,128)(2,1)S(1)} %shard_map.59), channel_id=1, source_target_pairs={{0,16},{16,0},{32,48},{48,32},{64,80},{80,64},{96,112},{112,96},{1... | collective-permute-start | bytes 1179656 | tf_op jit(solution)/shard_map/ppermute | solution.py:305
  91.0 1.0 shard_map.60.refs_0_
  92.1 0.7 collective-permute-done.4.blocks
  92.7 1.0 shard_map.61
  93.8 17.5 %all_to_all.21 = f32[16,8,512]{2,1,0:T(8,128)S(1)} all-to-all(f32[16,8,512]{2,1,0:T(8,128)S(1)} %bitcast.24), channel_id=1, replica_groups=mesh['col'=64,'red'=16] {'red'}, dimensions={0} | all-to-all | bytes 524288 | tf_op jit(solution)/shard_map/all_to_all | solution.py:310
  111.3 14.3 %all_to_all.22 = f32[16,8,512]{2,1,0:T(8,128)S(1)} all-to-all(f32[16,8,512]{2,1,0:T(8,128)S(1)} %broadcast_in_dim.5), channel_id=1, replica_groups=mesh['col'=64,'red'=16] {'red'}, dimensions={0} | all-to-all | bytes 524288 | tf_op jit(solution)/shard_map/all_to_all | solution.py:313
  125.6 0.7 copy.9
  (8 shorter events, 0.1 us)
Async XLA Ops:
  0.7 1.0 copy-start.1
  1.6 0.7 copy-start.2
  2.4 3.3 %collective-permute-start = (bf16[17,32,128]{2,1,0:T(8,128)(2,1)S(1)}, bf16[17,32,128]{2,1,0:T(8,128)(2,1)S(1)}, u32[]{:S(2)}, u32[]{:S(2)}) collective-permute-start(bf16[17,32,128]{2,1,0:T(8,128)(2,1)S(1)} %get-tuple-element.11), channel_id=1, source_target_pairs={{0,16},{16,0},{32,48},{48,32},{64,80},{80,64},{96,112},{112,96},{1... | collective-permute-start | bytes 417800 | tf_op jit(solution)/shard_map/ppermute | solution.py:282
  5.7 41.8 %collective-permute-start.3 = (bf16[32,32,128]{2,1,0:T(8,128)(2,1)S(1)}, bf16[32,32,128]{2,1,0:T(8,128)(2,1)}, u32[]{:S(2)}, u32[]{:S(2)}) collective-permute-start(bf16[32,32,128]{2,1,0:T(8,128)(2,1)S(1)} %pad_maximum_fusion.refs_0_), channel_id=1, source_target_pairs={{768,0},{208,16},{800,32},{240,48},{832,64},{16,80},{864,96},{48,1... | collective-permute-start | bytes 786440 | tf_op jit(solution)/shard_map/ppermute | solution.py:284
  10.4 37.1 %collective-permute-start.2 = (bf16[32,32,128]{2,1,0:T(8,128)(2,1)S(1)}, bf16[32,32,128]{2,1,0:T(8,128)(2,1)}, u32[]{:S(2)}, u32[]{:S(2)}) collective-permute-start(bf16[32,32,128]{2,1,0:T(8,128)(2,1)S(1)} %pad_maximum_fusion.refs_0_), channel_id=1, source_target_pairs={{512,0},{144,16},{544,32},{176,48},{576,64},{208,80},{608,96},{240... | collective-permute-start | bytes 786440 | tf_op jit(solution)/shard_map/ppermute | solution.py:284
  16.8 30.7 %collective-permute-start.1 = (bf16[32,32,128]{2,1,0:T(8,128)(2,1)S(1)}, bf16[32,32,128]{2,1,0:T(8,128)(2,1)}, u32[]{:S(2)}, u32[]{:S(2)}) collective-permute-start(bf16[32,32,128]{2,1,0:T(8,128)(2,1)S(1)} %pad_maximum_fusion.refs_0_), channel_id=1, source_target_pairs={{256,0},{80,16},{288,32},{112,48},{320,64},{144,80},{352,96},{176,... | collective-permute-start | bytes 786440 | tf_op jit(solution)/shard_map/ppermute | solution.py:284
  22.8 24.7 %all-to-all-start = ((s32[8,8,128]{2,1,0:T(8,128)}), s32[8,8,128]{2,1,0:T(8,128)S(1)}, u32[]{:S(2)}, u32[]{:S(2)}) async-start(s32[8,8,128]{2,1,0:T(8,128)} %get-tuple-element.13), calls=%async_computation | async-start | bytes 65536 | tf_op jit(solution)/shard_map/all_to_all | solution.py:287
  40.5 1.9 %copy-start = (bf16[1,1,64,24576]{3,2,1,0:T(8,128)(2,1)S(1)}, bf16[1,1,64,24576]{3,2,1,0:T(8,128)(2,1)}, u32[]{:S(2)}) copy-start(bf16[1,1,64,24576]{3,2,1,0:T(8,128)(2,1)} %param.6) | copy-start | bytes 9437188
  89.1 3.6 %collective-permute-start.4 = (bf16[48,32,128]{2,1,0:T(8,128)(2,1)S(1)}, bf16[48,32,128]{2,1,0:T(8,128)(2,1)S(1)}, u32[]{:S(2)}, u32[]{:S(2)}) collective-permute-start(bf16[48,32,128]{2,1,0:T(8,128)(2,1)S(1)} %shard_map.59), channel_id=1, source_target_pairs={{0,16},{16,0},{32,48},{48,32},{64,80},{80,64},{96,112},{112,96},{1... | collective-permute-start | bytes 1179656 | tf_op jit(solution)/shard_map/ppermute | solution.py:305

commit v7 on v6

--- a/solution.py
+++ b/solution.py
@@ -43,40 +43,60 @@
     return [(i, i ^ 1) for i in range(NY * NZ * NCORE)]
 
 
-def front_kernel(here, count, amplitudes, rows, mine, send, note):
+def front_kernel(here, count, amplitudes, rows, mine, send, listed, buf, ids_buf, note, sem):
     core = here[0] & 1
     blocks_here = mine.shape[0]
-    for pair in range(blocks_here // 2):
-        width = 2 * BLOCK
-        block = amplitudes[:, pl.ds(pair * width, width)].T
+    pairs, _, width = buf.shape
+    ids_copy = pltpu.make_async_copy(rows, ids_buf, sem.at[pairs])
+    ids_copy.start()
+
+    def copy(pair):
+        part = amplitudes.at[:, pl.ds(pair * width, width)]
+        return pltpu.make_async_copy(part, buf.at[pair], sem.at[pair])
+
+    for pair in range(pairs):
+        copy(pair).start()
+    for pair in range(pairs):
+        copy(pair).wait()
+        block = buf[pair].T
         for i in range(2):
             low = block[i * BLOCK : i * BLOCK + HALF]
             high = block[i * BLOCK + HALF : (i + 1) * BLOCK]
             mine[2 * pair + i] = jnp.where(core == 0, low, high)
             send[2 * pair + i] = jnp.where(core == 0, high, low)
-    ids = rows[...]
+    ids_copy.wait()
+    ids = ids_buf[...]
     alive = lax.broadcasted_iota(jnp.int32, ids.shape, 1) < count[0]
     note[...] = jnp.zeros(note.shape, jnp.float32)
     note[0:1, : ids.shape[1]] = (ids >> 4).astype(jnp.float32)
     note[1:2, : ids.shape[1]] = jnp.where(alive, (ids & blocks_here - 1) + 1, 0).astype(jnp.float32)
+    listed[...] = note[...].astype(listed.dtype)
     send[blocks_here] = note[...].astype(send.dtype)
 
 
 def front(amplitudes, rows, count, here):
     lanes, columns = amplitudes.shape
     blocks_here = columns // BLOCK
+    pairs = blocks_here // 2
     vmem = pl.BlockSpec(memory_space=pltpu.VMEM)
     smem = pl.BlockSpec(memory_space=pltpu.SMEM)
+    hbm = pl.BlockSpec(memory_space=pltpu.HBM)
     return pl.pallas_call(
         front_kernel,
         out_shape=(
             jax.ShapeDtypeStruct((blocks_here, HALF, lanes), amplitudes.dtype),
             jax.ShapeDtypeStruct((blocks_here + 1, HALF, lanes), amplitudes.dtype),
-        ),
-        in_specs=[smem, smem, vmem, vmem],
-        out_specs=(vmem, vmem),
-        scratch_shapes=[pltpu.VMEM((HALF, lanes), jnp.float32)],
-        compiler_params=LIMIT,
+            jax.ShapeDtypeStruct((HALF, lanes), amplitudes.dtype),
+        ),
+        in_specs=[smem, smem, hbm, hbm],
+        out_specs=(vmem, vmem, vmem),
+        scratch_shapes=[
+            pltpu.VMEM((pairs, lanes, 2 * BLOCK), amplitudes.dtype),
+            pltpu.VMEM(rows.shape, rows.dtype),
+            pltpu.VMEM((HALF, lanes), jnp.float32),
+            pltpu.SemaphoreType.DMA((pairs + 1,)),
+        ],
+        compiler_params=pltpu.CompilerParams(vmem_limit_bytes=60 * 1024 * 1024),
         cost_estimate=pl.CostEstimate(flops=0, bytes_accessed=4 * amplitudes.size, transcendentals=0),
     )(here, count, amplitudes, rows)
 
@@ -91,9 +111,9 @@
     down = lax.broadcasted_iota(jnp.int32, square, 0)
     along = lax.broadcasted_iota(jnp.int32, square, 1)
     total = jnp.zeros((members, lanes), jnp.float32)
-    for turn, note in enumerate((own, other)):
+    for turn, note in enumerate((own[...], other[other.shape[0] - 1])):
         device = core if turn == 0 else 1 - core
-        values = note[...].astype(jnp.float32)
+        values = note.astype(jnp.float32)
         owner = values[0:1].astype(jnp.int32)
         index = values[1:2]
         wide = jnp.broadcast_to(values[0:1], square)
@@ -212,60 +232,64 @@
     )(asked, *sources)
 
 
-def select_kernel(place, blocks, out):
-    for s in range(out.shape[0]):
-        out[s] = blocks[place[1, s]]
-
-
-def select(place, blocks, slots):
-    shape = (slots,) + blocks.shape[1:]
-    return pl.pallas_call(
-        select_kernel,
-        out_shape=jax.ShapeDtypeStruct(shape, blocks.dtype),
-        in_specs=[
-            pl.BlockSpec(memory_space=pltpu.SMEM),
-            pl.BlockSpec(memory_space=pltpu.VMEM),
-        ],
-        out_specs=pl.BlockSpec(memory_space=pltpu.VMEM),
-        compiler_params=LIMIT,
-        cost_estimate=pl.CostEstimate(
-            flops=0, bytes_accessed=2 * blocks.size, transcendentals=0
-        ),
-    )(place, blocks)
-
-
-def contract_kernel(place, blocks, weights, *refs):
-    *start, out = refs
-    total = start[0][...] if start else jnp.zeros(out.shape, jnp.float32)
-    half = 1 if start else 0
-    at = (lambda i: i) if start else (lambda i: place[0, i])
+def contract_half(blocks, weights, half, total):
     each = 2 * GROUP
     depth = each * HALF
     for g in range(weights.shape[1] // depth):
-        lhs = jnp.concatenate([blocks[at(g * each + s)] for s in range(each)], axis=0)
+        lhs = jnp.concatenate([blocks(g * each + s) for s in range(each)], axis=0)
         total += lax.dot_general(
             lhs,
             weights[half, pl.ds(g * depth, depth), :],
             (((0,), (0,)), ((), ())),
             preferred_element_type=jnp.float32,
         )
-    out[...] = total
-
-
-def contract(place, blocks, weights, *start):
+    return total
+
+
+def first_kernel(place, blocks, weights, chosen, out):
+    for s in range(chosen.shape[0]):
+        chosen[s] = blocks[place[1, s]]
+    out[...] = contract_half(
+        lambda s: blocks[place[0, s]], weights, 0, jnp.zeros(out.shape, jnp.float32)
+    )
+
+
+def second_kernel(blocks, weights, start, out):
+    out[...] = contract_half(lambda s: blocks[s], weights, 1, start[...])
+
+
+def first(place, blocks, weights):
     _, depth, cols = weights.shape
-    rows = blocks.shape[-1]
-    return pl.pallas_call(
-        contract_kernel,
-        out_shape=jax.ShapeDtypeStruct((rows, cols), jnp.float32),
-        in_specs=[pl.BlockSpec(memory_space=pltpu.SMEM)]
-        + [pl.BlockSpec(memory_space=pltpu.VMEM)] * (2 + len(start)),
-        out_specs=pl.BlockSpec(memory_space=pltpu.VMEM),
+    half, rows = blocks.shape[1:]
+    vmem = pl.BlockSpec(memory_space=pltpu.VMEM)
+    return pl.pallas_call(
+        first_kernel,
+        out_shape=(
+            jax.ShapeDtypeStruct((depth // half, half, rows), blocks.dtype),
+            jax.ShapeDtypeStruct((rows, cols), jnp.float32),
+        ),
+        in_specs=[pl.BlockSpec(memory_space=pltpu.SMEM), vmem, vmem],
+        out_specs=(vmem, vmem),
         compiler_params=LIMIT,
         cost_estimate=pl.CostEstimate(
-            flops=2 * depth * rows * cols, bytes_accessed=5 * 1024 * 1024, transcendentals=0
-        ),
-    )(place, blocks, weights, *start)
+            flops=2 * depth * rows * cols, bytes_accessed=4 * 1024 * 1024, transcendentals=0
+        ),
+    )(place, blocks, weights)
+
+
+def second(blocks, weights, start):
+    _, depth, cols = weights.shape
+    vmem = pl.BlockSpec(memory_space=pltpu.VMEM)
+    return pl.pallas_call(
+        second_kernel,
+        out_shape=jax.ShapeDtypeStruct(start.shape, start.dtype),
+        in_specs=[vmem, vmem, vmem],
+        out_specs=vmem,
+        compiler_params=LIMIT,
+        cost_estimate=pl.CostEstimate(
+            flops=2 * depth * start.size, bytes_accessed=2 * 1024 * 1024, transcendentals=0
+        ),
+    )(blocks, weights, start)
 
 
 def body(amplitudes, block_tiles, block_rows, tile_mask, block_counts):
@@ -278,12 +302,12 @@
     core = here & 1
     here = here.reshape(1)
 
-    mine, send = front(amplitudes, block_rows[0], block_counts[0], here)
+    mine, send, listed = front(amplitudes, block_rows[0], block_counts[0], here)
     given = lax.ppermute(send, "col", swap_pairs())
-    chip = jnp.concatenate([mine, given[:-1]])
+    chip = jnp.concatenate([mine, given])
     sources = [chip] + [lax.ppermute(chip, "col", step_pairs(s)) for s in range(1, STEPS)]
 
-    ask, place = requests(send[-1], given[-1], here)
+    ask, place = requests(listed, given, here)
     asked = lax.all_to_all(
         ask, "col", split_axis=0, concat_axis=0, tiled=True, axis_index_groups=groups
     )
@@ -302,9 +326,9 @@
         axis_index_groups=groups,
     ).reshape(-1, HALF, rows)
 
-    received = lax.ppermute(select(place, incoming, slots), "col", swap_pairs())
-    first = contract(place, incoming, weights)
-    partial_value = contract(place, received, weights, first)
+    chosen, product = first(place, incoming, weights)
+    received = lax.ppermute(chosen, "col", swap_pairs())
+    partial_value = second(received, weights, product)
 
     slices = partial_value.reshape(n_red, rows // n_red, cols_here)
     gathered = lax.all_to_all(slices, "red", split_axis=0, concat_axis=0, tiled=True)

time: 127 us -> 128 us (level)
    pallas_call x1, Pallas kernels: 0.12 us -> 2.14 us  [front(): pl.pallas_call(front_kernel, out_shape=(jax.ShapeDtypeStruct((blocks_here...]
    pallas_call x3 -> x2, Pallas kernels: 2.65 us -> 1.41 us  [the longest x1 1.02 us: first(): pl.pallas_call(first_kernel, out_shape=(jax.ShapeDtypeStruct((depth // ha...]
    unnamed x7 -> x6, local copies, waits for them, and re-layouts: 4.19 us -> 4.19 us
  transfers between devices with their start and end apart: 6 -> 6, of which waited for: 3 -> 3; matrix products, arithmetic and copies ran while one was open for 1% -> 2% of each run, Pallas kernels for 2% -> 1%
where the time goes in v7:
time: 128 us; the launch traced here: 127 us
  blocking collectives  71.2 us (56%)
  starting transfers between devices  36.7 us (29%)
  waiting for transfers between devices  6.77 us (5%)
  Pallas kernels  6.63 us (5%)
  local copies, waits for them, and re-layouts  4.57 us (4%)
    all_to_all x1, blocking collectives, body(): lax.all_to_all(outgoing.reshape(MEMBERS, -1, HALF, rows), 'col', split_ax...  39.4 us
    all_to_all x1, blocking collectives, body(): lax.all_to_all(slices, 'red', split_axis=0, concat_axis=0, tiled=True)  17.5 us
    all_to_all x1, starting transfers between devices, body(): lax.all_to_all(ask, 'col', split_axis=0, concat_axis=0, tiled=True, axis_...  16.7 us
    ppermute x3, starting transfers between devices, body(): lax.ppermute(chip, 'col', step_pairs(s))  16.1 us
    all_to_all x1, blocking collectives, body(): lax.all_to_all(copies, 'red', split_axis=0, concat_axis=0, tiled=True)  14.3 us
    all_to_all x1, waiting for transfers between devices, body(): lax.all_to_all(ask, 'col', split_axis=0, concat_axis=0, tiled=True, axis_...  4.45 us
    unnamed x6, local copies, waits for them, and re-layouts  4.19 us
  transfers between devices with their start and end apart: 6, of which 3 were waited for; matrix products, arithmetic and copies ran while one was open for 2% of the time, Pallas kernels for 1%

profile of v7, /device:TPU:2, one launch (start us, length us, event | category | flops | bytes accessed | tf_op | source)
XLA Modules:
  0.0 127.3 jit_solution(3782611010522712901)
XLA Ops:
  0.7 2.1 %shard_map.55 = (bf16[16,32,128]{2,1,0:T(8,128)(2,1)}, bf16[17,32,128]{2,1,0:T(8,128)(2,1)}, bf16[32,128]{1,0:T(8,128)(2,1)}) custom-call(s32[1]{0:T(128)} %bitcast.here, s32[1]{0:T(128)} %bitcast.14.count, bf16[128,1024]{1,0:T(8,128)(2,1)} %amplitudes.1, s32[1,48]{1,0:T(1,128)} %bitcast.21), custom_call_target="tpu_custom_call" | custom-call | bytes 524288 | tf_op jit(solution)/shard_map/pallas_call | solution.py:84
  2.8 1.9 %collective-permute-start = (bf16[17,32,128]{2,1,0:T(8,128)(2,1)}, bf16[17,32,128]{2,1,0:T(8,128)(2,1)S(1)}, u32[]{:S(2)}, u32[]{:S(2)}) collective-permute-start(bf16[17,32,128]{2,1,0:T(8,128)(2,1)} %get-tuple-element.15), channel_id=1, source_target_pairs={{0,16},{16,0},{32,48},{48,32},{64,80},{80,64},{96,112},{112,96},{1... | collective-permute-start | bytes 417800 | tf_op jit(solution)/shard_map/ppermute | solution.py:306
  4.7 0.9 constant_dynamic-update-slice_fusion.1
  5.6 0.6 collective-permute-done.other
  6.3 4.7 %collective-permute-start.3 = (bf16[33,32,128]{2,1,0:T(8,128)(2,1)S(1)}, bf16[33,32,128]{2,1,0:T(8,128)(2,1)}, u32[]{:S(2)}, u32[]{:S(2)}) collective-permute-start(bf16[33,32,128]{2,1,0:T(8,128)(2,1)S(1)} %constant_dynamic-update-slice_fusion.refs_0_), channel_id=1, source_target_pairs={{768,0},{208,16},{800,32},{240,48},{832,64},{16,80},{864,96},{48,1... | collective-permute-start | bytes 811016 | tf_op jit(solution)/shard_map/ppermute | solution.py:308
  11.0 6.4 %collective-permute-start.2 = (bf16[33,32,128]{2,1,0:T(8,128)(2,1)S(1)}, bf16[33,32,128]{2,1,0:T(8,128)(2,1)}, u32[]{:S(2)}, u32[]{:S(2)}) collective-permute-start(bf16[33,32,128]{2,1,0:T(8,128)(2,1)S(1)} %constant_dynamic-update-slice_fusion.refs_0_), channel_id=1, source_target_pairs={{512,0},{144,16},{544,32},{176,48},{576,64},{208,80},{608,96},{240... | collective-permute-start | bytes 811016 | tf_op jit(solution)/shard_map/ppermute | solution.py:308
  17.4 5.0 %collective-permute-start.1 = (bf16[33,32,128]{2,1,0:T(8,128)(2,1)S(1)}, bf16[33,32,128]{2,1,0:T(8,128)(2,1)}, u32[]{:S(2)}, u32[]{:S(2)}) collective-permute-start(bf16[33,32,128]{2,1,0:T(8,128)(2,1)S(1)} %constant_dynamic-update-slice_fusion.refs_0_), channel_id=1, source_target_pairs={{256,0},{80,16},{288,32},{112,48},{320,64},{144,80},{352,96},{176,... | collective-permute-start | bytes 811016 | tf_op jit(solution)/shard_map/ppermute | solution.py:308
  22.5 0.0 copy-start.1
  22.5 0.7 copy-done.1
  23.2 0.9 shard_map.56
  24.1 16.7 %all-to-all-start = ((s32[8,8,128]{2,1,0:T(8,128)}), s32[8,8,128]{2,1,0:T(8,128)S(1)}, u32[]{:S(2)}, u32[]{:S(2)}) async-start(s32[8,8,128]{2,1,0:T(8,128)} %get-tuple-element.17), calls=%async_computation | async-start | bytes 65536 | tf_op jit(solution)/shard_map/all_to_all | solution.py:311
  40.8 0.7 fusion
  41.5 0.1 copy.6
  41.6 0.1 broadcast_in_dim.4
  41.7 0.1 convert_element_type.15.keep
  41.8 0.0 copy-start
  41.8 1.9 %copy-done = bf16[1,1,64,24576]{3,2,1,0:T(8,128)(2,1)S(1)} copy-done((bf16[1,1,64,24576]{3,2,1,0:T(8,128)(2,1)S(1)}, bf16[1,1,64,24576]{3,2,1,0:T(8,128)(2,1)}, u32[]{:S(2)}) %copy-start) | copy-done | bytes 3145752
  43.7 0.6 shard_map.57.weights
  44.3 4.5 %all-to-all-done.asked = s32[8,8,128]{2,1,0:T(8,128)S(1)} async-done(((s32[8,8,128]{2,1,0:T(8,128)}), s32[8,8,128]{2,1,0:T(8,128)S(1)}, u32[]{:S(2)}, u32[]{:S(2)}) %all-to-all-start) | async-done | bytes 32800 | tf_op jit(solution)/shard_map/all_to_all | solution.py:311
  48.8 0.0 collective-permute-done.3.refs_3_
  48.8 0.0 collective-permute-done.2.refs_2_
  48.8 0.0 collective-permute-done.1.refs_1_
  48.8 1.5 %shard_map.58 = bf16[256,32,128]{2,1,0:T(8,128)(2,1)S(1)} custom-call(s32[8,8,128]{2,1,0:T(8,128)S(1)} %all-to-all-done.asked, bf16[33,32,128]{2,1,0:T(8,128)(2,1)S(1)} %constant_dynamic-update-slice_fusion.refs_0_, bf16[33,32,128]{2,1,0:T(8,128)(2,1)} %collective-permute-done.1.refs_1_, bf16[33,32,128]{2,1,0:T(8,128)(2,1)} %collective-permute-done.2.refs_2_, ...), custom_call_target="tpu_custom_call" | custom-call | bytes 4194304 | tf_op jit(solution)/shard_map/pallas_call | solution.py:222
  50.3 39.4 %all_to_all.20 = bf16[8,32,32,128]{3,2,1,0:T(8,128)(2,1)S(1)} all-to-all(bf16[8,32,32,128]{3,2,1,0:T(8,128)(2,1)S(1)} %bitcast.16), channel_id=1, replica_groups={{0,32,64,96,128,160,192,224},{256,288,320,352,384,416,448,480},{512,544..., dimensions={0} | all-to-all | bytes 4194304 | tf_op jit(solution)/shard_map/all_to_all | solution.py:320
  89.8 1.0 shard_map.59
  90.8 1.9 %collective-permute-start.4 = (bf16[48,32,128]{2,1,0:T(8,128)(2,1)S(1)}, bf16[48,32,128]{2,1,0:T(8,128)(2,1)S(1)}, u32[]{:S(2)}, u32[]{:S(2)}) collective-permute-start(bf16[48,32,128]{2,1,0:T(8,128)(2,1)S(1)} %get-tuple-element.21), channel_id=1, source_target_pairs={{0,16},{16,0},{32,48},{48,32},{64,80},{80,64},{96,112},{112,96},{1... | collective-permute-start | bytes 1179656 | tf_op jit(solution)/shard_map/ppermute | solution.py:330
  92.7 1.7 %collective-permute-done.4.blocks = bf16[48,32,128]{2,1,0:T(8,128)(2,1)S(1)} collective-permute-done((bf16[48,32,128]{2,1,0:T(8,128)(2,1)S(1)}, bf16[48,32,128]{2,1,0:T(8,128)(2,1)S(1)}, u32[]{:S(2)}, u32[]{:S(2)}) %collective-permute-start.4) | collective-permute-done | bytes 393248 | tf_op jit(solution)/shard_map/ppermute | solution.py:330
  94.4 0.4 shard_map.60
  94.8 17.5 %all_to_all.21 = f32[16,8,512]{2,1,0:T(8,128)S(1)} all-to-all(f32[16,8,512]{2,1,0:T(8,128)S(1)} %bitcast.19), channel_id=1, replica_groups=mesh['col'=64,'red'=16] {'red'}, dimensions={0} | all-to-all | bytes 524288 | tf_op jit(solution)/shard_map/all_to_all | solution.py:334
  112.3 14.3 %all_to_all.22 = f32[16,8,512]{2,1,0:T(8,128)S(1)} all-to-all(f32[16,8,512]{2,1,0:T(8,128)S(1)} %broadcast_in_dim.5), channel_id=1, replica_groups=mesh['col'=64,'red'=16] {'red'}, dimensions={0} | all-to-all | bytes 524288 | tf_op jit(solution)/shard_map/all_to_all | solution.py:337
  126.6 0.7 copy.10
  (4 shorter events, 0.1 us)
Async XLA Ops:
  2.8 3.5 %collective-permute-start = (bf16[17,32,128]{2,1,0:T(8,128)(2,1)}, bf16[17,32,128]{2,1,0:T(8,128)(2,1)S(1)}, u32[]{:S(2)}, u32[]{:S(2)}) collective-permute-start(bf16[17,32,128]{2,1,0:T(8,128)(2,1)} %get-tuple-element.15), channel_id=1, source_target_pairs={{0,16},{16,0},{32,48},{48,32},{64,80},{80,64},{96,112},{112,96},{1... | collective-permute-start | bytes 417800 | tf_op jit(solution)/shard_map/ppermute | solution.py:306
  6.3 42.5 %collective-permute-start.3 = (bf16[33,32,128]{2,1,0:T(8,128)(2,1)S(1)}, bf16[33,32,128]{2,1,0:T(8,128)(2,1)}, u32[]{:S(2)}, u32[]{:S(2)}) collective-permute-start(bf16[33,32,128]{2,1,0:T(8,128)(2,1)S(1)} %constant_dynamic-update-slice_fusion.refs_0_), channel_id=1, source_target_pairs={{768,0},{208,16},{800,32},{240,48},{832,64},{16,80},{864,96},{48,1... | collective-permute-start | bytes 811016 | tf_op jit(solution)/shard_map/ppermute | solution.py:308
  11.0 37.8 %collective-permute-start.2 = (bf16[33,32,128]{2,1,0:T(8,128)(2,1)S(1)}, bf16[33,32,128]{2,1,0:T(8,128)(2,1)}, u32[]{:S(2)}, u32[]{:S(2)}) collective-permute-start(bf16[33,32,128]{2,1,0:T(8,128)(2,1)S(1)} %constant_dynamic-update-slice_fusion.refs_0_), channel_id=1, source_target_pairs={{512,0},{144,16},{544,32},{176,48},{576,64},{208,80},{608,96},{240... | collective-permute-start | bytes 811016 | tf_op jit(solution)/shard_map/ppermute | solution.py:308
  17.4 31.4 %collective-permute-start.1 = (bf16[33,32,128]{2,1,0:T(8,128)(2,1)S(1)}, bf16[33,32,128]{2,1,0:T(8,128)(2,1)}, u32[]{:S(2)}, u32[]{:S(2)}) collective-permute-start(bf16[33,32,128]{2,1,0:T(8,128)(2,1)S(1)} %constant_dynamic-update-slice_fusion.refs_0_), channel_id=1, source_target_pairs={{256,0},{80,16},{288,32},{112,48},{320,64},{144,80},{352,96},{176,... | collective-permute-start | bytes 811016 | tf_op jit(solution)/shard_map/ppermute | solution.py:308
  22.5 0.7 copy-start.1
  24.1 24.7 %all-to-all-start = ((s32[8,8,128]{2,1,0:T(8,128)}), s32[8,8,128]{2,1,0:T(8,128)S(1)}, u32[]{:S(2)}, u32[]{:S(2)}) async-start(s32[8,8,128]{2,1,0:T(8,128)} %get-tuple-element.17), calls=%async_computation | async-start | bytes 65536 | tf_op jit(solution)/shard_map/all_to_all | solution.py:311
  41.8 1.9 %copy-start = (bf16[1,1,64,24576]{3,2,1,0:T(8,128)(2,1)S(1)}, bf16[1,1,64,24576]{3,2,1,0:T(8,128)(2,1)}, u32[]{:S(2)}) copy-start(bf16[1,1,64,24576]{3,2,1,0:T(8,128)(2,1)} %param.6) | copy-start | bytes 9437188
  90.8 3.6 %collective-permute-start.4 = (bf16[48,32,128]{2,1,0:T(8,128)(2,1)S(1)}, bf16[48,32,128]{2,1,0:T(8,128)(2,1)S(1)}, u32[]{:S(2)}, u32[]{:S(2)}) collective-permute-start(bf16[48,32,128]{2,1,0:T(8,128)(2,1)S(1)} %get-tuple-element.21), channel_id=1, source_target_pairs={{0,16},{16,0},{32,48},{48,32},{64,80},{80,64},{96,112},{112,96},{1... | collective-permute-start | bytes 1179656 | tf_op jit(solution)/shard_map/ppermute | solution.py:330

commit v8 on v3

--- a/solution.py
+++ b/solution.py
@@ -8,13 +8,93 @@
 BLOCK = 64
 CAP = 2
 GROUP = 4
-
-
-def peer_rank(owners):
-    width = owners.shape[0]
-    same = owners[:, None] == owners[None, :]
-    earlier = jnp.arange(width)[None, :] < jnp.arange(width)[:, None]
-    return jnp.sum((same & earlier).astype(jnp.int32), axis=-1)
+NY = 4
+NZ = 8
+NCORE = 2
+STEPS = 4
+MEMBERS = 8
+LIMIT = pltpu.CompilerParams(vmem_limit_bytes=16 * 1024 * 1024)
+
+
+def col_index(y, z, core):
+    return (y % NY * NZ + z % NZ) * NCORE + core
+
+
+def server_groups():
+    along_z = [[col_index(y, z, 0) for z in range(NZ)] for y in range(NY)]
+    along_y = [
+        [col_index(y, 2 * pair + odd, 1) for y in range(NY) for odd in range(2)]
+        for pair in range(NZ // 2)
+    ]
+    return along_z + along_y
+
+
+def step_pairs(step):
+    pairs = []
+    for y in range(NY):
+        for z in range(NZ):
+            pairs.append((col_index(y + step, z, 0), col_index(y, z, 0)))
+            pairs.append((col_index(y, z + 2 * step, 1), col_index(y, z, 1)))
+    return pairs
+
+
+def swap_pairs():
+    return [(i, i ^ 1) for i in range(NY * NZ * NCORE)]
+
+
+def requests_kernel(here, count, rows, ask, place):
+    core = here[0] & 1
+    z = here[0] >> 1 & NZ - 1
+    y = here[0] >> 4
+    members, _, lanes = ask.shape
+    slots = rows.shape[1]
+    per_member = STEPS * NCORE * CAP
+    square = (lanes, lanes)
+    down = lax.broadcasted_iota(jnp.int32, square, 0)
+    along = lax.broadcasted_iota(jnp.int32, square, 1)
+    place[...] = jnp.zeros(place.shape, jnp.int32)
+    place[0:1, :slots] = rows[...]
+    ids = place[0:1, :]
+    live = along < jnp.minimum(count[0], slots)
+    owner = ids >> 4
+    index = jnp.where(live[0:1], (ids & 15) + 1, 0).astype(jnp.float32)
+    wide = jnp.broadcast_to(owner.astype(jnp.float32), square)
+    earlier = (wide.T == wide) & (down < along) & (down < jnp.minimum(count[0], slots))
+    rank = jnp.sum(jnp.where(earlier, 1.0, 0.0), axis=0, keepdims=True).astype(jnp.int32)
+    owner_z = owner >> 1 & NZ - 1
+    owner_y = owner >> 4
+    server = jnp.where(core == 0, owner_z, owner_y * 2 + (owner_z & 1))
+    step = jnp.where(core == 0, owner_y - y, (owner_z >> 1) - (z >> 1)) & STEPS - 1
+    within = (step * NCORE + (owner & 1 ^ core)) * CAP + rank
+    place[0:1, :] = jnp.minimum(server * per_member + within, members * per_member - 1)
+    line = lax.broadcasted_iota(jnp.int32, (members, lanes), 0)
+    asked = jnp.where(line == server, jnp.broadcast_to(index, (members, lanes)), 0.0)
+    slot = jnp.where(down == within, 1.0, 0.0)
+    found = lax.dot_general(
+        asked.astype(jnp.bfloat16),
+        slot.astype(jnp.bfloat16),
+        (((1,), (1,)), ((), ())),
+        preferred_element_type=jnp.float32,
+    ).astype(jnp.int32)
+    for member in range(members):
+        ask[member] = jnp.broadcast_to(found[member : member + 1], ask.shape[1:])
+
+
+def requests(here, count, rows):
+    lanes = 128
+    vmem = pl.BlockSpec(memory_space=pltpu.VMEM)
+    smem = pl.BlockSpec(memory_space=pltpu.SMEM)
+    return pl.pallas_call(
+        requests_kernel,
+        out_shape=(
+            jax.ShapeDtypeStruct((MEMBERS, 8, lanes), jnp.int32),
+            jax.ShapeDtypeStruct((8, lanes), jnp.int32),
+        ),
+        in_specs=[smem, smem, vmem],
+        out_specs=(vmem, vmem),
+        compiler_params=LIMIT,
+        cost_estimate=pl.CostEstimate(flops=0, bytes_accessed=65536, transcendentals=0),
+    )(here, count, rows)
 
 
 def stack_kernel(tiles, keep, out, buf, sem):
@@ -49,18 +129,48 @@
             pltpu.VMEM((chunks, BLOCK, GROUP * cols), tiles.dtype),
             pltpu.SemaphoreType.DMA((chunks,)),
         ],
-        compiler_params=pltpu.CompilerParams(vmem_limit_bytes=16 * 1024 * 1024),
+        compiler_params=LIMIT,
         cost_estimate=pl.CostEstimate(
             flops=slots * BLOCK * cols, bytes_accessed=4 * slots * BLOCK * cols, transcendentals=0
         ),
     )(tiles, keep)
+
+
+def pick_kernel(asked, *refs):
+    *sources, out = refs
+    members = asked.shape[0]
+    per_member = out.shape[0] // members
+    blocks_here = sources[0].shape[0] // NCORE
+    for member in range(members):
+        for slot in range(per_member):
+            step = slot // (NCORE * CAP)
+            core = slot // CAP % NCORE
+            block = jnp.maximum(asked[member, 0, slot] - 1, 0)
+            out[member * per_member + slot] = sources[step][core * blocks_here + block]
+
+
+def pick(asked, sources):
+    members = asked.shape[0]
+    slots = members * STEPS * NCORE * CAP
+    shape = (slots,) + sources[0].shape[1:]
+    return pl.pallas_call(
+        pick_kernel,
+        out_shape=jax.ShapeDtypeStruct(shape, sources[0].dtype),
+        in_specs=[pl.BlockSpec(memory_space=pltpu.SMEM)]
+        + [pl.BlockSpec(memory_space=pltpu.VMEM)] * len(sources),
+        out_specs=pl.BlockSpec(memory_space=pltpu.VMEM),
+        compiler_params=LIMIT,
+        cost_estimate=pl.CostEstimate(
+            flops=0, bytes_accessed=4 * slots * BLOCK * shape[-1], transcendentals=0
+        ),
+    )(asked, *sources)
 
 
 def contract_kernel(place, blocks, weights, out):
     total = jnp.zeros(out.shape, jnp.float32)
     depth = GROUP * BLOCK
     for g in range(weights.shape[0] // depth):
-        lhs = jnp.concatenate([blocks[place[g * GROUP + s]] for s in range(GROUP)], axis=0)
+        lhs = jnp.concatenate([blocks[place[0, g * GROUP + s]] for s in range(GROUP)], axis=0)
         total += lax.dot_general(
             lhs,
             weights[pl.ds(g * depth, depth), :],
@@ -82,7 +192,7 @@
             pl.BlockSpec(memory_space=pltpu.VMEM),
         ],
         out_specs=pl.BlockSpec(memory_space=pltpu.VMEM),
-        compiler_params=pltpu.CompilerParams(vmem_limit_bytes=16 * 1024 * 1024),
+        compiler_params=LIMIT,
         cost_estimate=pl.CostEstimate(
             flops=2 * depth * rows * cols, bytes_accessed=5 * 1024 * 1024, transcendentals=0
         ),
@@ -90,31 +200,36 @@
 
 
 def body(amplitudes, block_tiles, block_rows, tile_mask, block_counts):
-    row_ids = block_rows[0, 0]
-    slots = row_ids.shape[0]
-    col_tiles = tile_mask.shape[-1]
-    cols_here = col_tiles * BLOCK
+    slots = block_rows.shape[-1]
+    cols_here = tile_mask.shape[-1] * BLOCK
     rows = amplitudes.shape[0]
-    blocks_here = amplitudes.shape[1] // BLOCK
-    n_col = lax.axis_size("col")
     n_red = lax.axis_size("red")
+    groups = server_groups()
+    here = lax.axis_index("col").astype(jnp.int32).reshape(1)
+
+    own = amplitudes.T.reshape(-1, BLOCK, rows)
+    chip = jnp.concatenate([own, lax.ppermute(own, "col", swap_pairs())])
+    sources = [chip] + [lax.ppermute(chip, "col", step_pairs(s)) for s in range(1, STEPS)]
+
+    ask, place = requests(here, block_counts[0], block_rows[0])
+    asked = lax.all_to_all(
+        ask, "col", split_axis=0, concat_axis=0, tiled=True, axis_index_groups=groups
+    )
+
     alive = jnp.arange(slots) < block_counts[0, 0]
-
-    owners = row_ids // blocks_here
-    place = owners * CAP + peer_rank(owners)
-    here = (place[None, :] == jnp.arange(n_col * CAP)[:, None]) & alive[None, :]
-    ask = jnp.sum(jnp.where(here, (row_ids % blocks_here + 1)[None, :], 0), axis=-1)
-    asked = lax.all_to_all(ask.reshape(n_col, CAP), "col", split_axis=0, concat_axis=0, tiled=True)
-
-    blocks = amplitudes.T.reshape(blocks_here, BLOCK, rows)
-    outgoing = blocks[jnp.maximum(asked - 1, 0)]
-    incoming = lax.all_to_all(outgoing, "col", split_axis=0, concat_axis=0, tiled=True)
-
     keep = jnp.repeat(tile_mask[0, 0] * alive[:, None], BLOCK, axis=1).astype(jnp.bfloat16)
     weights = stack(block_tiles[0, 0], keep)
-    partial_value = contract(
-        jnp.clip(place, 0, n_col * CAP - 1), incoming.reshape(n_col * CAP, BLOCK, rows), weights
-    )
+    asked, weights = lax.optimization_barrier((asked, weights))
+    outgoing = pick(asked, sources)
+    incoming = lax.all_to_all(
+        outgoing.reshape(MEMBERS, -1, BLOCK, rows),
+        "col",
+        split_axis=0,
+        concat_axis=0,
+        tiled=True,
+        axis_index_groups=groups,
+    ).reshape(-1, BLOCK, rows)
+    partial_value = contract(place, incoming, weights)
 
     slices = partial_value.reshape(n_red, rows // n_red, cols_here)
     gathered = lax.all_to_all(slices, "red", split_axis=0, concat_axis=0, tiled=True)

time: 134 us -> 133 us (level)
  the two profiles are of different devices: /device:TPU:114 before, /device:TPU:2 now
where the time goes in v8:
time: 133 us; the launch traced here: 132 us
  blocking collectives  76.8 us (58%)
  starting transfers between devices  34.7 us (26%)
  waiting for transfers between devices  9.21 us (7%)
  local copies, waits for them, and re-layouts  4.72 us (4%)
  Pallas kernels  4.47 us (3%)
  other arithmetic  1.56 us (1%)
    all_to_all x1, blocking collectives, body(): lax.all_to_all(outgoing.reshape(MEMBERS, -1, BLOCK, rows), 'col', split_a...  44.9 us
    all_to_all x1, blocking collectives, body(): lax.all_to_all(slices, 'red', split_axis=0, concat_axis=0, tiled=True)  17.9 us
    all_to_all x1, starting transfers between devices, body(): lax.all_to_all(ask, 'col', split_axis=0, concat_axis=0, tiled=True, axis_...  16.7 us
    ppermute x3, starting transfers between devices, body(): lax.ppermute(chip, 'col', step_pairs(s))  16.1 us
    all_to_all x1, blocking collectives, body(): lax.all_to_all(copies, 'red', split_axis=0, concat_axis=0, tiled=True)  13.9 us
    all_to_all x1, waiting for transfers between devices, body(): lax.all_to_all(ask, 'col', split_axis=0, concat_axis=0, tiled=True, axis_...  7.7 us
    unnamed x5, local copies, waits for them, and re-layouts  3.24 us
  transfers between devices with their start and end apart: 5, of which 2 were waited for; matrix products, arithmetic and copies ran while one was open for 1% of the time, Pallas kernels for 1%

profile of v8, /device:TPU:2, one launch (start us, length us, event | category | flops | bytes accessed | tf_op | source)
XLA Modules:
  0.0 132.2 jit_solution(12460400047636895152)
XLA Ops:
  0.0 1.1 copy.7
  1.1 1.9 %collective-permute-start = (bf16[16,64,128]{2,1,0:T(8,128)(2,1)S(1)}, bf16[16,64,128]{2,1,0:T(8,128)(2,1)S(1)}, u32[]{:S(2)}, u32[]{:S(2)}) collective-permute-start(bf16[16,64,128]{2,1,0:T(8,128)(2,1)S(1)} %bitcast.23), channel_id=1, source_target_pairs={{0,16},{16,0},{32,48},{48,32},{64,80},{80,64},{96,112},{112,96},{1... | collective-permute-start | bytes 786440 | tf_op jit(solution)/shard_map/ppermute | solution.py:211
  3.1 1.5 %collective-permute-done = bf16[16,64,128]{2,1,0:T(8,128)(2,1)S(1)} collective-permute-done((bf16[16,64,128]{2,1,0:T(8,128)(2,1)S(1)}, bf16[16,64,128]{2,1,0:T(8,128)(2,1)S(1)}, u32[]{:S(2)}, u32[]{:S(2)}) %collective-permute-start) | collective-permute-done | bytes 262176 | tf_op jit(solution)/shard_map/ppermute | solution.py:211
  4.6 0.8 pad_maximum_fusion.refs_0_
  5.4 4.7 %collective-permute-start.3 = (bf16[32,64,128]{2,1,0:T(8,128)(2,1)}, bf16[32,64,128]{2,1,0:T(8,128)(2,1)}, u32[]{:S(2)}, u32[]{:S(2)}) collective-permute-start(bf16[32,64,128]{2,1,0:T(8,128)(2,1)} %pad_maximum_fusion.refs_0_), channel_id=1, source_target_pairs={{768,0},{208,16},{800,32},{240,48},{832,64},{16,80},{864,96},{48,1... | collective-permute-start | bytes 1572872 | tf_op jit(solution)/shard_map/ppermute | solution.py:212
  10.1 6.4 %collective-permute-start.2 = (bf16[32,64,128]{2,1,0:T(8,128)(2,1)}, bf16[32,64,128]{2,1,0:T(8,128)(2,1)}, u32[]{:S(2)}, u32[]{:S(2)}) collective-permute-start(bf16[32,64,128]{2,1,0:T(8,128)(2,1)} %pad_maximum_fusion.refs_0_), channel_id=1, source_target_pairs={{512,0},{144,16},{544,32},{176,48},{576,64},{208,80},{608,96},{240... | collective-permute-start | bytes 1572872 | tf_op jit(solution)/shard_map/ppermute | solution.py:212
  16.5 5.0 %collective-permute-start.1 = (bf16[32,64,128]{2,1,0:T(8,128)(2,1)}, bf16[32,64,128]{2,1,0:T(8,128)(2,1)}, u32[]{:S(2)}, u32[]{:S(2)}) collective-permute-start(bf16[32,64,128]{2,1,0:T(8,128)(2,1)} %pad_maximum_fusion.refs_0_), channel_id=1, source_target_pairs={{256,0},{80,16},{288,32},{112,48},{320,64},{144,80},{352,96},{176,... | collective-permute-start | bytes 1572872 | tf_op jit(solution)/shard_map/ppermute | solution.py:212
  22.2 0.0 copy-start.1
  22.2 0.6 copy-done.1
  22.9 0.9 shard_map.55
  23.7 16.7 %all-to-all-start = ((s32[8,8,128]{2,1,0:T(8,128)}), s32[8,8,128]{2,1,0:T(8,128)S(1)}, u32[]{:S(2)}, u32[]{:S(2)}) async-start(s32[8,8,128]{2,1,0:T(8,128)} %get-tuple-element.10), calls=%async_computation | async-start | bytes 65536 | tf_op jit(solution)/shard_map/all_to_all | solution.py:215
  40.4 0.7 fusion
  41.1 0.1 copy.6
  41.2 0.1 broadcast_in_dim.4
  41.4 0.1 convert_element_type.15.keep
  41.5 0.0 copy-start
  41.5 1.9 %copy-done = bf16[1,1,64,24576]{3,2,1,0:T(8,128)(2,1)S(1)} copy-done((bf16[1,1,64,24576]{3,2,1,0:T(8,128)(2,1)S(1)}, bf16[1,1,64,24576]{3,2,1,0:T(8,128)(2,1)}, u32[]{:S(2)}) %copy-start) | copy-done | bytes 3145752
  43.4 0.6 shard_map.56.weights
  44.0 7.7 %all-to-all-done.asked = s32[8,8,128]{2,1,0:T(8,128)S(1)} async-done(((s32[8,8,128]{2,1,0:T(8,128)}), s32[8,8,128]{2,1,0:T(8,128)S(1)}, u32[]{:S(2)}, u32[]{:S(2)}) %all-to-all-start) | async-done | bytes 32800 | tf_op jit(solution)/shard_map/all_to_all | solution.py:215
  51.7 0.0 collective-permute-done.3.refs_3_
  51.7 0.0 collective-permute-done.2.refs_2_
  51.7 0.0 collective-permute-done.1.refs_1_
  51.7 1.7 %shard_map.57 = bf16[128,64,128]{2,1,0:T(8,128)(2,1)S(1)} custom-call(s32[8,8,128]{2,1,0:T(8,128)S(1)} %all-to-all-done.asked, bf16[32,64,128]{2,1,0:T(8,128)(2,1)} %pad_maximum_fusion.refs_0_, bf16[32,64,128]{2,1,0:T(8,128)(2,1)} %collective-permute-done.1.refs_1_, bf16[32,64,128]{2,1,0:T(8,128)(2,1)} %collective-permute-done.2.refs_2_, ...), custom_call_target="tpu_custom_call" | custom-call | bytes 4194304 | tf_op jit(solution)/shard_map/pallas_call | solution.py:156
  53.5 44.9 %all_to_all.20 = bf16[8,16,64,128]{3,2,1,0:T(8,128)(2,1)S(1)} all-to-all(bf16[8,16,64,128]{3,2,1,0:T(8,128)(2,1)S(1)} %bitcast.17), channel_id=1, replica_groups={{0,32,64,96,128,160,192,224},{256,288,320,352,384,416,448,480},{512,544..., dimensions={0} | all-to-all | bytes 4194304 | tf_op jit(solution)/shard_map/all_to_all | solution.py:224
  98.4 1.2 shard_map.58
  99.6 17.9 %all_to_all.21 = f32[16,8,512]{2,1,0:T(8,128)S(1)} all-to-all(f32[16,8,512]{2,1,0:T(8,128)S(1)} %bitcast.20), channel_id=1, replica_groups=mesh['col'=64,'red'=16] {'red'}, dimensions={0} | all-to-all | bytes 524288 | tf_op jit(solution)/shard_map/all_to_all | solution.py:235
  117.6 13.9 %all_to_all.22 = f32[16,8,512]{2,1,0:T(8,128)S(1)} all-to-all(f32[16,8,512]{2,1,0:T(8,128)S(1)} %broadcast_in_dim.5), channel_id=1, replica_groups=mesh['col'=64,'red'=16] {'red'}, dimensions={0} | all-to-all | bytes 524288 | tf_op jit(solution)/shard_map/all_to_all | solution.py:238
  131.5 0.7 copy.10
  (3 shorter events, 0.0 us)
Async XLA Ops:
  1.1 3.4 %collective-permute-start = (bf16[16,64,128]{2,1,0:T(8,128)(2,1)S(1)}, bf16[16,64,128]{2,1,0:T(8,128)(2,1)S(1)}, u32[]{:S(2)}, u32[]{:S(2)}) collective-permute-start(bf16[16,64,128]{2,1,0:T(8,128)(2,1)S(1)} %bitcast.23), channel_id=1, source_target_pairs={{0,16},{16,0},{32,48},{48,32},{64,80},{80,64},{96,112},{112,96},{1... | collective-permute-start | bytes 786440 | tf_op jit(solution)/shard_map/ppermute | solution.py:211
  5.4 46.3 %collective-permute-start.3 = (bf16[32,64,128]{2,1,0:T(8,128)(2,1)}, bf16[32,64,128]{2,1,0:T(8,128)(2,1)}, u32[]{:S(2)}, u32[]{:S(2)}) collective-permute-start(bf16[32,64,128]{2,1,0:T(8,128)(2,1)} %pad_maximum_fusion.refs_0_), channel_id=1, source_target_pairs={{768,0},{208,16},{800,32},{240,48},{832,64},{16,80},{864,96},{48,1... | collective-permute-start | bytes 1572872 | tf_op jit(solution)/shard_map/ppermute | solution.py:212
  10.1 41.6 %collective-permute-start.2 = (bf16[32,64,128]{2,1,0:T(8,128)(2,1)}, bf16[32,64,128]{2,1,0:T(8,128)(2,1)}, u32[]{:S(2)}, u32[]{:S(2)}) collective-permute-start(bf16[32,64,128]{2,1,0:T(8,128)(2,1)} %pad_maximum_fusion.refs_0_), channel_id=1, source_target_pairs={{512,0},{144,16},{544,32},{176,48},{576,64},{208,80},{608,96},{240... | collective-permute-start | bytes 1572872 | tf_op jit(solution)/shard_map/ppermute | solution.py:212
  16.5 35.2 %collective-permute-start.1 = (bf16[32,64,128]{2,1,0:T(8,128)(2,1)}, bf16[32,64,128]{2,1,0:T(8,128)(2,1)}, u32[]{:S(2)}, u32[]{:S(2)}) collective-permute-start(bf16[32,64,128]{2,1,0:T(8,128)(2,1)} %pad_maximum_fusion.refs_0_), channel_id=1, source_target_pairs={{256,0},{80,16},{288,32},{112,48},{320,64},{144,80},{352,96},{176,... | collective-permute-start | bytes 1572872 | tf_op jit(solution)/shard_map/ppermute | solution.py:212
  22.2 0.7 copy-start.1
  23.7 28.0 %all-to-all-start = ((s32[8,8,128]{2,1,0:T(8,128)}), s32[8,8,128]{2,1,0:T(8,128)S(1)}, u32[]{:S(2)}, u32[]{:S(2)}) async-start(s32[8,8,128]{2,1,0:T(8,128)} %get-tuple-element.10), calls=%async_computation | async-start | bytes 65536 | tf_op jit(solution)/shard_map/all_to_all | solution.py:215
  41.5 1.9 %copy-start = (bf16[1,1,64,24576]{3,2,1,0:T(8,128)(2,1)S(1)}, bf16[1,1,64,24576]{3,2,1,0:T(8,128)(2,1)}, u32[]{:S(2)}) copy-start(bf16[1,1,64,24576]{3,2,1,0:T(8,128)(2,1)} %param.6) | copy-start | bytes 9437188

commit v9 on v6

--- a/solution.py
+++ b/solution.py
@@ -91,9 +91,9 @@
     down = lax.broadcasted_iota(jnp.int32, square, 0)
     along = lax.broadcasted_iota(jnp.int32, square, 1)
     total = jnp.zeros((members, lanes), jnp.float32)
-    for turn, note in enumerate((own, other)):
+    for turn, note in enumerate((own[...], other[other.shape[0] - 1])):
         device = core if turn == 0 else 1 - core
-        values = note[...].astype(jnp.float32)
+        values = note.astype(jnp.float32)
         owner = values[0:1].astype(jnp.int32)
         index = values[1:2]
         wide = jnp.broadcast_to(values[0:1], square)
@@ -234,38 +234,59 @@
     )(place, blocks)
 
 
-def contract_kernel(place, blocks, weights, *refs):
-    *start, out = refs
-    total = start[0][...] if start else jnp.zeros(out.shape, jnp.float32)
-    half = 1 if start else 0
-    at = (lambda i: i) if start else (lambda i: place[0, i])
+def contract_half(blocks, weights, half, total):
     each = 2 * GROUP
     depth = each * HALF
     for g in range(weights.shape[1] // depth):
-        lhs = jnp.concatenate([blocks[at(g * each + s)] for s in range(each)], axis=0)
+        lhs = jnp.concatenate([blocks(g * each + s) for s in range(each)], axis=0)
         total += lax.dot_general(
             lhs,
             weights[half, pl.ds(g * depth, depth), :],
             (((0,), (0,)), ((), ())),
             preferred_element_type=jnp.float32,
         )
-    out[...] = total
-
-
-def contract(place, blocks, weights, *start):
+    return total
+
+
+def first_kernel(place, blocks, weights, out):
+    out[...] = contract_half(
+        lambda s: blocks[place[0, s]], weights, 0, jnp.zeros(out.shape, jnp.float32)
+    )
+
+
+def second_kernel(blocks, weights, start, out):
+    out[...] = contract_half(lambda s: blocks[s], weights, 1, start[...])
+
+
+def first(place, blocks, weights):
     _, depth, cols = weights.shape
     rows = blocks.shape[-1]
-    return pl.pallas_call(
-        contract_kernel,
+    vmem = pl.BlockSpec(memory_space=pltpu.VMEM)
+    return pl.pallas_call(
+        first_kernel,
         out_shape=jax.ShapeDtypeStruct((rows, cols), jnp.float32),
-        in_specs=[pl.BlockSpec(memory_space=pltpu.SMEM)]
-        + [pl.BlockSpec(memory_space=pltpu.VMEM)] * (2 + len(start)),
-        out_specs=pl.BlockSpec(memory_space=pltpu.VMEM),
-        compiler_params=LIMIT,
-        cost_estimate=pl.CostEstimate(
-            flops=2 * depth * rows * cols, bytes_accessed=5 * 1024 * 1024, transcendentals=0
-        ),
-    )(place, blocks, weights, *start)
+        in_specs=[pl.BlockSpec(memory_space=pltpu.SMEM), vmem, vmem],
+        out_specs=vmem,
+        compiler_params=LIMIT,
+        cost_estimate=pl.CostEstimate(
+            flops=2 * depth * rows * cols, bytes_accessed=4 * 1024 * 1024, transcendentals=0
+        ),
+    )(place, blocks, weights)
+
+
+def second(blocks, weights, start):
+    _, depth, cols = weights.shape
+    vmem = pl.BlockSpec(memory_space=pltpu.VMEM)
+    return pl.pallas_call(
+        second_kernel,
+        out_shape=jax.ShapeDtypeStruct(start.shape, start.dtype),
+        in_specs=[vmem, vmem, vmem],
+        out_specs=vmem,
+        compiler_params=LIMIT,
+        cost_estimate=pl.CostEstimate(
+            flops=2 * depth * start.size, bytes_accessed=2 * 1024 * 1024, transcendentals=0
+        ),
+    )(blocks, weights, start)
 
 
 def body(amplitudes, block_tiles, block_rows, tile_mask, block_counts):
@@ -283,7 +304,7 @@
     chip = jnp.concatenate([mine, given[:-1]])
     sources = [chip] + [lax.ppermute(chip, "col", step_pairs(s)) for s in range(1, STEPS)]
 
-    ask, place = requests(send[-1], given[-1], here)
+    ask, place = requests(send[-1], given, here)
     asked = lax.all_to_all(
         ask, "col", split_axis=0, concat_axis=0, tiled=True, axis_index_groups=groups
     )
@@ -303,8 +324,7 @@
     ).reshape(-1, HALF, rows)
 
     received = lax.ppermute(select(place, incoming, slots), "col", swap_pairs())
-    first = contract(place, incoming, weights)
-    partial_value = contract(place, received, weights, first)
+    partial_value = second(received, weights, first(place, incoming, weights))
 
     slices = partial_value.reshape(n_red, rows // n_red, cols_here)
     gathered = lax.all_to_all(slices, "red", split_axis=0, concat_axis=0, tiled=True)

time: 127 us -> 126 us (level)
  no operation moved by 1% of the time
where the time goes in v9:
time: 126 us
  blocking collectives  71.2 us (57%)
  starting transfers between devices  36.7 us (29%)
  waiting for transfers between devices  6.45 us (5%)
  Pallas kernels  5.25 us (4%)
  local copies, waits for them, and re-layouts  4.56 us (4%)
    all_to_all x1, blocking collectives, body(): lax.all_to_all(outgoing.reshape(MEMBERS, -1, HALF, rows), 'col', split_ax...  39.4 us
    all_to_all x1, blocking collectives, body(): lax.all_to_all(slices, 'red', split_axis=0, concat_axis=0, tiled=True)  17.5 us
    all_to_all x1, starting transfers between devices, body(): lax.all_to_all(ask, 'col', split_axis=0, concat_axis=0, tiled=True, axis_...  16.7 us
    ppermute x3, starting transfers between devices, body(): lax.ppermute(chip, 'col', step_pairs(s))  16.1 us
    all_to_all x1, blocking collectives, body(): lax.all_to_all(copies, 'red', split_axis=0, concat_axis=0, tiled=True)  14.3 us
    all_to_all x1, waiting for transfers between devices, body(): lax.all_to_all(ask, 'col', split_axis=0, concat_axis=0, tiled=True, axis_...  4.45 us
    unnamed x7, local copies, waits for them, and re-layouts  4.19 us
  transfers between devices with their start and end apart: 6, of which 3 were waited for; matrix products, arithmetic and copies ran while one was open for 1% of the time, Pallas kernels for 2%

profile of v9, /device:TPU:2, one launch (start us, length us, event | category | flops | bytes accessed | tf_op | source)
XLA Modules:
  0.0 125.7 jit_solution(13953744710678554244)
XLA Ops:
  0.7 0.0 copy-start.1
  0.7 0.9 copy-done.1
  1.6 0.7 copy-done.2
  2.3 0.1 shard_map.55
  2.4 1.9 %collective-permute-start = (bf16[17,32,128]{2,1,0:T(8,128)(2,1)S(1)}, bf16[17,32,128]{2,1,0:T(8,128)(2,1)S(1)}, u32[]{:S(2)}, u32[]{:S(2)}) collective-permute-start(bf16[17,32,128]{2,1,0:T(8,128)(2,1)S(1)} %get-tuple-element.11), channel_id=1, source_target_pairs={{0,16},{16,0},{32,48},{48,32},{64,80},{80,64},{96,112},{112,96},{1... | collective-permute-start | bytes 417800 | tf_op jit(solution)/shard_map/ppermute | solution.py:303
  4.3 1.3 %collective-permute-done.other = bf16[17,32,128]{2,1,0:T(8,128)(2,1)S(1)} collective-permute-done((bf16[17,32,128]{2,1,0:T(8,128)(2,1)S(1)}, bf16[17,32,128]{2,1,0:T(8,128)(2,1)S(1)}, u32[]{:S(2)}, u32[]{:S(2)}) %collective-permute-start) | collective-permute-done | bytes 139296 | tf_op jit(solution)/shard_map/ppermute | solution.py:303
  5.7 4.7 %collective-permute-start.3 = (bf16[32,32,128]{2,1,0:T(8,128)(2,1)S(1)}, bf16[32,32,128]{2,1,0:T(8,128)(2,1)}, u32[]{:S(2)}, u32[]{:S(2)}) collective-permute-start(bf16[32,32,128]{2,1,0:T(8,128)(2,1)S(1)} %pad_maximum_fusion.refs_0_), channel_id=1, source_target_pairs={{768,0},{208,16},{800,32},{240,48},{832,64},{16,80},{864,96},{48,1... | collective-permute-start | bytes 786440 | tf_op jit(solution)/shard_map/ppermute | solution.py:305
  10.4 6.4 %collective-permute-start.2 = (bf16[32,32,128]{2,1,0:T(8,128)(2,1)S(1)}, bf16[32,32,128]{2,1,0:T(8,128)(2,1)}, u32[]{:S(2)}, u32[]{:S(2)}) collective-permute-start(bf16[32,32,128]{2,1,0:T(8,128)(2,1)S(1)} %pad_maximum_fusion.refs_0_), channel_id=1, source_target_pairs={{512,0},{144,16},{544,32},{176,48},{576,64},{208,80},{608,96},{240... | collective-permute-start | bytes 786440 | tf_op jit(solution)/shard_map/ppermute | solution.py:305
  16.8 5.0 %collective-permute-start.1 = (bf16[32,32,128]{2,1,0:T(8,128)(2,1)S(1)}, bf16[32,32,128]{2,1,0:T(8,128)(2,1)}, u32[]{:S(2)}, u32[]{:S(2)}) collective-permute-start(bf16[32,32,128]{2,1,0:T(8,128)(2,1)S(1)} %pad_maximum_fusion.refs_0_), channel_id=1, source_target_pairs={{256,0},{80,16},{288,32},{112,48},{320,64},{144,80},{352,96},{176,... | collective-permute-start | bytes 786440 | tf_op jit(solution)/shard_map/ppermute | solution.py:305
  21.9 0.9 shard_map.56
  22.8 16.7 %all-to-all-start = ((s32[8,8,128]{2,1,0:T(8,128)}), s32[8,8,128]{2,1,0:T(8,128)S(1)}, u32[]{:S(2)}, u32[]{:S(2)}) async-start(s32[8,8,128]{2,1,0:T(8,128)} %get-tuple-element.13), calls=%async_computation | async-start | bytes 65536 | tf_op jit(solution)/shard_map/all_to_all | solution.py:308
  39.5 0.7 fusion
  40.2 0.1 copy.6
  40.3 0.1 broadcast_in_dim.4
  40.4 0.1 convert_element_type.15.keep
  40.5 0.0 copy-start
  40.5 1.9 %copy-done = bf16[1,1,64,24576]{3,2,1,0:T(8,128)(2,1)S(1)} copy-done((bf16[1,1,64,24576]{3,2,1,0:T(8,128)(2,1)S(1)}, bf16[1,1,64,24576]{3,2,1,0:T(8,128)(2,1)}, u32[]{:S(2)}) %copy-start) | copy-done | bytes 3145752
  42.4 0.6 shard_map.57.weights
  43.1 4.5 %all-to-all-done.asked = s32[8,8,128]{2,1,0:T(8,128)S(1)} async-done(((s32[8,8,128]{2,1,0:T(8,128)}), s32[8,8,128]{2,1,0:T(8,128)S(1)}, u32[]{:S(2)}, u32[]{:S(2)}) %all-to-all-start) | async-done | bytes 32800 | tf_op jit(solution)/shard_map/all_to_all | solution.py:308
  47.5 0.0 collective-permute-done.3.refs_3_
  47.5 0.0 collective-permute-done.2.refs_2_
  47.5 0.0 collective-permute-done.1.refs_1_
  47.5 1.5 %shard_map.58 = bf16[256,32,128]{2,1,0:T(8,128)(2,1)S(1)} custom-call(s32[8,8,128]{2,1,0:T(8,128)S(1)} %all-to-all-done.asked, bf16[32,32,128]{2,1,0:T(8,128)(2,1)S(1)} %pad_maximum_fusion.refs_0_, bf16[32,32,128]{2,1,0:T(8,128)(2,1)} %collective-permute-done.1.refs_1_, bf16[32,32,128]{2,1,0:T(8,128)(2,1)} %collective-permute-done.2.refs_2_, ...), custom_call_target="tpu_custom_call" | custom-call | bytes 4194304 | tf_op jit(solution)/shard_map/pallas_call | solution.py:202
  49.0 39.4 %all_to_all.20 = bf16[8,32,32,128]{3,2,1,0:T(8,128)(2,1)S(1)} all-to-all(bf16[8,32,32,128]{3,2,1,0:T(8,128)(2,1)S(1)} %bitcast.20), channel_id=1, replica_groups={{0,32,64,96,128,160,192,224},{256,288,320,352,384,416,448,480},{512,544..., dimensions={0} | all-to-all | bytes 4194304 | tf_op jit(solution)/shard_map/all_to_all | solution.py:317
  88.5 0.6 shard_map.59
  89.1 1.9 %collective-permute-start.4 = (bf16[48,32,128]{2,1,0:T(8,128)(2,1)S(1)}, bf16[48,32,128]{2,1,0:T(8,128)(2,1)S(1)}, u32[]{:S(2)}, u32[]{:S(2)}) collective-permute-start(bf16[48,32,128]{2,1,0:T(8,128)(2,1)S(1)} %shard_map.59), channel_id=1, source_target_pairs={{0,16},{16,0},{32,48},{48,32},{64,80},{80,64},{96,112},{112,96},{1... | collective-permute-start | bytes 1179656 | tf_op jit(solution)/shard_map/ppermute | solution.py:326
  91.0 1.0 shard_map.60.start
  92.1 0.7 collective-permute-done.4.blocks
  92.7 0.4 shard_map.61
  93.2 17.5 %all_to_all.21 = f32[16,8,512]{2,1,0:T(8,128)S(1)} all-to-all(f32[16,8,512]{2,1,0:T(8,128)S(1)} %bitcast.22), channel_id=1, replica_groups=mesh['col'=64,'red'=16] {'red'}, dimensions={0} | all-to-all | bytes 524288 | tf_op jit(solution)/shard_map/all_to_all | solution.py:330
  110.7 14.3 %all_to_all.22 = f32[16,8,512]{2,1,0:T(8,128)S(1)} all-to-all(f32[16,8,512]{2,1,0:T(8,128)S(1)} %broadcast_in_dim.5), channel_id=1, replica_groups=mesh['col'=64,'red'=16] {'red'}, dimensions={0} | all-to-all | bytes 524288 | tf_op jit(solution)/shard_map/all_to_all | solution.py:333
  125.0 0.7 copy.9
  (7 shorter events, 0.1 us)
Async XLA Ops:
  0.7 1.0 copy-start.1
  1.6 0.7 copy-start.2
  2.4 3.3 %collective-permute-start = (bf16[17,32,128]{2,1,0:T(8,128)(2,1)S(1)}, bf16[17,32,128]{2,1,0:T(8,128)(2,1)S(1)}, u32[]{:S(2)}, u32[]{:S(2)}) collective-permute-start(bf16[17,32,128]{2,1,0:T(8,128)(2,1)S(1)} %get-tuple-element.11), channel_id=1, source_target_pairs={{0,16},{16,0},{32,48},{48,32},{64,80},{80,64},{96,112},{112,96},{1... | collective-permute-start | bytes 417800 | tf_op jit(solution)/shard_map/ppermute | solution.py:303
  5.7 41.8 %collective-permute-start.3 = (bf16[32,32,128]{2,1,0:T(8,128)(2,1)S(1)}, bf16[32,32,128]{2,1,0:T(8,128)(2,1)}, u32[]{:S(2)}, u32[]{:S(2)}) collective-permute-start(bf16[32,32,128]{2,1,0:T(8,128)(2,1)S(1)} %pad_maximum_fusion.refs_0_), channel_id=1, source_target_pairs={{768,0},{208,16},{800,32},{240,48},{832,64},{16,80},{864,96},{48,1... | collective-permute-start | bytes 786440 | tf_op jit(solution)/shard_map/ppermute | solution.py:305
  10.4 37.1 %collective-permute-start.2 = (bf16[32,32,128]{2,1,0:T(8,128)(2,1)S(1)}, bf16[32,32,128]{2,1,0:T(8,128)(2,1)}, u32[]{:S(2)}, u32[]{:S(2)}) collective-permute-start(bf16[32,32,128]{2,1,0:T(8,128)(2,1)S(1)} %pad_maximum_fusion.refs_0_), channel_id=1, source_target_pairs={{512,0},{144,16},{544,32},{176,48},{576,64},{208,80},{608,96},{240... | collective-permute-start | bytes 786440 | tf_op jit(solution)/shard_map/ppermute | solution.py:305
  16.8 30.7 %collective-permute-start.1 = (bf16[32,32,128]{2,1,0:T(8,128)(2,1)S(1)}, bf16[32,32,128]{2,1,0:T(8,128)(2,1)}, u32[]{:S(2)}, u32[]{:S(2)}) collective-permute-start(bf16[32,32,128]{2,1,0:T(8,128)(2,1)S(1)} %pad_maximum_fusion.refs_0_), channel_id=1, source_target_pairs={{256,0},{80,16},{288,32},{112,48},{320,64},{144,80},{352,96},{176,... | collective-permute-start | bytes 786440 | tf_op jit(solution)/shard_map/ppermute | solution.py:305
  22.8 24.7 %all-to-all-start = ((s32[8,8,128]{2,1,0:T(8,128)}), s32[8,8,128]{2,1,0:T(8,128)S(1)}, u32[]{:S(2)}, u32[]{:S(2)}) async-start(s32[8,8,128]{2,1,0:T(8,128)} %get-tuple-element.13), calls=%async_computation | async-start | bytes 65536 | tf_op jit(solution)/shard_map/all_to_all | solution.py:308
  40.5 1.9 %copy-start = (bf16[1,1,64,24576]{3,2,1,0:T(8,128)(2,1)S(1)}, bf16[1,1,64,24576]{3,2,1,0:T(8,128)(2,1)}, u32[]{:S(2)}) copy-start(bf16[1,1,64,24576]{3,2,1,0:T(8,128)(2,1)} %param.6) | copy-start | bytes 9437188
  89.1 3.6 %collective-permute-start.4 = (bf16[48,32,128]{2,1,0:T(8,128)(2,1)S(1)}, bf16[48,32,128]{2,1,0:T(8,128)(2,1)S(1)}, u32[]{:S(2)}, u32[]{:S(2)}) collective-permute-start(bf16[48,32,128]{2,1,0:T(8,128)(2,1)S(1)} %shard_map.59), channel_id=1, source_target_pairs={{0,16},{16,0},{32,48},{48,32},{64,80},{80,64},{96,112},{112,96},{1... | collective-permute-start | bytes 1179656 | tf_op jit(solution)/shard_map/ppermute | solution.py:326

commit v10 on v9

--- a/solution.py
+++ b/solution.py
@@ -13,6 +13,7 @@
 NZ = 8
 NCORE = 2
 STEPS = 4
+ORDER = (0, 1, 3, 2)
 MEMBERS = 8
 LIMIT = pltpu.CompilerParams(vmem_limit_bytes=16 * 1024 * 1024)
 
@@ -192,7 +193,7 @@
             step = slot % (STEPS * NCORE * CAP) // (NCORE * CAP)
             core = slot // CAP % NCORE
             block = jnp.maximum(asked[member, 0, slot] - 1, 0)
-            out[member * per_member + slot] = sources[step][core * blocks_here + block]
+            out[member * per_member + slot] = sources[ORDER.index(step)][core * blocks_here + block]
 
 
 def pick(asked, sources):
@@ -302,7 +303,7 @@
     mine, send = front(amplitudes, block_rows[0], block_counts[0], here)
     given = lax.ppermute(send, "col", swap_pairs())
     chip = jnp.concatenate([mine, given[:-1]])
-    sources = [chip] + [lax.ppermute(chip, "col", step_pairs(s)) for s in range(1, STEPS)]
+    sources = [chip] + [lax.ppermute(chip, "col", step_pairs(s)) for s in ORDER[1:]]
 
     ask, place = requests(send[-1], given, here)
     asked = lax.all_to_all(

time: 126 us -> 126 us (level)
  no operation moved by 1% of the time
where the time goes in v10:
time: 126 us
  blocking collectives  71.2 us (57%)
  starting transfers between devices  36.7 us (29%)
  waiting for transfers between devices  6.46 us (5%)
  Pallas kernels  5.25 us (4%)
  local copies, waits for them, and re-layouts  4.56 us (4%)
    all_to_all x1, blocking collectives, body(): lax.all_to_all(outgoing.reshape(MEMBERS, -1, HALF, rows), 'col', split_ax...  39.4 us
    all_to_all x1, blocking collectives, body(): lax.all_to_all(slices, 'red', split_axis=0, concat_axis=0, tiled=True)  17.5 us
    all_to_all x1, starting transfers between devices, body(): lax.all_to_all(ask, 'col', split_axis=0, concat_axis=0, tiled=True, axis_...  16.7 us
    ppermute x3, starting transfers between devices, body(): lax.ppermute(chip, 'col', step_pairs(s))  16.1 us
    all_to_all x1, blocking collectives, body(): lax.all_to_all(copies, 'red', split_axis=0, concat_axis=0, tiled=True)  14.3 us
    all_to_all x1, waiting for transfers between devices, body(): lax.all_to_all(ask, 'col', split_axis=0, concat_axis=0, tiled=True, axis_...  4.45 us
    unnamed x7, local copies, waits for them, and re-layouts  4.19 us
  transfers between devices with their start and end apart: 6, of which 3 were waited for; matrix products, arithmetic and copies ran while one was open for 1% of the time, Pallas kernels for 2%

profile of v10, /device:TPU:2, one launch (start us, length us, event | category | flops | bytes accessed | tf_op | source)
XLA Modules:
  0.0 125.7 jit_solution(1417568229270473977)
XLA Ops:
  0.7 0.0 copy-start.1
  0.7 0.9 copy-done.1
  1.6 0.7 copy-done.2
  2.3 0.1 shard_map.55
  2.4 1.9 %collective-permute-start = (bf16[17,32,128]{2,1,0:T(8,128)(2,1)S(1)}, bf16[17,32,128]{2,1,0:T(8,128)(2,1)S(1)}, u32[]{:S(2)}, u32[]{:S(2)}) collective-permute-start(bf16[17,32,128]{2,1,0:T(8,128)(2,1)S(1)} %get-tuple-element.11), channel_id=1, source_target_pairs={{0,16},{16,0},{32,48},{48,32},{64,80},{80,64},{96,112},{112,96},{1... | collective-permute-start | bytes 417800 | tf_op jit(solution)/shard_map/ppermute | solution.py:304
  4.3 1.3 %collective-permute-done.other = bf16[17,32,128]{2,1,0:T(8,128)(2,1)S(1)} collective-permute-done((bf16[17,32,128]{2,1,0:T(8,128)(2,1)S(1)}, bf16[17,32,128]{2,1,0:T(8,128)(2,1)S(1)}, u32[]{:S(2)}, u32[]{:S(2)}) %collective-permute-start) | collective-permute-done | bytes 139296 | tf_op jit(solution)/shard_map/ppermute | solution.py:304
  5.7 8.2 %collective-permute-start.3 = (bf16[32,32,128]{2,1,0:T(8,128)(2,1)S(1)}, bf16[32,32,128]{2,1,0:T(8,128)(2,1)}, u32[]{:S(2)}, u32[]{:S(2)}) collective-permute-start(bf16[32,32,128]{2,1,0:T(8,128)(2,1)S(1)} %pad_maximum_fusion.refs_0_), channel_id=1, source_target_pairs={{512,0},{144,16},{544,32},{176,48},{576,64},{208,80},{608,96},{240... | collective-permute-start | bytes 786440 | tf_op jit(solution)/shard_map/ppermute | solution.py:306
  13.9 2.9 %collective-permute-start.2 = (bf16[32,32,128]{2,1,0:T(8,128)(2,1)S(1)}, bf16[32,32,128]{2,1,0:T(8,128)(2,1)}, u32[]{:S(2)}, u32[]{:S(2)}) collective-permute-start(bf16[32,32,128]{2,1,0:T(8,128)(2,1)S(1)} %pad_maximum_fusion.refs_0_), channel_id=1, source_target_pairs={{768,0},{208,16},{800,32},{240,48},{832,64},{16,80},{864,96},{48,1... | collective-permute-start | bytes 786440 | tf_op jit(solution)/shard_map/ppermute | solution.py:306
  16.8 5.0 %collective-permute-start.1 = (bf16[32,32,128]{2,1,0:T(8,128)(2,1)S(1)}, bf16[32,32,128]{2,1,0:T(8,128)(2,1)}, u32[]{:S(2)}, u32[]{:S(2)}) collective-permute-start(bf16[32,32,128]{2,1,0:T(8,128)(2,1)S(1)} %pad_maximum_fusion.refs_0_), channel_id=1, source_target_pairs={{256,0},{80,16},{288,32},{112,48},{320,64},{144,80},{352,96},{176,... | collective-permute-start | bytes 786440 | tf_op jit(solution)/shard_map/ppermute | solution.py:306
  21.9 0.9 shard_map.56
  22.8 16.7 %all-to-all-start = ((s32[8,8,128]{2,1,0:T(8,128)}), s32[8,8,128]{2,1,0:T(8,128)S(1)}, u32[]{:S(2)}, u32[]{:S(2)}) async-start(s32[8,8,128]{2,1,0:T(8,128)} %get-tuple-element.13), calls=%async_computation | async-start | bytes 65536 | tf_op jit(solution)/shard_map/all_to_all | solution.py:309
  39.5 0.7 fusion
  40.2 0.1 copy.6
  40.3 0.1 broadcast_in_dim.4
  40.4 0.1 convert_element_type.15.keep
  40.5 0.0 copy-start
  40.5 1.9 %copy-done = bf16[1,1,64,24576]{3,2,1,0:T(8,128)(2,1)S(1)} copy-done((bf16[1,1,64,24576]{3,2,1,0:T(8,128)(2,1)S(1)}, bf16[1,1,64,24576]{3,2,1,0:T(8,128)(2,1)}, u32[]{:S(2)}) %copy-start) | copy-done | bytes 3145752
  42.4 0.6 shard_map.57.weights
  43.0 4.5 %all-to-all-done.asked = s32[8,8,128]{2,1,0:T(8,128)S(1)} async-done(((s32[8,8,128]{2,1,0:T(8,128)}), s32[8,8,128]{2,1,0:T(8,128)S(1)}, u32[]{:S(2)}, u32[]{:S(2)}) %all-to-all-start) | async-done | bytes 32800 | tf_op jit(solution)/shard_map/all_to_all | solution.py:309
  47.5 0.0 collective-permute-done.3.refs_3_
  47.5 0.0 collective-permute-done.2.refs_2_
  47.5 0.0 collective-permute-done.1.refs_1_
  47.5 1.5 %shard_map.58 = bf16[256,32,128]{2,1,0:T(8,128)(2,1)S(1)} custom-call(s32[8,8,128]{2,1,0:T(8,128)S(1)} %all-to-all-done.asked, bf16[32,32,128]{2,1,0:T(8,128)(2,1)S(1)} %pad_maximum_fusion.refs_0_, bf16[32,32,128]{2,1,0:T(8,128)(2,1)} %collective-permute-done.1.refs_1_, bf16[32,32,128]{2,1,0:T(8,128)(2,1)} %collective-permute-done.2.refs_2_, ...), custom_call_target="tpu_custom_call" | custom-call | bytes 4194304 | tf_op jit(solution)/shard_map/pallas_call | solution.py:203
  49.0 39.4 %all_to_all.20 = bf16[8,32,32,128]{3,2,1,0:T(8,128)(2,1)S(1)} all-to-all(bf16[8,32,32,128]{3,2,1,0:T(8,128)(2,1)S(1)} %bitcast.20), channel_id=1, replica_groups={{0,32,64,96,128,160,192,224},{256,288,320,352,384,416,448,480},{512,544..., dimensions={0} | all-to-all | bytes 4194304 | tf_op jit(solution)/shard_map/all_to_all | solution.py:318
  88.5 0.6 shard_map.59
  89.1 1.9 %collective-permute-start.4 = (bf16[48,32,128]{2,1,0:T(8,128)(2,1)S(1)}, bf16[48,32,128]{2,1,0:T(8,128)(2,1)S(1)}, u32[]{:S(2)}, u32[]{:S(2)}) collective-permute-start(bf16[48,32,128]{2,1,0:T(8,128)(2,1)S(1)} %shard_map.59), channel_id=1, source_target_pairs={{0,16},{16,0},{32,48},{48,32},{64,80},{80,64},{96,112},{112,96},{1... | collective-permute-start | bytes 1179656 | tf_op jit(solution)/shard_map/ppermute | solution.py:327
  91.0 1.0 shard_map.60.start
  92.0 0.7 collective-permute-done.4.blocks
  92.7 0.4 shard_map.61
  93.2 17.5 %all_to_all.21 = f32[16,8,512]{2,1,0:T(8,128)S(1)} all-to-all(f32[16,8,512]{2,1,0:T(8,128)S(1)} %bitcast.22), channel_id=1, replica_groups=mesh['col'=64,'red'=16] {'red'}, dimensions={0} | all-to-all | bytes 524288 | tf_op jit(solution)/shard_map/all_to_all | solution.py:331
  110.7 14.3 %all_to_all.22 = f32[16,8,512]{2,1,0:T(8,128)S(1)} all-to-all(f32[16,8,512]{2,1,0:T(8,128)S(1)} %broadcast_in_dim.5), channel_id=1, replica_groups=mesh['col'=64,'red'=16] {'red'}, dimensions={0} | all-to-all | bytes 524288 | tf_op jit(solution)/shard_map/all_to_all | solution.py:334
  125.0 0.7 copy.9
  (7 shorter events, 0.1 us)
Async XLA Ops:
  0.7 1.0 copy-start.1
  1.6 0.7 copy-start.2
  2.4 3.3 %collective-permute-start = (bf16[17,32,128]{2,1,0:T(8,128)(2,1)S(1)}, bf16[17,32,128]{2,1,0:T(8,128)(2,1)S(1)}, u32[]{:S(2)}, u32[]{:S(2)}) collective-permute-start(bf16[17,32,128]{2,1,0:T(8,128)(2,1)S(1)} %get-tuple-element.11), channel_id=1, source_target_pairs={{0,16},{16,0},{32,48},{48,32},{64,80},{80,64},{96,112},{112,96},{1... | collective-permute-start | bytes 417800 | tf_op jit(solution)/shard_map/ppermute | solution.py:304
  5.7 41.8 %collective-permute-start.3 = (bf16[32,32,128]{2,1,0:T(8,128)(2,1)S(1)}, bf16[32,32,128]{2,1,0:T(8,128)(2,1)}, u32[]{:S(2)}, u32[]{:S(2)}) collective-permute-start(bf16[32,32,128]{2,1,0:T(8,128)(2,1)S(1)} %pad_maximum_fusion.refs_0_), channel_id=1, source_target_pairs={{512,0},{144,16},{544,32},{176,48},{576,64},{208,80},{608,96},{240... | collective-permute-start | bytes 786440 | tf_op jit(solution)/shard_map/ppermute | solution.py:306
  13.9 33.6 %collective-permute-start.2 = (bf16[32,32,128]{2,1,0:T(8,128)(2,1)S(1)}, bf16[32,32,128]{2,1,0:T(8,128)(2,1)}, u32[]{:S(2)}, u32[]{:S(2)}) collective-permute-start(bf16[32,32,128]{2,1,0:T(8,128)(2,1)S(1)} %pad_maximum_fusion.refs_0_), channel_id=1, source_target_pairs={{768,0},{208,16},{800,32},{240,48},{832,64},{16,80},{864,96},{48,1... | collective-permute-start | bytes 786440 | tf_op jit(solution)/shard_map/ppermute | solution.py:306
  16.8 30.7 %collective-permute-start.1 = (bf16[32,32,128]{2,1,0:T(8,128)(2,1)S(1)}, bf16[32,32,128]{2,1,0:T(8,128)(2,1)}, u32[]{:S(2)}, u32[]{:S(2)}) collective-permute-start(bf16[32,32,128]{2,1,0:T(8,128)(2,1)S(1)} %pad_maximum_fusion.refs_0_), channel_id=1, source_target_pairs={{256,0},{80,16},{288,32},{112,48},{320,64},{144,80},{352,96},{176,... | collective-permute-start | bytes 786440 | tf_op jit(solution)/shard_map/ppermute | solution.py:306
  22.8 24.7 %all-to-all-start = ((s32[8,8,128]{2,1,0:T(8,128)}), s32[8,8,128]{2,1,0:T(8,128)S(1)}, u32[]{:S(2)}, u32[]{:S(2)}) async-start(s32[8,8,128]{2,1,0:T(8,128)} %get-tuple-element.13), calls=%async_computation | async-start | bytes 65536 | tf_op jit(solution)/shard_map/all_to_all | solution.py:309
  40.5 1.9 %copy-start = (bf16[1,1,64,24576]{3,2,1,0:T(8,128)(2,1)S(1)}, bf16[1,1,64,24576]{3,2,1,0:T(8,128)(2,1)}, u32[]{:S(2)}) copy-start(bf16[1,1,64,24576]{3,2,1,0:T(8,128)(2,1)} %param.6) | copy-start | bytes 9437188
  89.1 3.6 %collective-permute-start.4 = (bf16[48,32,128]{2,1,0:T(8,128)(2,1)S(1)}, bf16[48,32,128]{2,1,0:T(8,128)(2,1)S(1)}, u32[]{:S(2)}, u32[]{:S(2)}) collective-permute-start(bf16[48,32,128]{2,1,0:T(8,128)(2,1)S(1)} %shard_map.59), channel_id=1, source_target_pairs={{0,16},{16,0},{32,48},{48,32},{64,80},{80,64},{96,112},{112,96},{1... | collective-permute-start | bytes 1179656 | tf_op jit(solution)/shard_map/ppermute | solution.py:327

commit v11 on v10

--- a/solution.py
+++ b/solution.py
@@ -128,7 +128,7 @@
     return pl.pallas_call(
         requests_kernel,
         out_shape=(
-            jax.ShapeDtypeStruct((MEMBERS, 8, lanes), jnp.int32),
+            jax.ShapeDtypeStruct((MEMBERS, 1, lanes), jnp.int32),
             jax.ShapeDtypeStruct((8, lanes), jnp.int32),
         ),
         in_specs=[pl.BlockSpec(memory_space=pltpu.SMEM), vmem, vmem],

time: 126 us -> 126 us (level)
  no operation moved by 1% of the time
where the time goes in v11:
time: 126 us
  blocking collectives  71.6 us (57%)
  starting transfers between devices  36.7 us (29%)
  waiting for transfers between devices  6.03 us (5%)
  Pallas kernels  5.22 us (4%)
  local copies, waits for them, and re-layouts  4.56 us (4%)
    all_to_all x1, blocking collectives, body(): lax.all_to_all(outgoing.reshape(MEMBERS, -1, HALF, rows), 'col', split_ax...  39.8 us
    all_to_all x1, blocking collectives, body(): lax.all_to_all(slices, 'red', split_axis=0, concat_axis=0, tiled=True)  17.5 us
    all_to_all x1, starting transfers between devices, body(): lax.all_to_all(ask, 'col', split_axis=0, concat_axis=0, tiled=True, axis_...  16.7 us
    ppermute x3, starting transfers between devices, body(): lax.ppermute(chip, 'col', step_pairs(s))  16.1 us
    all_to_all x1, blocking collectives, body(): lax.all_to_all(copies, 'red', split_axis=0, concat_axis=0, tiled=True)  14.3 us
    unnamed x7, local copies, waits for them, and re-layouts  4.19 us
    all_to_all x1, waiting for transfers between devices, body(): lax.all_to_all(ask, 'col', split_axis=0, concat_axis=0, tiled=True, axis_...  4.03 us
  transfers between devices with their start and end apart: 6, of which 3 were waited for; matrix products, arithmetic and copies ran while one was open for 1% of the time, Pallas kernels for 2%

profile of v11, /device:TPU:2, one launch (start us, length us, event | category | flops | bytes accessed | tf_op | source)
XLA Modules:
  0.0 125.7 jit_solution(8234936292386277209)
XLA Ops:
  0.7 0.0 copy-start.1
  0.7 0.9 copy-done.1
  1.6 0.7 copy-done.2
  2.3 0.1 shard_map.55
  2.4 1.9 %collective-permute-start = (bf16[17,32,128]{2,1,0:T(8,128)(2,1)S(1)}, bf16[17,32,128]{2,1,0:T(8,128)(2,1)S(1)}, u32[]{:S(2)}, u32[]{:S(2)}) collective-permute-start(bf16[17,32,128]{2,1,0:T(8,128)(2,1)S(1)} %get-tuple-element.11), channel_id=1, source_target_pairs={{0,16},{16,0},{32,48},{48,32},{64,80},{80,64},{96,112},{112,96},{1... | collective-permute-start | bytes 417800 | tf_op jit(solution)/shard_map/ppermute | solution.py:304
  4.3 1.3 %collective-permute-done.other = bf16[17,32,128]{2,1,0:T(8,128)(2,1)S(1)} collective-permute-done((bf16[17,32,128]{2,1,0:T(8,128)(2,1)S(1)}, bf16[17,32,128]{2,1,0:T(8,128)(2,1)S(1)}, u32[]{:S(2)}, u32[]{:S(2)}) %collective-permute-start) | collective-permute-done | bytes 139296 | tf_op jit(solution)/shard_map/ppermute | solution.py:304
  5.7 8.2 %collective-permute-start.3 = (bf16[32,32,128]{2,1,0:T(8,128)(2,1)S(1)}, bf16[32,32,128]{2,1,0:T(8,128)(2,1)}, u32[]{:S(2)}, u32[]{:S(2)}) collective-permute-start(bf16[32,32,128]{2,1,0:T(8,128)(2,1)S(1)} %pad_maximum_fusion.refs_0_), channel_id=1, source_target_pairs={{512,0},{144,16},{544,32},{176,48},{576,64},{208,80},{608,96},{240... | collective-permute-start | bytes 786440 | tf_op jit(solution)/shard_map/ppermute | solution.py:306
  13.9 2.9 %collective-permute-start.2 = (bf16[32,32,128]{2,1,0:T(8,128)(2,1)S(1)}, bf16[32,32,128]{2,1,0:T(8,128)(2,1)}, u32[]{:S(2)}, u32[]{:S(2)}) collective-permute-start(bf16[32,32,128]{2,1,0:T(8,128)(2,1)S(1)} %pad_maximum_fusion.refs_0_), channel_id=1, source_target_pairs={{768,0},{208,16},{800,32},{240,48},{832,64},{16,80},{864,96},{48,1... | collective-permute-start | bytes 786440 | tf_op jit(solution)/shard_map/ppermute | solution.py:306
  16.8 5.0 %collective-permute-start.1 = (bf16[32,32,128]{2,1,0:T(8,128)(2,1)S(1)}, bf16[32,32,128]{2,1,0:T(8,128)(2,1)}, u32[]{:S(2)}, u32[]{:S(2)}) collective-permute-start(bf16[32,32,128]{2,1,0:T(8,128)(2,1)S(1)} %pad_maximum_fusion.refs_0_), channel_id=1, source_target_pairs={{256,0},{80,16},{288,32},{112,48},{320,64},{144,80},{352,96},{176,... | collective-permute-start | bytes 786440 | tf_op jit(solution)/shard_map/ppermute | solution.py:306
  21.9 0.9 shard_map.56
  22.8 16.7 %all-to-all-start = ((s32[8,1,128]{2,1,0:T(1,128)}), s32[8,1,128]{2,1,0:T(1,128)S(1)}, u32[]{:S(2)}, u32[]{:S(2)}) async-start(s32[8,1,128]{2,1,0:T(1,128)} %get-tuple-element.13), calls=%async_computation | async-start | bytes 8192 | tf_op jit(solution)/shard_map/all_to_all | solution.py:309
  39.4 0.7 fusion
  40.1 0.1 copy.6
  40.2 0.1 broadcast_in_dim.4
  40.4 0.1 convert_element_type.15.keep
  40.5 0.0 copy-start
  40.5 1.9 %copy-done = bf16[1,1,64,24576]{3,2,1,0:T(8,128)(2,1)S(1)} copy-done((bf16[1,1,64,24576]{3,2,1,0:T(8,128)(2,1)S(1)}, bf16[1,1,64,24576]{3,2,1,0:T(8,128)(2,1)}, u32[]{:S(2)}) %copy-start) | copy-done | bytes 3145752
  42.4 0.6 shard_map.57.weights
  43.0 4.0 %all-to-all-done.asked = s32[8,1,128]{2,1,0:T(1,128)S(1)} async-done(((s32[8,1,128]{2,1,0:T(1,128)}), s32[8,1,128]{2,1,0:T(1,128)S(1)}, u32[]{:S(2)}, u32[]{:S(2)}) %all-to-all-start) | async-done | bytes 4128 | tf_op jit(solution)/shard_map/all_to_all | solution.py:309
  47.1 0.0 collective-permute-done.3.refs_3_
  47.1 0.0 collective-permute-done.2.refs_2_
  47.1 0.0 collective-permute-done.1.refs_1_
  47.1 1.5 %shard_map.58 = bf16[256,32,128]{2,1,0:T(8,128)(2,1)S(1)} custom-call(s32[8,1,128]{2,1,0:T(1,128)S(1)} %all-to-all-done.asked, bf16[32,32,128]{2,1,0:T(8,128)(2,1)S(1)} %pad_maximum_fusion.refs_0_, bf16[32,32,128]{2,1,0:T(8,128)(2,1)} %collective-permute-done.1.refs_1_, bf16[32,32,128]{2,1,0:T(8,128)(2,1)} %collective-permute-done.2.refs_2_, ...), custom_call_target="tpu_custom_call" | custom-call | bytes 4194304 | tf_op jit(solution)/shard_map/pallas_call | solution.py:203
  48.6 39.8 %all_to_all.20 = bf16[8,32,32,128]{3,2,1,0:T(8,128)(2,1)S(1)} all-to-all(bf16[8,32,32,128]{3,2,1,0:T(8,128)(2,1)S(1)} %bitcast.20), channel_id=1, replica_groups={{0,32,64,96,128,160,192,224},{256,288,320,352,384,416,448,480},{512,544..., dimensions={0} | all-to-all | bytes 4194304 | tf_op jit(solution)/shard_map/all_to_all | solution.py:318
  88.4 0.6 shard_map.59
  89.1 1.9 %collective-permute-start.4 = (bf16[48,32,128]{2,1,0:T(8,128)(2,1)S(1)}, bf16[48,32,128]{2,1,0:T(8,128)(2,1)S(1)}, u32[]{:S(2)}, u32[]{:S(2)}) collective-permute-start(bf16[48,32,128]{2,1,0:T(8,128)(2,1)S(1)} %shard_map.59), channel_id=1, source_target_pairs={{0,16},{16,0},{32,48},{48,32},{64,80},{80,64},{96,112},{112,96},{1... | collective-permute-start | bytes 1179656 | tf_op jit(solution)/shard_map/ppermute | solution.py:327
  91.0 1.0 shard_map.60.start
  92.0 0.7 collective-permute-done.4.blocks
  92.7 0.4 shard_map.61
  93.1 17.5 %all_to_all.21 = f32[16,8,512]{2,1,0:T(8,128)S(1)} all-to-all(f32[16,8,512]{2,1,0:T(8,128)S(1)} %bitcast.22), channel_id=1, replica_groups=mesh['col'=64,'red'=16] {'red'}, dimensions={0} | all-to-all | bytes 524288 | tf_op jit(solution)/shard_map/all_to_all | solution.py:331
  110.6 14.3 %all_to_all.22 = f32[16,8,512]{2,1,0:T(8,128)S(1)} all-to-all(f32[16,8,512]{2,1,0:T(8,128)S(1)} %broadcast_in_dim.5), channel_id=1, replica_groups=mesh['col'=64,'red'=16] {'red'}, dimensions={0} | all-to-all | bytes 524288 | tf_op jit(solution)/shard_map/all_to_all | solution.py:334
  125.0 0.7 copy.9
  (7 shorter events, 0.1 us)
Async XLA Ops:
  0.7 1.0 copy-start.1
  1.6 0.7 copy-start.2
  2.4 3.3 %collective-permute-start = (bf16[17,32,128]{2,1,0:T(8,128)(2,1)S(1)}, bf16[17,32,128]{2,1,0:T(8,128)(2,1)S(1)}, u32[]{:S(2)}, u32[]{:S(2)}) collective-permute-start(bf16[17,32,128]{2,1,0:T(8,128)(2,1)S(1)} %get-tuple-element.11), channel_id=1, source_target_pairs={{0,16},{16,0},{32,48},{48,32},{64,80},{80,64},{96,112},{112,96},{1... | collective-permute-start | bytes 417800 | tf_op jit(solution)/shard_map/ppermute | solution.py:304
  5.7 41.4 %collective-permute-start.3 = (bf16[32,32,128]{2,1,0:T(8,128)(2,1)S(1)}, bf16[32,32,128]{2,1,0:T(8,128)(2,1)}, u32[]{:S(2)}, u32[]{:S(2)}) collective-permute-start(bf16[32,32,128]{2,1,0:T(8,128)(2,1)S(1)} %pad_maximum_fusion.refs_0_), channel_id=1, source_target_pairs={{512,0},{144,16},{544,32},{176,48},{576,64},{208,80},{608,96},{240... | collective-permute-start | bytes 786440 | tf_op jit(solution)/shard_map/ppermute | solution.py:306
  13.9 33.2 %collective-permute-start.2 = (bf16[32,32,128]{2,1,0:T(8,128)(2,1)S(1)}, bf16[32,32,128]{2,1,0:T(8,128)(2,1)}, u32[]{:S(2)}, u32[]{:S(2)}) collective-permute-start(bf16[32,32,128]{2,1,0:T(8,128)(2,1)S(1)} %pad_maximum_fusion.refs_0_), channel_id=1, source_target_pairs={{768,0},{208,16},{800,32},{240,48},{832,64},{16,80},{864,96},{48,1... | collective-permute-start | bytes 786440 | tf_op jit(solution)/shard_map/ppermute | solution.py:306
  16.8 30.2 %collective-permute-start.1 = (bf16[32,32,128]{2,1,0:T(8,128)(2,1)S(1)}, bf16[32,32,128]{2,1,0:T(8,128)(2,1)}, u32[]{:S(2)}, u32[]{:S(2)}) collective-permute-start(bf16[32,32,128]{2,1,0:T(8,128)(2,1)S(1)} %pad_maximum_fusion.refs_0_), channel_id=1, source_target_pairs={{256,0},{80,16},{288,32},{112,48},{320,64},{144,80},{352,96},{176,... | collective-permute-start | bytes 786440 | tf_op jit(solution)/shard_map/ppermute | solution.py:306
  22.8 24.3 %all-to-all-start = ((s32[8,1,128]{2,1,0:T(1,128)}), s32[8,1,128]{2,1,0:T(1,128)S(1)}, u32[]{:S(2)}, u32[]{:S(2)}) async-start(s32[8,1,128]{2,1,0:T(1,128)} %get-tuple-element.13), calls=%async_computation | async-start | bytes 8192 | tf_op jit(solution)/shard_map/all_to_all | solution.py:309
  40.5 1.9 %copy-start = (bf16[1,1,64,24576]{3,2,1,0:T(8,128)(2,1)S(1)}, bf16[1,1,64,24576]{3,2,1,0:T(8,128)(2,1)}, u32[]{:S(2)}) copy-start(bf16[1,1,64,24576]{3,2,1,0:T(8,128)(2,1)} %param.6) | copy-start | bytes 9437188
  89.1 3.6 %collective-permute-start.4 = (bf16[48,32,128]{2,1,0:T(8,128)(2,1)S(1)}, bf16[48,32,128]{2,1,0:T(8,128)(2,1)S(1)}, u32[]{:S(2)}, u32[]{:S(2)}) collective-permute-start(bf16[48,32,128]{2,1,0:T(8,128)(2,1)S(1)} %shard_map.59), channel_id=1, source_target_pairs={{0,16},{16,0},{32,48},{48,32},{64,80},{80,64},{96,112},{112,96},{1... | collective-permute-start | bytes 1179656 | tf_op jit(solution)/shard_map/ppermute | solution.py:327

commit v12 on v11

--- a/solution.py
+++ b/solution.py
@@ -302,6 +302,9 @@
 
     mine, send = front(amplitudes, block_rows[0], block_counts[0], here)
     given = lax.ppermute(send, "col", swap_pairs())
+    alive = jnp.arange(slots) < block_counts[0, 0]
+    keep = jnp.repeat(tile_mask[0, 0] * alive[:, None], BLOCK, axis=1).astype(jnp.bfloat16)
+    given, keep = lax.optimization_barrier((given, keep))
     chip = jnp.concatenate([mine, given[:-1]])
     sources = [chip] + [lax.ppermute(chip, "col", step_pairs(s)) for s in ORDER[1:]]
 
@@ -310,8 +313,6 @@
         ask, "col", split_axis=0, concat_axis=0, tiled=True, axis_index_groups=groups
     )
 
-    alive = jnp.arange(slots) < block_counts[0, 0]
-    keep = jnp.repeat(tile_mask[0, 0] * alive[:, None], BLOCK, axis=1).astype(jnp.bfloat16)
     weights = stack(core.reshape(1), block_tiles[0, 0], keep)
     asked, weights = lax.optimization_barrier((asked, weights))
     outgoing = pick(asked, sources)

time: 126 us -> 126 us (level)
  no operation moved by 1% of the time
where the time goes in v12:
time: 126 us
  blocking collectives  71.6 us (57%)
  starting transfers between devices  36.7 us (29%)
  waiting for transfers between devices  6.03 us (5%)
  Pallas kernels  5.23 us (4%)
  local copies, waits for them, and re-layouts  4.56 us (4%)
    all_to_all x1, blocking collectives, body(): lax.all_to_all(outgoing.reshape(MEMBERS, -1, HALF, rows), 'col', split_ax...  39.8 us
    all_to_all x1, blocking collectives, body(): lax.all_to_all(slices, 'red', split_axis=0, concat_axis=0, tiled=True)  17.5 us
    all_to_all x1, starting transfers between devices, body(): lax.all_to_all(ask, 'col', split_axis=0, concat_axis=0, tiled=True, axis_...  16.7 us
    ppermute x3, starting transfers between devices, body(): lax.ppermute(chip, 'col', step_pairs(s))  16.1 us
    all_to_all x1, blocking collectives, body(): lax.all_to_all(copies, 'red', split_axis=0, concat_axis=0, tiled=True)  14.3 us
    all_to_all x1, waiting for transfers between devices, body(): lax.all_to_all(ask, 'col', split_axis=0, concat_axis=0, tiled=True, axis_...  5.08 us
    unnamed x7, local copies, waits for them, and re-layouts  4.19 us
  transfers between devices with their start and end apart: 6, of which 3 were waited for; matrix products, arithmetic and copies ran while one was open for 1% of the time, Pallas kernels for 2%

profile of v12, /device:TPU:2, one launch (start us, length us, event | category | flops | bytes accessed | tf_op | source)
XLA Modules:
  0.0 125.6 jit_solution(6550335013096320850)
XLA Ops:
  0.7 0.0 copy-start.1
  0.7 0.9 copy-done.1
  1.6 0.0 copy-start.2
  1.6 0.7 copy-done.2
  2.3 0.1 shard_map.55
  2.4 1.9 %collective-permute-start = (bf16[17,32,128]{2,1,0:T(8,128)(2,1)S(1)}, bf16[17,32,128]{2,1,0:T(8,128)(2,1)S(1)}, u32[]{:S(2)}, u32[]{:S(2)}) collective-permute-start(bf16[17,32,128]{2,1,0:T(8,128)(2,1)S(1)} %get-tuple-element.13), channel_id=1, source_target_pairs={{0,16},{16,0},{32,48},{48,32},{64,80},{80,64},{96,112},{112,96},{1... | collective-permute-start | bytes 417800 | tf_op jit(solution)/shard_map/ppermute | solution.py:304
  4.3 0.7 fusion
  5.0 0.1 copy.6
  5.1 0.1 broadcast_in_dim.4
  5.2 0.1 convert_element_type.17.keep
  5.4 0.3 collective-permute-done.other
  5.7 8.2 %collective-permute-start.3 = (bf16[32,32,128]{2,1,0:T(8,128)(2,1)S(1)}, bf16[32,32,128]{2,1,0:T(8,128)(2,1)}, u32[]{:S(2)}, u32[]{:S(2)}) collective-permute-start(bf16[32,32,128]{2,1,0:T(8,128)(2,1)S(1)} %pad_maximum_fusion.refs_0_), channel_id=1, source_target_pairs={{512,0},{144,16},{544,32},{176,48},{576,64},{208,80},{608,96},{240... | collective-permute-start | bytes 786440 | tf_op jit(solution)/shard_map/ppermute | solution.py:309
  13.9 2.9 %collective-permute-start.2 = (bf16[32,32,128]{2,1,0:T(8,128)(2,1)S(1)}, bf16[32,32,128]{2,1,0:T(8,128)(2,1)}, u32[]{:S(2)}, u32[]{:S(2)}) collective-permute-start(bf16[32,32,128]{2,1,0:T(8,128)(2,1)S(1)} %pad_maximum_fusion.refs_0_), channel_id=1, source_target_pairs={{768,0},{208,16},{800,32},{240,48},{832,64},{16,80},{864,96},{48,1... | collective-permute-start | bytes 786440 | tf_op jit(solution)/shard_map/ppermute | solution.py:309
  16.8 5.0 %collective-permute-start.1 = (bf16[32,32,128]{2,1,0:T(8,128)(2,1)S(1)}, bf16[32,32,128]{2,1,0:T(8,128)(2,1)}, u32[]{:S(2)}, u32[]{:S(2)}) collective-permute-start(bf16[32,32,128]{2,1,0:T(8,128)(2,1)S(1)} %pad_maximum_fusion.refs_0_), channel_id=1, source_target_pairs={{256,0},{80,16},{288,32},{112,48},{320,64},{144,80},{352,96},{176,... | collective-permute-start | bytes 786440 | tf_op jit(solution)/shard_map/ppermute | solution.py:309
  21.9 0.9 shard_map.56
  22.8 16.7 %all-to-all-start = ((s32[8,1,128]{2,1,0:T(1,128)}), s32[8,1,128]{2,1,0:T(1,128)S(1)}, u32[]{:S(2)}, u32[]{:S(2)}) async-start(s32[8,1,128]{2,1,0:T(1,128)} %get-tuple-element.16), calls=%async_computation | async-start | bytes 8192 | tf_op jit(solution)/shard_map/all_to_all | solution.py:312
  39.5 1.9 %copy-done = bf16[1,1,64,24576]{3,2,1,0:T(8,128)(2,1)S(1)} copy-done((bf16[1,1,64,24576]{3,2,1,0:T(8,128)(2,1)S(1)}, bf16[1,1,64,24576]{3,2,1,0:T(8,128)(2,1)}, u32[]{:S(2)}) %copy-start) | copy-done | bytes 3145752
  41.3 0.6 shard_map.57.weights
  42.0 5.1 %all-to-all-done.asked = s32[8,1,128]{2,1,0:T(1,128)S(1)} async-done(((s32[8,1,128]{2,1,0:T(1,128)}), s32[8,1,128]{2,1,0:T(1,128)S(1)}, u32[]{:S(2)}, u32[]{:S(2)}) %all-to-all-start) | async-done | bytes 4128 | tf_op jit(solution)/shard_map/all_to_all | solution.py:312
  47.1 0.0 collective-permute-done.3.refs_3_
  47.1 0.0 collective-permute-done.2.refs_2_
  47.1 0.0 collective-permute-done.1.refs_1_
  47.1 1.5 %shard_map.58 = bf16[256,32,128]{2,1,0:T(8,128)(2,1)S(1)} custom-call(s32[8,1,128]{2,1,0:T(1,128)S(1)} %all-to-all-done.asked, bf16[32,32,128]{2,1,0:T(8,128)(2,1)S(1)} %pad_maximum_fusion.refs_0_, bf16[32,32,128]{2,1,0:T(8,128)(2,1)} %collective-permute-done.1.refs_1_, bf16[32,32,128]{2,1,0:T(8,128)(2,1)} %collective-permute-done.2.refs_2_, ...), custom_call_target="tpu_custom_call" | custom-call | bytes 4194304 | tf_op jit(solution)/shard_map/pallas_call | solution.py:203
  48.6 39.8 %all_to_all.20 = bf16[8,32,32,128]{3,2,1,0:T(8,128)(2,1)S(1)} all-to-all(bf16[8,32,32,128]{3,2,1,0:T(8,128)(2,1)S(1)} %bitcast.20), channel_id=1, replica_groups={{0,32,64,96,128,160,192,224},{256,288,320,352,384,416,448,480},{512,544..., dimensions={0} | all-to-all | bytes 4194304 | tf_op jit(solution)/shard_map/all_to_all | solution.py:319
  88.4 0.6 shard_map.59
  89.0 1.9 %collective-permute-start.4 = (bf16[48,32,128]{2,1,0:T(8,128)(2,1)S(1)}, bf16[48,32,128]{2,1,0:T(8,128)(2,1)S(1)}, u32[]{:S(2)}, u32[]{:S(2)}) collective-permute-start(bf16[48,32,128]{2,1,0:T(8,128)(2,1)S(1)} %shard_map.59), channel_id=1, source_target_pairs={{0,16},{16,0},{32,48},{48,32},{64,80},{80,64},{96,112},{112,96},{1... | collective-permute-start | bytes 1179656 | tf_op jit(solution)/shard_map/ppermute | solution.py:328
  91.0 1.0 shard_map.60.start
  92.0 0.7 collective-permute-done.4.blocks
  92.7 0.4 shard_map.61
  93.1 17.5 %all_to_all.21 = f32[16,8,512]{2,1,0:T(8,128)S(1)} all-to-all(f32[16,8,512]{2,1,0:T(8,128)S(1)} %bitcast.22), channel_id=1, replica_groups=mesh['col'=64,'red'=16] {'red'}, dimensions={0} | all-to-all | bytes 524288 | tf_op jit(solution)/shard_map/all_to_all | solution.py:332
  110.6 14.3 %all_to_all.22 = f32[16,8,512]{2,1,0:T(8,128)S(1)} all-to-all(f32[16,8,512]{2,1,0:T(8,128)S(1)} %broadcast_in_dim.5), channel_id=1, replica_groups=mesh['col'=64,'red'=16] {'red'}, dimensions={0} | all-to-all | bytes 524288 | tf_op jit(solution)/shard_map/all_to_all | solution.py:335
  124.9 0.7 copy.9
  (7 shorter events, 0.1 us)
Async XLA Ops:
  0.7 1.0 copy-start.1
  1.6 0.7 copy-start.2
  2.4 3.3 %collective-permute-start = (bf16[17,32,128]{2,1,0:T(8,128)(2,1)S(1)}, bf16[17,32,128]{2,1,0:T(8,128)(2,1)S(1)}, u32[]{:S(2)}, u32[]{:S(2)}) collective-permute-start(bf16[17,32,128]{2,1,0:T(8,128)(2,1)S(1)} %get-tuple-element.13), channel_id=1, source_target_pairs={{0,16},{16,0},{32,48},{48,32},{64,80},{80,64},{96,112},{112,96},{1... | collective-permute-start | bytes 417800 | tf_op jit(solution)/shard_map/ppermute | solution.py:304
  5.7 41.4 %collective-permute-start.3 = (bf16[32,32,128]{2,1,0:T(8,128)(2,1)S(1)}, bf16[32,32,128]{2,1,0:T(8,128)(2,1)}, u32[]{:S(2)}, u32[]{:S(2)}) collective-permute-start(bf16[32,32,128]{2,1,0:T(8,128)(2,1)S(1)} %pad_maximum_fusion.refs_0_), channel_id=1, source_target_pairs={{512,0},{144,16},{544,32},{176,48},{576,64},{208,80},{608,96},{240... | collective-permute-start | bytes 786440 | tf_op jit(solution)/shard_map/ppermute | solution.py:309
  13.9 33.2 %collective-permute-start.2 = (bf16[32,32,128]{2,1,0:T(8,128)(2,1)S(1)}, bf16[32,32,128]{2,1,0:T(8,128)(2,1)}, u32[]{:S(2)}, u32[]{:S(2)}) collective-permute-start(bf16[32,32,128]{2,1,0:T(8,128)(2,1)S(1)} %pad_maximum_fusion.refs_0_), channel_id=1, source_target_pairs={{768,0},{208,16},{800,32},{240,48},{832,64},{16,80},{864,96},{48,1... | collective-permute-start | bytes 786440 | tf_op jit(solution)/shard_map/ppermute | solution.py:309
  16.8 30.2 %collective-permute-start.1 = (bf16[32,32,128]{2,1,0:T(8,128)(2,1)S(1)}, bf16[32,32,128]{2,1,0:T(8,128)(2,1)}, u32[]{:S(2)}, u32[]{:S(2)}) collective-permute-start(bf16[32,32,128]{2,1,0:T(8,128)(2,1)S(1)} %pad_maximum_fusion.refs_0_), channel_id=1, source_target_pairs={{256,0},{80,16},{288,32},{112,48},{320,64},{144,80},{352,96},{176,... | collective-permute-start | bytes 786440 | tf_op jit(solution)/shard_map/ppermute | solution.py:309
  22.8 24.3 %all-to-all-start = ((s32[8,1,128]{2,1,0:T(1,128)}), s32[8,1,128]{2,1,0:T(1,128)S(1)}, u32[]{:S(2)}, u32[]{:S(2)}) async-start(s32[8,1,128]{2,1,0:T(1,128)} %get-tuple-element.16), calls=%async_computation | async-start | bytes 8192 | tf_op jit(solution)/shard_map/all_to_all | solution.py:312
  39.4 1.9 %copy-start = (bf16[1,1,64,24576]{3,2,1,0:T(8,128)(2,1)S(1)}, bf16[1,1,64,24576]{3,2,1,0:T(8,128)(2,1)}, u32[]{:S(2)}) copy-start(bf16[1,1,64,24576]{3,2,1,0:T(8,128)(2,1)} %param.6) | copy-start | bytes 9437188
  89.0 3.6 %collective-permute-start.4 = (bf16[48,32,128]{2,1,0:T(8,128)(2,1)S(1)}, bf16[48,32,128]{2,1,0:T(8,128)(2,1)S(1)}, u32[]{:S(2)}, u32[]{:S(2)}) collective-permute-start(bf16[48,32,128]{2,1,0:T(8,128)(2,1)S(1)} %shard_map.59), channel_id=1, source_target_pairs={{0,16},{16,0},{32,48},{48,32},{64,80},{80,64},{96,112},{112,96},{1... | collective-permute-start | bytes 1179656 | tf_op jit(solution)/shard_map/ppermute | solution.py:328

commit v13 on v12

--- a/solution.py
+++ b/solution.py
@@ -13,7 +13,7 @@
 NZ = 8
 NCORE = 2
 STEPS = 4
-ORDER = (0, 1, 3, 2)
+ORDER = (0, 3, 1, 2)
 MEMBERS = 8
 LIMIT = pltpu.CompilerParams(vmem_limit_bytes=16 * 1024 * 1024)
 

time: 126 us -> 127 us (level)
  blocking collectives: 71.6 us -> 73.2 us
    all_to_all x1, blocking collectives: 39.8 us -> 41.1 us  [body(): lax.all_to_all(outgoing.reshape(MEMBERS, -1, HALF, rows), 'col', split_ax...]
where the time goes in v13:
time: 127 us; the launch traced here: 126 us
  blocking collectives  73.2 us (58%)
  starting transfers between devices  35.5 us (28%)
  waiting for transfers between devices  6.03 us (5%)
  Pallas kernels  5.23 us (4%)
  local copies, waits for them, and re-layouts  4.56 us (4%)
    all_to_all x1, blocking collectives, body(): lax.all_to_all(outgoing.reshape(MEMBERS, -1, HALF, rows), 'col', split_ax...  41.1 us
    all_to_all x1, blocking collectives, body(): lax.all_to_all(slices, 'red', split_axis=0, concat_axis=0, tiled=True)  17.8 us
    all_to_all x1, starting transfers between devices, body(): lax.all_to_all(ask, 'col', split_axis=0, concat_axis=0, tiled=True, axis_...  16.7 us
    ppermute x3, starting transfers between devices, body(): lax.ppermute(chip, 'col', step_pairs(s))  14.9 us
    all_to_all x1, blocking collectives, body(): lax.all_to_all(copies, 'red', split_axis=0, concat_axis=0, tiled=True)  14.3 us
    all_to_all x1, waiting for transfers between devices, body(): lax.all_to_all(ask, 'col', split_axis=0, concat_axis=0, tiled=True, axis_...  5.08 us
    unnamed x7, local copies, waits for them, and re-layouts  4.19 us
  transfers between devices with their start and end apart: 6, of which 3 were waited for; matrix products, arithmetic and copies ran while one was open for 1% of the time, Pallas kernels for 2%

profile of v13, /device:TPU:2, one launch (start us, length us, event | category | flops | bytes accessed | tf_op | source)
XLA Modules:
  0.0 126.0 jit_solution(6156649769290096283)
XLA Ops:
  0.7 0.0 copy-start.1
  0.7 0.9 copy-done.1
  1.6 0.0 copy-start.2
  1.6 0.7 copy-done.2
  2.3 0.1 shard_map.55
  2.4 1.9 %collective-permute-start = (bf16[17,32,128]{2,1,0:T(8,128)(2,1)S(1)}, bf16[17,32,128]{2,1,0:T(8,128)(2,1)S(1)}, u32[]{:S(2)}, u32[]{:S(2)}) collective-permute-start(bf16[17,32,128]{2,1,0:T(8,128)(2,1)S(1)} %get-tuple-element.13), channel_id=1, source_target_pairs={{0,16},{16,0},{32,48},{48,32},{64,80},{80,64},{96,112},{112,96},{1... | collective-permute-start | bytes 417800 | tf_op jit(solution)/shard_map/ppermute | solution.py:304
  4.3 0.7 fusion
  5.0 0.1 copy.6
  5.1 0.1 broadcast_in_dim.4
  5.2 0.1 convert_element_type.17.keep
  5.4 0.3 collective-permute-done.other
  5.7 8.2 %collective-permute-start.3 = (bf16[32,32,128]{2,1,0:T(8,128)(2,1)S(1)}, bf16[32,32,128]{2,1,0:T(8,128)(2,1)}, u32[]{:S(2)}, u32[]{:S(2)}) collective-permute-start(bf16[32,32,128]{2,1,0:T(8,128)(2,1)S(1)} %pad_maximum_fusion.refs_0_), channel_id=1, source_target_pairs={{512,0},{144,16},{544,32},{176,48},{576,64},{208,80},{608,96},{240... | collective-permute-start | bytes 786440 | tf_op jit(solution)/shard_map/ppermute | solution.py:309
  13.9 2.0 %collective-permute-start.2 = (bf16[32,32,128]{2,1,0:T(8,128)(2,1)S(1)}, bf16[32,32,128]{2,1,0:T(8,128)(2,1)}, u32[]{:S(2)}, u32[]{:S(2)}) collective-permute-start(bf16[32,32,128]{2,1,0:T(8,128)(2,1)S(1)} %pad_maximum_fusion.refs_0_), channel_id=1, source_target_pairs={{256,0},{80,16},{288,32},{112,48},{320,64},{144,80},{352,96},{176,... | collective-permute-start | bytes 786440 | tf_op jit(solution)/shard_map/ppermute | solution.py:309
  15.9 4.7 %collective-permute-start.1 = (bf16[32,32,128]{2,1,0:T(8,128)(2,1)S(1)}, bf16[32,32,128]{2,1,0:T(8,128)(2,1)}, u32[]{:S(2)}, u32[]{:S(2)}) collective-permute-start(bf16[32,32,128]{2,1,0:T(8,128)(2,1)S(1)} %pad_maximum_fusion.refs_0_), channel_id=1, source_target_pairs={{768,0},{208,16},{800,32},{240,48},{832,64},{16,80},{864,96},{48,1... | collective-permute-start | bytes 786440 | tf_op jit(solution)/shard_map/ppermute | solution.py:309
  20.7 0.9 shard_map.56
  21.6 16.7 %all-to-all-start = ((s32[8,1,128]{2,1,0:T(1,128)}), s32[8,1,128]{2,1,0:T(1,128)S(1)}, u32[]{:S(2)}, u32[]{:S(2)}) async-start(s32[8,1,128]{2,1,0:T(1,128)} %get-tuple-element.16), calls=%async_computation | async-start | bytes 8192 | tf_op jit(solution)/shard_map/all_to_all | solution.py:312
  38.2 1.9 %copy-done = bf16[1,1,64,24576]{3,2,1,0:T(8,128)(2,1)S(1)} copy-done((bf16[1,1,64,24576]{3,2,1,0:T(8,128)(2,1)S(1)}, bf16[1,1,64,24576]{3,2,1,0:T(8,128)(2,1)}, u32[]{:S(2)}) %copy-start) | copy-done | bytes 3145752
  40.1 0.6 shard_map.57.weights
  40.8 5.1 %all-to-all-done.asked = s32[8,1,128]{2,1,0:T(1,128)S(1)} async-done(((s32[8,1,128]{2,1,0:T(1,128)}), s32[8,1,128]{2,1,0:T(1,128)S(1)}, u32[]{:S(2)}, u32[]{:S(2)}) %all-to-all-start) | async-done | bytes 4128 | tf_op jit(solution)/shard_map/all_to_all | solution.py:312
  45.8 0.0 collective-permute-done.3.refs_3_
  45.8 0.0 collective-permute-done.2.refs_2_
  45.8 0.0 collective-permute-done.1.refs_1_
  45.9 1.5 %shard_map.58 = bf16[256,32,128]{2,1,0:T(8,128)(2,1)S(1)} custom-call(s32[8,1,128]{2,1,0:T(1,128)S(1)} %all-to-all-done.asked, bf16[32,32,128]{2,1,0:T(8,128)(2,1)S(1)} %pad_maximum_fusion.refs_0_, bf16[32,32,128]{2,1,0:T(8,128)(2,1)} %collective-permute-done.1.refs_1_, bf16[32,32,128]{2,1,0:T(8,128)(2,1)} %collective-permute-done.2.refs_2_, ...), custom_call_target="tpu_custom_call" | custom-call | bytes 4194304 | tf_op jit(solution)/shard_map/pallas_call | solution.py:203
  47.4 41.1 %all_to_all.20 = bf16[8,32,32,128]{3,2,1,0:T(8,128)(2,1)S(1)} all-to-all(bf16[8,32,32,128]{3,2,1,0:T(8,128)(2,1)S(1)} %bitcast.20), channel_id=1, replica_groups={{0,32,64,96,128,160,192,224},{256,288,320,352,384,416,448,480},{512,544..., dimensions={0} | all-to-all | bytes 4194304 | tf_op jit(solution)/shard_map/all_to_all | solution.py:319
  88.5 0.6 shard_map.59
  89.1 1.9 %collective-permute-start.4 = (bf16[48,32,128]{2,1,0:T(8,128)(2,1)S(1)}, bf16[48,32,128]{2,1,0:T(8,128)(2,1)S(1)}, u32[]{:S(2)}, u32[]{:S(2)}) collective-permute-start(bf16[48,32,128]{2,1,0:T(8,128)(2,1)S(1)} %shard_map.59), channel_id=1, source_target_pairs={{0,16},{16,0},{32,48},{48,32},{64,80},{80,64},{96,112},{112,96},{1... | collective-permute-start | bytes 1179656 | tf_op jit(solution)/shard_map/ppermute | solution.py:328
  91.1 1.0 shard_map.60.start
  92.1 0.7 collective-permute-done.4.blocks
  92.8 0.4 shard_map.61
  93.2 17.8 %all_to_all.21 = f32[16,8,512]{2,1,0:T(8,128)S(1)} all-to-all(f32[16,8,512]{2,1,0:T(8,128)S(1)} %bitcast.22), channel_id=1, replica_groups=mesh['col'=64,'red'=16] {'red'}, dimensions={0} | all-to-all | bytes 524288 | tf_op jit(solution)/shard_map/all_to_all | solution.py:332
  111.0 14.3 %all_to_all.22 = f32[16,8,512]{2,1,0:T(8,128)S(1)} all-to-all(f32[16,8,512]{2,1,0:T(8,128)S(1)} %broadcast_in_dim.5), channel_id=1, replica_groups=mesh['col'=64,'red'=16] {'red'}, dimensions={0} | all-to-all | bytes 524288 | tf_op jit(solution)/shard_map/all_to_all | solution.py:335
  125.3 0.7 copy.9
  (7 shorter events, 0.1 us)
Async XLA Ops:
  0.7 1.0 copy-start.1
  1.6 0.7 copy-start.2
  2.4 3.3 %collective-permute-start = (bf16[17,32,128]{2,1,0:T(8,128)(2,1)S(1)}, bf16[17,32,128]{2,1,0:T(8,128)(2,1)S(1)}, u32[]{:S(2)}, u32[]{:S(2)}) collective-permute-start(bf16[17,32,128]{2,1,0:T(8,128)(2,1)S(1)} %get-tuple-element.13), channel_id=1, source_target_pairs={{0,16},{16,0},{32,48},{48,32},{64,80},{80,64},{96,112},{112,96},{1... | collective-permute-start | bytes 417800 | tf_op jit(solution)/shard_map/ppermute | solution.py:304
  5.7 40.2 %collective-permute-start.3 = (bf16[32,32,128]{2,1,0:T(8,128)(2,1)S(1)}, bf16[32,32,128]{2,1,0:T(8,128)(2,1)}, u32[]{:S(2)}, u32[]{:S(2)}) collective-permute-start(bf16[32,32,128]{2,1,0:T(8,128)(2,1)S(1)} %pad_maximum_fusion.refs_0_), channel_id=1, source_target_pairs={{512,0},{144,16},{544,32},{176,48},{576,64},{208,80},{608,96},{240... | collective-permute-start | bytes 786440 | tf_op jit(solution)/shard_map/ppermute | solution.py:309
  13.9 32.0 %collective-permute-start.2 = (bf16[32,32,128]{2,1,0:T(8,128)(2,1)S(1)}, bf16[32,32,128]{2,1,0:T(8,128)(2,1)}, u32[]{:S(2)}, u32[]{:S(2)}) collective-permute-start(bf16[32,32,128]{2,1,0:T(8,128)(2,1)S(1)} %pad_maximum_fusion.refs_0_), channel_id=1, source_target_pairs={{256,0},{80,16},{288,32},{112,48},{320,64},{144,80},{352,96},{176,... | collective-permute-start | bytes 786440 | tf_op jit(solution)/shard_map/ppermute | solution.py:309
  15.9 29.9 %collective-permute-start.1 = (bf16[32,32,128]{2,1,0:T(8,128)(2,1)S(1)}, bf16[32,32,128]{2,1,0:T(8,128)(2,1)}, u32[]{:S(2)}, u32[]{:S(2)}) collective-permute-start(bf16[32,32,128]{2,1,0:T(8,128)(2,1)S(1)} %pad_maximum_fusion.refs_0_), channel_id=1, source_target_pairs={{768,0},{208,16},{800,32},{240,48},{832,64},{16,80},{864,96},{48,1... | collective-permute-start | bytes 786440 | tf_op jit(solution)/shard_map/ppermute | solution.py:309
  21.6 24.3 %all-to-all-start = ((s32[8,1,128]{2,1,0:T(1,128)}), s32[8,1,128]{2,1,0:T(1,128)S(1)}, u32[]{:S(2)}, u32[]{:S(2)}) async-start(s32[8,1,128]{2,1,0:T(1,128)} %get-tuple-element.16), calls=%async_computation | async-start | bytes 8192 | tf_op jit(solution)/shard_map/all_to_all | solution.py:312
  38.2 1.9 %copy-start = (bf16[1,1,64,24576]{3,2,1,0:T(8,128)(2,1)S(1)}, bf16[1,1,64,24576]{3,2,1,0:T(8,128)(2,1)}, u32[]{:S(2)}) copy-start(bf16[1,1,64,24576]{3,2,1,0:T(8,128)(2,1)} %param.6) | copy-start | bytes 9437188
  89.1 3.6 %collective-permute-start.4 = (bf16[48,32,128]{2,1,0:T(8,128)(2,1)S(1)}, bf16[48,32,128]{2,1,0:T(8,128)(2,1)S(1)}, u32[]{:S(2)}, u32[]{:S(2)}) collective-permute-start(bf16[48,32,128]{2,1,0:T(8,128)(2,1)S(1)} %shard_map.59), channel_id=1, source_target_pairs={{0,16},{16,0},{32,48},{48,32},{64,80},{80,64},{96,112},{112,96},{1... | collective-permute-start | bytes 1179656 | tf_op jit(solution)/shard_map/ppermute | solution.py:328
